TPU v7x, 32 devices: a whole 2x2x4 slice. The times are simulated.
32 devices in a mesh: ep: 8 (over z, y), fs: 4 (over x, core).
Axes of the slice: x: 2, y: 2, z: 4, core: 2. Of those that a mesh axis runs over, the one named last changes fastest.
Arguments:
- tokens: bfloat16 [8192, 768], P(('ep', 'fs')), may hold values from -6 to 6
- cotangent: bfloat16 [8192, 768], P(('ep', 'fs')), may hold values from -6 to 6
- routes: int32 [8192, 2], P(('ep', 'fs')), may hold values from 0 to 15, all different within a row; in each aligned block of 256 rows (0 to 255, 256 to 511, ...) at most 48 rows name the same one
- priority: int32 [8192], P(('ep', 'fs')), may hold values 0 or 1
- gain_attn: bfloat16 [768], P('fs'), may hold values from 0.25 to 1.75
- w_query: bfloat16 [768, 768], P('fs'), may hold values from -0.21875 to 0.21875
- w_key: bfloat16 [768, 768], P('fs'), may hold values from -0.21875 to 0.21875
- w_value: bfloat16 [768, 768], P('fs'), may hold values from -0.21875 to 0.21875
- w_out: bfloat16 [768, 768], P('fs'), may hold values from -0.875 to 0.875
- gain_ffn: bfloat16 [768], P('fs'), may hold values from 0.25 to 1.75
- w_shared_gate: bfloat16 [768, 2048], P('fs'), may hold values from -0.21875 to 0.21875
- w_shared_up: bfloat16 [768, 2048], P('fs'), may hold values from -0.21875 to 0.21875
- w_shared_down: bfloat16 [2048, 768], P('fs'), may hold values from -0.125 to 0.125
- w_router: bfloat16 [768, 16], P('fs'), may hold values from -0.15625 to 0.15625
- w_expert_gate: bfloat16 [768, 32768], P(None, ('ep', 'fs')), may hold values from -0.21875 to 0.21875
- w_expert_up: bfloat16 [768, 32768], P(None, ('ep', 'fs')), may hold values from -0.21875 to 0.21875
- w_expert_down: bfloat16 [32768, 768], P(('ep', 'fs')), may hold values from -0.125 to 0.125
Outputs:
- output: bfloat16 [8192, 768], P(('ep', 'fs'))
- grad_tokens: float32 [8192, 768], P(('ep', 'fs'))
- grad_gain_attn: float32 [768], P('fs')
- grad_w_query: float32 [768, 768], P('fs')
- grad_w_key: float32 [768, 768], P('fs')
- grad_w_value: float32 [768, 768], P('fs')
- grad_w_out: float32 [768, 768], P('fs')
- grad_gain_ffn: float32 [768], P('fs')
- grad_w_shared_gate: float32 [768, 2048], P('fs')
- grad_w_shared_up: float32 [768, 2048], P('fs')
- grad_w_shared_down: float32 [2048, 768], P('fs')
- grad_w_router: float32 [768, 16], P('fs')
- grad_w_expert_gate: float32 [768, 32768], P(None, ('ep', 'fs'))
- grad_w_expert_up: float32 [768, 32768], P(None, ('ep', 'fs'))
- grad_w_expert_down: float32 [32768, 768], P(('ep', 'fs'))
Inputs may be any that keep to these rules, and one draw needn't show every extreme that they name: The two routes of a token differ; among the 256 tokens of one device no expert is named by more than 48 tokens, and in some device's tokens one is named by exactly 48. Route priority[t] of token t is its first choice.
All inputs are finite; a program needn't handle non-finite values. No bound on the sum of `priority` on one device may be relied on, other than what follows from the above.
Results may differ from a plain program's by a relative error of at most 0.02.
Values may be sent and summed in bfloat16 or wider, within the bound.
No kernel may reach another device: no remote copies, remote signals or barrier semaphores. Data moves between devices by JAX's collectives and lax.ppermute only.
A program may use at most 192 MiB of HBM per device.

v0:
```python
import jax
import jax.numpy as jnp
from jax import lax
from jax.sharding import PartitionSpec as P

HEADS = 12
EXPERTS = 16
MOST = 48


EPS = 1e-06
SCALE = 0.125
NEG = -1e30


def matmul(left_op, right_op):
    return jnp.dot(left_op, right_op, preferred_element_type=jnp.float32)


def contract_rows(left_op, right_op):
    return lax.dot_general(
        left_op, right_op, (((0,), (0,)), ((), ())), preferred_element_type=jnp.float32
    )


def contract_cols(left_op, right_op):
    return lax.dot_general(
        left_op, right_op, (((1,), (1,)), ((), ())), preferred_element_type=jnp.float32
    )


def rms_forward(values, gain_vec):
    inverse = lax.rsqrt(jnp.mean(values * values, -1, keepdims=True) + EPS)
    return (values * inverse * gain_vec, inverse)


def rms_backward(upstream, values, inverse, gain_vec):
    scaled = upstream * gain_vec
    grad_gain = jnp.sum(upstream * values * inverse, 0)
    grad_values = inverse * scaled - values * inverse**3 * jnp.mean(
        scaled * values, -1, keepdims=True
    )
    return (grad_values, grad_gain)


def rope_tables(positions, half_size):
    freq = jnp.exp(-jnp.log(10000.0) * jnp.arange(half_size).astype(jnp.float32) / half_size)
    angle = positions.astype(jnp.float32)[:, None] * freq[None, :]
    return (jnp.cos(angle), jnp.sin(angle))


def rotate(values, cosine, sine_tab):
    half_size = values.shape[-1] // 2
    first_half, second_half = (values[..., :half_size], values[..., half_size:])
    cosine, sine_tab = (cosine[:, None, :], sine_tab[:, None, :])
    return jnp.concatenate(
        [
            first_half * cosine - second_half * sine_tab,
            second_half * cosine + first_half * sine_tab,
        ],
        -1,
    )


def unrotate(values, cosine, sine_tab):
    half_size = values.shape[-1] // 2
    first_half, second_half = (values[..., :half_size], values[..., half_size:])
    cosine, sine_tab = (cosine[:, None, :], sine_tab[:, None, :])
    return jnp.concatenate(
        [
            first_half * cosine + second_half * sine_tab,
            second_half * cosine - first_half * sine_tab,
        ],
        -1,
    )


def silu_grad(gate_val):
    sigma = jax.nn.sigmoid(gate_val)
    return (gate_val * sigma, sigma * (1.0 + gate_val * (1.0 - sigma)))


def shards(
    tokens,
    cotangent,
    routes,
    priority,
    gain_attn,
    w_query,
    w_key,
    w_value,
    w_out,
    gain_ffn,
    w_shared_gate,
    w_shared_up,
    w_shared_down,
    w_router,
    w_expert_gate,
    w_expert_up,
    w_expert_down,
):
    (
        gain_one,
        query_mat,
        key_mat,
        value_mat,
        out_mat,
        gain_two,
        sgate_mat,
        sup_mat,
        sdown_mat,
        router_mat,
    ) = (
        lax.all_gather(gain_attn, "fs", axis=0, tiled=True),
        lax.all_gather(w_query, "fs", axis=0, tiled=True),
        lax.all_gather(w_key, "fs", axis=0, tiled=True),
        lax.all_gather(w_value, "fs", axis=0, tiled=True),
        lax.all_gather(w_out, "fs", axis=0, tiled=True),
        lax.all_gather(gain_ffn, "fs", axis=0, tiled=True),
        lax.all_gather(w_shared_gate, "fs", axis=0, tiled=True),
        lax.all_gather(w_shared_up, "fs", axis=0, tiled=True),
        lax.all_gather(w_shared_down, "fs", axis=0, tiled=True),
        lax.all_gather(w_router, "fs", axis=0, tiled=True),
    )
    tok_rows, model_width = tokens.shape
    head_count = HEADS
    head_size = model_width // head_count
    fs_count = lax.axis_size("fs")
    ep_count = lax.axis_size("ep")
    x_float = tokens.astype(jnp.float32)
    normed_one, inverse_one = rms_forward(x_float, gain_one)
    attn_input = normed_one.astype(jnp.bfloat16)
    positions = lax.axis_index("fs") * tok_rows + jnp.arange(tok_rows)
    cosine, sine_tab = rope_tables(positions, head_size // 2)
    head_shape = (tok_rows, head_count, head_size)
    query_rot = rotate(matmul(attn_input, query_mat).reshape(head_shape), cosine, sine_tab).astype(
        jnp.bfloat16
    )
    key_rot = (
        rotate(matmul(attn_input, key_mat).reshape(head_shape), cosine, sine_tab)
        .astype(jnp.bfloat16)
        .reshape(tok_rows, model_width)
    )
    value_low = matmul(attn_input, value_mat).astype(jnp.bfloat16)
    keys_all, values_all = (
        lax.all_gather(key_rot, "fs", axis=0, tiled=True),
        lax.all_gather(value_low, "fs", axis=0, tiled=True),
    )
    seq_len = keys_all.shape[0]
    causal = positions[:, None] >= jnp.arange(seq_len)[None, :]
    query_heads = query_rot.transpose(1, 0, 2)
    key_heads = keys_all.reshape(seq_len, head_count, head_size).transpose(1, 0, 2)
    value_heads = values_all.reshape(seq_len, head_count, head_size).transpose(1, 0, 2)

    def head_forward(pieces):
        query_head, key_head, value_head = pieces
        scores = jnp.where(causal, contract_cols(query_head, key_head) * SCALE, NEG)
        row_max = jnp.max(scores, -1, keepdims=True)
        exp_scores = jnp.exp(scores - row_max)
        row_total = jnp.sum(exp_scores, -1, keepdims=True)
        weights = (exp_scores / row_total).astype(jnp.bfloat16)
        return (matmul(weights, value_head), (row_max + jnp.log(row_total))[:, 0])

    attended, lse_heads = lax.map(head_forward, (query_heads, key_heads, value_heads))
    attended_low = attended.transpose(1, 0, 2).reshape(tok_rows, model_width).astype(jnp.bfloat16)
    residual = x_float + matmul(attended_low, out_mat)
    normed_two, inverse_two = rms_forward(residual, gain_two)
    ffn_input = normed_two.astype(jnp.bfloat16)
    shared_gate = matmul(ffn_input, sgate_mat)
    shared_up = matmul(ffn_input, sup_mat)
    shared_silu, shared_slope = silu_grad(shared_gate)
    shared_hidden = (shared_silu * shared_up).astype(jnp.bfloat16)
    shared_out = matmul(shared_hidden, sdown_mat)
    logits = matmul(ffn_input, router_mat)
    chosen = jnp.take_along_axis(logits, routes, 1)
    chosen_exp = jnp.exp(chosen - jnp.max(chosen, -1, keepdims=True))
    gates = chosen_exp / jnp.sum(chosen_exp, -1, keepdims=True)
    expert_iota = jnp.arange(EXPERTS)
    classes = jnp.stack([priority, 1 - priority], 1)
    route_hits = (routes[:, :, None] == expert_iota).astype(jnp.int32)
    per_class = jnp.stack(
        [
            jnp.sum(route_hits * (classes == class_id)[:, :, None].astype(jnp.int32), 1)
            for class_id in (0, 1)
        ]
    )
    counts = jnp.sum(per_class, 1)
    all_counts = lax.all_gather(counts[None], ("ep", "fs"), axis=0, tiled=True)
    my_rank = lax.axis_index("ep") * fs_count + lax.axis_index("fs")
    earlier = (jnp.arange(all_counts.shape[0]) < my_rank).astype(jnp.int32)
    ahead = jnp.sum(all_counts * earlier[:, None, None], 0)
    before = jnp.cumsum(per_class, 1) - per_class
    zero_row = jnp.zeros((EXPERTS,), jnp.int32)
    global_table = (
        before + (ahead + jnp.stack([zero_row, jnp.sum(all_counts[:, 0, :], 0)]))[:, None, :]
    )
    local_table = before + jnp.stack([zero_row, counts[0]])[:, None, :]

    def pair_value(class_table):
        picked = jnp.where(
            (classes == 0)[:, :, None], class_table[0][:, None, :], class_table[1][:, None, :]
        )
        return jnp.sum(picked * route_hits, -1)

    position = pair_value(global_table)
    slot_rank = pair_value(local_table)
    capacity = 5 * tok_rows * ep_count * fs_count // 32
    kept_mask = (position < capacity).astype(jnp.float32)
    pair_weight = gates * kept_mask
    flat_slot = (routes * MOST + slot_rank).reshape(-1)
    token_ids = jnp.broadcast_to(jnp.arange(tok_rows)[:, None], (tok_rows, 2)).reshape(-1)
    slot_token = jnp.full((EXPERTS * MOST,), tok_rows, jnp.int32).at[flat_slot].set(token_ids)
    slot_weight = (
        jnp.zeros((EXPERTS * MOST,), jnp.float32).at[flat_slot].set(pair_weight.reshape(-1))
    )
    input_pad = jnp.concatenate([ffn_input, jnp.zeros((1, model_width), jnp.bfloat16)])
    grad_pad = jnp.concatenate([cotangent, jnp.zeros((1, model_width), jnp.bfloat16)])
    grad_rows_pad = grad_pad[slot_token].astype(jnp.float32)
    rows_sent = input_pad[slot_token]
    grads_sent = (slot_weight[:, None] * grad_rows_pad).astype(jnp.bfloat16)
    local_count = max(1, EXPERTS // ep_count)
    replicas = max(1, ep_count // EXPERTS)
    groups = EXPERTS // local_count
    gate_cols, up_cols, down_rows = (
        lax.all_gather(w_expert_gate, "fs", axis=1, tiled=True),
        lax.all_gather(w_expert_up, "fs", axis=1, tiled=True),
        lax.all_gather(w_expert_down, "fs", axis=0, tiled=True),
    )
    hidden_part = gate_cols.shape[1] // local_count
    gate_local = gate_cols.reshape(model_width, local_count, hidden_part).transpose(1, 0, 2)
    up_local = up_cols.reshape(model_width, local_count, hidden_part).transpose(1, 0, 2)
    down_local = down_rows.reshape(local_count, hidden_part, model_width)

    def spread(buffer):
        wide = buffer.reshape(groups, 1, local_count * MOST, model_width)
        wide = jnp.broadcast_to(wide, (groups, replicas, local_count * MOST, model_width))
        return wide.reshape(ep_count, local_count * MOST, model_width)

    def collect(buffer):
        return jnp.sum(
            buffer.reshape(groups, replicas, local_count * MOST, model_width), 1
        ).reshape(EXPERTS * MOST, model_width)

    def owner_layout(received):
        return (
            received.reshape(ep_count, local_count, MOST, model_width)
            .transpose(1, 0, 2, 3)
            .reshape(local_count, ep_count * MOST, model_width)
        )

    def source_layout(owned):
        return (
            owned.reshape(local_count, ep_count, MOST, model_width)
            .transpose(1, 0, 2, 3)
            .reshape(ep_count, local_count * MOST, model_width)
        )

    send_rows = spread(rows_sent)
    send_grads = spread(grads_sent)
    got_rows = lax.all_to_all(send_rows, "ep", split_axis=0, concat_axis=0, tiled=True)
    own_rows = owner_layout(got_rows)
    gate_val = jnp.einsum("lrd,ldh->lrh", own_rows, gate_local, preferred_element_type=jnp.float32)
    up_val = jnp.einsum("lrd,ldh->lrh", own_rows, up_local, preferred_element_type=jnp.float32)
    silu_val, slope_val = silu_grad(gate_val)
    hidden_val = (silu_val * up_val).astype(jnp.bfloat16)
    out_rows = jnp.einsum(
        "lrh,lhd->lrd", hidden_val, down_local, preferred_element_type=jnp.float32
    )
    out_rows, saved_vals = (out_rows, (up_val, silu_val, slope_val, hidden_val))
    back_out = lax.all_to_all(
        source_layout(out_rows).astype(jnp.bfloat16), "ep", split_axis=0, concat_axis=0, tiled=True
    ).astype(jnp.float32)
    slot_out = collect(back_out)
    mixed = (
        jnp.zeros((tok_rows + 1, model_width), jnp.float32)
        .at[slot_token]
        .add(slot_weight[:, None] * slot_out)[:tok_rows]
    )
    output = (residual + shared_out + mixed).astype(jnp.bfloat16)
    grad_float = cotangent.astype(jnp.float32)
    slot_dot = jnp.sum(grad_rows_pad * slot_out, -1)
    grad_weight = slot_dot[flat_slot].reshape(tok_rows, 2) * kept_mask
    grad_chosen = gates * (grad_weight - jnp.sum(gates * grad_weight, -1, keepdims=True))
    grad_logits = jnp.sum(route_hits.astype(jnp.float32) * grad_chosen[:, :, None], 1).astype(
        jnp.bfloat16
    )
    grad_sdown = contract_rows(shared_hidden, cotangent)
    grad_shidden = contract_cols(cotangent, sdown_mat)
    grad_sgate = (grad_shidden * shared_up * shared_slope).astype(jnp.bfloat16)
    grad_sup = (grad_shidden * shared_silu).astype(jnp.bfloat16)
    grad_sgate_w = contract_rows(ffn_input, grad_sgate)
    grad_sup_w = contract_rows(ffn_input, grad_sup)
    grad_router = contract_rows(ffn_input, grad_logits)
    got_grads = lax.all_to_all(send_grads, "ep", split_axis=0, concat_axis=0, tiled=True)
    own_grads = owner_layout(got_grads)
    up_val, silu_val, slope_val, hidden_val = saved_vals
    grad_hidden = jnp.einsum(
        "lrd,lhd->lrh", own_grads, down_local, preferred_element_type=jnp.float32
    )
    grad_gate = (grad_hidden * up_val * slope_val).astype(jnp.bfloat16)
    grad_up = (grad_hidden * silu_val).astype(jnp.bfloat16)
    grad_rows = jnp.einsum(
        "lrh,ldh->lrd", grad_gate, gate_local, preferred_element_type=jnp.float32
    )
    grad_rows = grad_rows + jnp.einsum(
        "lrh,ldh->lrd", grad_up, up_local, preferred_element_type=jnp.float32
    )
    grad_gate_w = jnp.einsum(
        "lrd,lrh->ldh", own_rows, grad_gate, preferred_element_type=jnp.float32
    )
    grad_up_w = jnp.einsum("lrd,lrh->ldh", own_rows, grad_up, preferred_element_type=jnp.float32)
    grad_down_w = jnp.einsum(
        "lrh,lrd->lhd", hidden_val, own_grads, preferred_element_type=jnp.float32
    )
    din_rows, grad_gate_w, grad_up_w, grad_down_w = (grad_rows, grad_gate_w, grad_up_w, grad_down_w)
    back_din = lax.all_to_all(
        source_layout(din_rows), "ep", split_axis=0, concat_axis=0, tiled=True
    )
    slot_din = collect(back_din)
    grad_ffn = (
        contract_cols(grad_sgate, sgate_mat)
        + contract_cols(grad_sup, sup_mat)
        + contract_cols(grad_logits, router_mat)
    )
    grad_ffn = (
        grad_ffn
        + jnp.zeros((tok_rows + 1, model_width), jnp.float32)
        .at[slot_token]
        .add(slot_din)[:tok_rows]
    )
    grad_resid_norm, grad_gain_two = rms_backward(grad_ffn, residual, inverse_two, gain_two)
    grad_resid = grad_float + grad_resid_norm
    grad_branch = grad_resid.astype(jnp.bfloat16)
    grad_out_w = contract_rows(attended_low, grad_branch)
    grad_attended = contract_cols(grad_branch, out_mat).astype(jnp.bfloat16)
    grad_heads = grad_attended.reshape(head_shape).transpose(1, 0, 2)

    def head_backward(pieces):
        query_head, key_head, value_head, grad_head, lse_head = pieces
        scores = jnp.where(causal, contract_cols(query_head, key_head) * SCALE, NEG)
        probs = jnp.exp(scores - lse_head[:, None])
        grad_probs = contract_cols(grad_head, value_head)
        inner = jnp.sum(probs * grad_probs, -1, keepdims=True)
        grad_scores = (probs * (grad_probs - inner)).astype(jnp.bfloat16)
        grad_query = matmul(grad_scores, key_head) * SCALE
        grad_keys = contract_rows(grad_scores, query_head) * SCALE
        grad_values = contract_rows(probs.astype(jnp.bfloat16), grad_head)
        return (grad_query, grad_keys, grad_values)

    grad_query, grad_keys, grad_values = lax.map(
        head_backward, (query_heads, key_heads, value_heads, grad_heads, lse_heads)
    )
    keys_part = grad_keys.transpose(1, 0, 2).reshape(seq_len, model_width)
    values_part = grad_values.transpose(1, 0, 2).reshape(seq_len, model_width)
    keys_own, values_own = (
        lax.psum_scatter(
            keys_part.astype(jnp.bfloat16), "fs", scatter_dimension=0, tiled=True
        ).astype(jnp.float32),
        lax.psum_scatter(
            values_part.astype(jnp.bfloat16), "fs", scatter_dimension=0, tiled=True
        ).astype(jnp.float32),
    )
    grad_query_low = (
        unrotate(grad_query.transpose(1, 0, 2), cosine, sine_tab)
        .reshape(tok_rows, model_width)
        .astype(jnp.bfloat16)
    )
    grad_key_low = (
        unrotate(keys_own.reshape(head_shape), cosine, sine_tab)
        .reshape(tok_rows, model_width)
        .astype(jnp.bfloat16)
    )
    grad_value_low = values_own.astype(jnp.bfloat16)
    grad_query_w = contract_rows(attn_input, grad_query_low)
    grad_key_w = contract_rows(attn_input, grad_key_low)
    grad_value_w = contract_rows(attn_input, grad_value_low)
    grad_input_norm = (
        contract_cols(grad_query_low, query_mat)
        + contract_cols(grad_key_low, key_mat)
        + contract_cols(grad_value_low, value_mat)
    )
    grad_x_norm, grad_gain_one = rms_backward(grad_input_norm, x_float, inverse_one, gain_one)
    grad_tokens = grad_resid + grad_x_norm
    (
        sum_gain_one,
        sum_query_w,
        sum_key_w,
        sum_value_w,
        sum_out_w,
        sum_gain_two,
        sum_sgate_w,
        sum_sup_w,
        sum_sdown,
        sum_router,
    ) = (
        lax.psum_scatter(
            grad_gain_one.astype(jnp.bfloat16), "fs", scatter_dimension=0, tiled=True
        ).astype(jnp.float32),
        lax.psum_scatter(
            grad_query_w.astype(jnp.bfloat16), "fs", scatter_dimension=0, tiled=True
        ).astype(jnp.float32),
        lax.psum_scatter(
            grad_key_w.astype(jnp.bfloat16), "fs", scatter_dimension=0, tiled=True
        ).astype(jnp.float32),
        lax.psum_scatter(
            grad_value_w.astype(jnp.bfloat16), "fs", scatter_dimension=0, tiled=True
        ).astype(jnp.float32),
        lax.psum_scatter(
            grad_out_w.astype(jnp.bfloat16), "fs", scatter_dimension=0, tiled=True
        ).astype(jnp.float32),
        lax.psum_scatter(
            grad_gain_two.astype(jnp.bfloat16), "fs", scatter_dimension=0, tiled=True
        ).astype(jnp.float32),
        lax.psum_scatter(
            grad_sgate_w.astype(jnp.bfloat16), "fs", scatter_dimension=0, tiled=True
        ).astype(jnp.float32),
        lax.psum_scatter(
            grad_sup_w.astype(jnp.bfloat16), "fs", scatter_dimension=0, tiled=True
        ).astype(jnp.float32),
        lax.psum_scatter(
            grad_sdown.astype(jnp.bfloat16), "fs", scatter_dimension=0, tiled=True
        ).astype(jnp.float32),
        lax.psum_scatter(
            grad_router.astype(jnp.bfloat16), "fs", scatter_dimension=0, tiled=True
        ).astype(jnp.float32),
    )
    (
        sum_gain_one,
        sum_query_w,
        sum_key_w,
        sum_value_w,
        sum_out_w,
        sum_gain_two,
        sum_sgate_w,
        sum_sup_w,
        sum_sdown,
        sum_router,
    ) = lax.psum(
        (
            sum_gain_one,
            sum_query_w,
            sum_key_w,
            sum_value_w,
            sum_out_w,
            sum_gain_two,
            sum_sgate_w,
            sum_sup_w,
            sum_sdown,
            sum_router,
        ),
        "ep",
    )
    expert_gate_g, expert_up_g, expert_down_g = (
        lax.psum_scatter(
            grad_gate_w.transpose(1, 0, 2)
            .reshape(model_width, local_count * hidden_part)
            .astype(jnp.bfloat16),
            "fs",
            scatter_dimension=1,
            tiled=True,
        ).astype(jnp.float32),
        lax.psum_scatter(
            grad_up_w.transpose(1, 0, 2)
            .reshape(model_width, local_count * hidden_part)
            .astype(jnp.bfloat16),
            "fs",
            scatter_dimension=1,
            tiled=True,
        ).astype(jnp.float32),
        lax.psum_scatter(
            grad_down_w.reshape(local_count * hidden_part, model_width).astype(jnp.bfloat16),
            "fs",
            scatter_dimension=0,
            tiled=True,
        ).astype(jnp.float32),
    )
    return (
        output,
        grad_tokens,
        sum_gain_one,
        sum_query_w,
        sum_key_w,
        sum_value_w,
        sum_out_w,
        sum_gain_two,
        sum_sgate_w,
        sum_sup_w,
        sum_sdown,
        sum_router,
        expert_gate_g,
        expert_up_g,
        expert_down_g,
    )


def solution(mesh):
    return jax.shard_map(
        shards,
        mesh=mesh,
        in_specs=(
            P(("ep", "fs"), None),
            P(("ep", "fs"), None),
            P(("ep", "fs"), None),
            P(("ep", "fs")),
            P("fs"),
            P("fs", None),
            P("fs", None),
            P("fs", None),
            P("fs", None),
            P("fs"),
            P("fs", None),
            P("fs", None),
            P("fs", None),
            P("fs", None),
            P(None, ("ep", "fs")),
            P(None, ("ep", "fs")),
            P(("ep", "fs"), None),
        ),
        out_specs=(
            P(("ep", "fs"), None),
            P(("ep", "fs"), None),
            P("fs"),
            P("fs", None),
            P("fs", None),
            P("fs", None),
            P("fs", None),
            P("fs"),
            P("fs", None),
            P("fs", None),
            P("fs", None),
            P("fs", None),
            P(None, ("ep", "fs")),
            P(None, ("ep", "fs")),
            P(("ep", "fs"), None),
        ),
        check_vma=False,
    )
```

profile of v0, /device:TPU:0, one launch (start us, length us, event | category | flops | bytes accessed | tf_op | source)
XLA Modules:
  0.0 1177.1 jit_solution(10833656451999130276)
XLA Ops:
  13.2 8.3 all-reduce.10
  23.5 6.2 all-gather.16.cloned.1.call-done
  31.8 17.0 %all-gather.18.cloned.1.call-done = bf16[768,768]{1,0:T(8,128)(2,1)} async-done(((bf16[192,768]{1,0:T(8,128)(2,1)}), bf16[768,768]{1,0:T(8,128)(2,1)}) %all-gather.18.cloned.1.call-update) | async-done | bytes 1179664 | tf_op jit(solution)/shard_map/all_gather | solution.py:116
  51.9 16.0 %all-gather.22.cloned.1.call-done = bf16[768,768]{1,0:T(8,128)(2,1)} async-done(((bf16[192,768]{1,0:T(8,128)(2,1)}), bf16[768,768]{1,0:T(8,128)(2,1)}) %all-gather.22.cloned.1.call-update) | async-done | bytes 1179664 | tf_op jit(solution)/shard_map/all_gather | solution.py:117
  76.3 40.6 %all-gather.1 = s32[32,2,16]{2,1,0:T(2,128)S(1)} all-gather(s32[1,2,16]{2,1,0:T(2,128)S(1)} %bitcast.333), channel_id=2, replica_groups=mesh['ep'=8,'fs'=4] {'ep','fs'}, dimensions={0}, use_global_device_ids=true | all-gather | bytes 4224 | tf_op jit(solution)/shard_map/all_gather | solution.py:188
  123.2 4.1 copy.181
  131.8 52.4 %while.30 = (s32[]{:T(128)}, bf16[12,256,64]{1,2,0:T(8,128)(2,1)S(1)}, f32[12,256]{1,0:T(8,128)}, bf16[12,256,64]{2,1,0:T(8,128)(2,1)S(1)}, bf16[12,1024,64]{2,1...) while((s32[]{:T(128)}, bf16[12,256,64]{1,2,0:T(8,128)(2,1)S(1)}, ...), condition=%wide.region_4.5_spmd.clone.clone, body=%wide.region_1.4_spmd.clone.sunk.clone | while | flops 69467904 | bytes 3814481 | solution.py:164
  195.4 28.6 %all-to-all-done = bf16[8,96,768]{2,1,0:T(8,128)(2,1)S(1)} async-done(((bf16[8,96,768]{2,1,0:T(8,128)(2,1)}), bf16[8,96,768]{2,1,0:T(8,128)(2,1)S(1)}, u32[]{:S(2)}, u32[]{:S(2)}) %all-to-all-start) | async-done | bytes 1179680 | tf_op jit(solution)/shard_map/all_to_all | solution.py:260
  225.1 8.7 copy.192
  233.8 9.0 copy.194
  242.8 4.8 fusion.52
  250.3 5.5 multiply_convert_fusion.3
  255.8 19.9 %all-gather.38.cloned.1.call-done = bf16[4096,768]{1,0:T(8,128)(2,1)} async-done(((bf16[1024,768]{1,0:T(8,128)(2,1)}), bf16[4096,768]{1,0:T(8,128)(2,1)}) %all-gather.38.cloned.1.call-update) | async-done | bytes 6291472 | tf_op jit(solution)/shard_map/all_gather | solution.py:227
  275.7 6.3 convolution_convert_fusion.8
  283.1 5.5 all-to-all-start.1
  292.2 5.3 all-gather.2
  298.3 4.5 gather_fusion.3
  303.1 14.6 %all-to-all-done.1 = bf16[8,96,768]{2,1,0:T(8,128)(2,1)} async-done(((bf16[8,96,768]{2,1,0:T(8,128)(2,1)}), bf16[8,96,768]{2,1,0:T(8,128)(2,1)}, u32[]{:S(2)}, u32[]{:S(2)}) %all-to-all-start.1) | async-done | bytes 1179680 | tf_op jit(solution)/shard_map/all_to_all | solution.py:270
  331.1 28.3 %all-to-all-done.2 = bf16[8,96,768]{2,1,0:T(8,128)(2,1)S(1)} async-done(((bf16[8,96,768]{2,1,0:T(8,128)(2,1)}), bf16[8,96,768]{2,1,0:T(8,128)(2,1)S(1)}, u32[]{:S(2)}, u32[]{:S(2)}) %all-to-all-start.2) | async-done | bytes 1179680 | tf_op jit(solution)/shard_map/all_to_all | solution.py:294
  359.5 10.1 multiply_convert_fusion.2
  369.6 7.0 fusion.46
  376.7 4.8 fusion.58
  383.1 4.4 all-to-all-start.3
  388.0 4.2 fusion.104
  392.2 4.3 fusion.105
  396.5 4.8 multiply_convert_fusion.4
  405.2 35.7 %all-to-all-done.3 = f32[8,96,768]{2,1,0:T(8,128)} async-done(((f32[8,96,768]{2,1,0:T(8,128)}), f32[8,96,768]{2,1,0:T(8,128)}, u32[]{:S(2)}, u32[]{:S(2)}) %all-to-all-start.3) | async-done | bytes 2359328 | tf_op jit(solution)/shard_map/all_to_all | solution.py:316
  440.9 8.9 scatter_custom_fusion.3
  456.6 108.0 %while.31 = (s32[]{:T(128)}, f32[12,256,64]{1,2,0:T(8,128)}, bf16[12,1024,64]{1,2,0:T(8,128)(2,1)}, bf16[12,1024,64]{1,2,0:T(8,128)(2,1)}, bf16[12,256,64]{2,1,0...) while((s32[]{:T(128)}, f32[12,256,64]{1,2,0:T(8,128)}, ...), condition=%wide.region_27.28_spmd.clone.clone, body=%wide.region_25.27_spmd.clone.sunk.clone | while | flops 170475264 | bytes 9448553 | solution.py:350
  565.2 3.9 convolution_convert_fusion.3
  569.3 4.0 convolution_convert_fusion.2
  581.0 10.0 reduce-scatter.16.cloned.1.call-done
  599.5 22.8 %reduce-scatter.18.cloned.1.call-done = bf16[256,768]{0,1:T(8,128)(2,1)} async-done(((bf16[1024,768]{0,1:T(8,128)(2,1)}), bf16[256,768]{0,1:T(8,128)(2,1)}) %reduce-scatter.18.cloned.1.call-update) | async-done | bytes 393232 | tf_op jit(solution)/shard_map/reduce_scatter | solution.py:359
  625.0 8.5 convolution_convert_fusion
  633.6 8.6 convert_bitcast_fusion.1
  642.2 8.6 copy.205
  651.0 8.4 convert_bitcast_fusion
  659.4 8.6 copy.207
  668.7 35.7 %reduce-scatter.30.cloned.1.call-done = bf16[192,2048]{1,0:T(8,128)(2,1)} async-done(((bf16[768,2048]{1,0:T(8,128)(2,1)}), bf16[192,2048]{1,0:T(8,128)(2,1)}) %reduce-scatter.30.cloned.1.call-update) | async-done | bytes 786448 | tf_op jit(solution)/shard_map/reduce_scatter | solution.py:417
  704.4 40.4 %reduce-scatter.32.cloned.1.call-done = bf16[512,768]{1,0:T(8,128)(2,1)} async-done(((bf16[2048,768]{1,0:T(8,128)(2,1)}), bf16[512,768]{1,0:T(8,128)(2,1)}) %reduce-scatter.32.cloned.1.call-update) | async-done | bytes 786448 | tf_op jit(solution)/shard_map/reduce_scatter | solution.py:420
  747.8 8.9 scatter_custom_fusion.2
  760.5 7.0 reduce-scatter.40.cloned.1.call-done
  768.4 27.6 %reduce-scatter.26.cloned.1.call-done = bf16[192,768]{1,0:T(8,128)(2,1)} async-done(((bf16[768,768]{1,0:T(8,128)(2,1)}), bf16[192,768]{1,0:T(8,128)(2,1)}) %reduce-scatter.26.cloned.1.call-update) | async-done | bytes 294928 | tf_op jit(solution)/shard_map/reduce_scatter | solution.py:408
  799.8 6.4 all-reduce.9
  811.4 12.8 %reduce-scatter.22.cloned.1.call-done = bf16[192,768]{1,0:T(8,128)(2,1)} async-done(((bf16[768,768]{1,0:T(8,128)(2,1)}), bf16[192,768]{1,0:T(8,128)(2,1)}) %reduce-scatter.22.cloned.1.call-update) | async-done | bytes 294928 | tf_op jit(solution)/shard_map/reduce_scatter | solution.py:402
  824.2 29.1 %reduce-scatter.20.cloned.1.call-done = bf16[192,768]{1,0:T(8,128)(2,1)} async-done(((bf16[768,768]{1,0:T(8,128)(2,1)}), bf16[192,768]{1,0:T(8,128)(2,1)}) %reduce-scatter.20.cloned.1.call-update) | async-done | bytes 294928 | tf_op jit(solution)/shard_map/reduce_scatter | solution.py:399
  853.2 28.9 %reduce-scatter.24.cloned.1.call-done = bf16[192,768]{1,0:T(8,128)(2,1)} async-done(((bf16[768,768]{1,0:T(8,128)(2,1)}), bf16[192,768]{1,0:T(8,128)(2,1)}) %reduce-scatter.24.cloned.1.call-update) | async-done | bytes 294928 | tf_op jit(solution)/shard_map/reduce_scatter | solution.py:405
  882.1 278.8 %all-reduce.12 = (f32[192]{0:T(256)}, f32[192,768]{1,0:T(8,128)}, f32[192,768]{1,0:T(8,128)}, f32[192,768]{1,0:T(8,128)}, f32[192,768]{1,0:T(8,128)}, /*index=5*...) all-reduce(f32[192]{0:T(256)} %dynamic-slice_convert_fusion.1, ...), channel_id=1, replica_groups=mesh['ep'=8,'fs'=4] {'ep'}, use_global_device_ids=true, to_apply=%region_33.34 | all-reduce | flops 1772928 | bytes 10638336 | tf_op jit(solution)/shard_map/psum | solution.py:438
  (422 shorter events, 283.1 us)
Async XLA Ops:
  7.2 41.6 %copy-start = (bf16[256,768]{1,0:T(8,128)(2,1)S(1)}, bf16[256,768]{1,0:T(8,128)(2,1)}, u32[]{:S(2)}) copy-start(bf16[256,768]{1,0:T(8,128)(2,1)} %param.21) | copy-start | bytes 1179652
  7.2 22.6 %all-gather.16.cloned.1.call-start = ((), (), s32[]{:S(2)}) async-start(), calls=%async_computation.17 | async-start | bytes 1474560 | tf_op jit(solution)/shard_map/all_gather | solution.py:115
  7.9 40.9 %all-gather.18.cloned.1.call-start = ((), (), s32[]{:S(2)}) async-start(), calls=%async_computation.18 | async-start | bytes 1474560 | tf_op jit(solution)/shard_map/all_gather | solution.py:116
  8.7 59.2 %all-gather.22.cloned.1.call-start = ((), (), s32[]{:S(2)}) async-start(), calls=%async_computation.20 | async-start | bytes 1474560 | tf_op jit(solution)/shard_map/all_gather | solution.py:117
  9.4 113.8 %all-gather.20.cloned.1.call-start = ((), (), s32[]{:S(2)}) async-start(), calls=%async_computation.19 | async-start | bytes 1966080 | tf_op jit(solution)/shard_map/all_gather | solution.py:146
  21.5 46.3 %copy-start.26 = (f32[768]{0:T(1024)}, f32[768]{0:T(1024)S(1)}, u32[]{:S(2)}) copy-start(f32[768]{0:T(1024)S(1)} %convert_element_type.271) | copy-start | bytes 9220
  23.3 44.6 %copy-start.31 = (f32[256]{0:T(256)}, f32[256]{0:T(256)S(1)}, u32[]{:S(2)}) copy-start(f32[256]{0:T(256)S(1)} %get-tuple-element.394) | copy-start | bytes 3076
  23.5 27.2 %copy-start.22 = (f32[256,32]{0,1:T(8,128)}, f32[256,32]{0,1:T(8,128)S(1)}, u32[]{:S(2)}) copy-start(f32[256,32]{0,1:T(8,128)S(1)} %get-tuple-element.391) | copy-start | bytes 98308
  23.5 27.2 %copy-start.24 = (f32[256,32]{0,1:T(8,128)}, f32[256,32]{0,1:T(8,128)S(1)}, u32[]{:S(2)}) copy-start(f32[256,32]{0,1:T(8,128)S(1)} %get-tuple-element.392) | copy-start | bytes 98308
  51.0 20.1 %copy-start.14 = (bf16[768,1024]{1,0:T(8,128)(2,1)S(1)}, bf16[768,1024]{1,0:T(8,128)(2,1)}, u32[]{:S(2)}) copy-start(bf16[768,1024]{1,0:T(8,128)(2,1)} %param.35) | copy-start | bytes 4718596
  51.8 75.5 %all-gather.24.cloned.1.call-start = ((), (), s32[]{:S(2)}) async-start(), calls=%async_computation.21 | async-start | bytes 1966080 | tf_op jit(solution)/shard_map/all_gather | solution.py:147
  70.5 113.8 %all-gather.26.cloned.1.call-start = ((), (), s32[]{:S(2)}) async-start(), calls=%async_computation.22 | async-start | bytes 1474560 | tf_op jit(solution)/shard_map/all_gather | solution.py:118
  71.0 154.1 %all-gather.34.cloned.1.call-start = ((), (), s32[]{:S(2)}) async-start(), calls=%async_computation.26 | async-start | bytes 7864320 | tf_op jit(solution)/shard_map/all_gather | solution.py:225
  72.7 161.1 %all-gather.36.cloned.1.call-start = ((), (), s32[]{:S(2)}) async-start(), calls=%async_computation.27 | async-start | bytes 7864320 | tf_op jit(solution)/shard_map/all_gather | solution.py:226
  75.3 200.3 %all-gather.38.cloned.1.call-start = ((), (), s32[]{:S(2)}) async-start(), calls=%async_computation.28 | async-start | bytes 7864320 | tf_op jit(solution)/shard_map/all_gather | solution.py:227
  191.2 32.8 %all-to-all-start = ((bf16[8,96,768]{2,1,0:T(8,128)(2,1)}), bf16[8,96,768]{2,1,0:T(8,128)(2,1)S(1)}, u32[]{:S(2)}, u32[]{:S(2)}) async-start(bf16[8,96,768]{2,1,0:T(8,128)(2,1)} %bitcast.26), calls=%async_computation | async-start | bytes 2359296 | tf_op jit(solution)/shard_map/all_to_all | solution.py:260
  194.8 193.2 %all-gather.28.cloned.1.call-start = ((), (), s32[]{:S(2)}) async-start(), calls=%async_computation.23 | async-start | bytes 3932160 | tf_op jit(solution)/shard_map/all_gather | solution.py:120
  283.1 34.6 %all-to-all-start.1 = ((bf16[8,96,768]{2,1,0:T(8,128)(2,1)}), bf16[8,96,768]{2,1,0:T(8,128)(2,1)}, u32[]{:S(2)}, u32[]{:S(2)}) async-start(bf16[8,96,768]{2,1,0:T(8,128)(2,1)} %bitcast.37), calls=%async_computation.1 | async-start | bytes 2359296 | tf_op jit(solution)/shard_map/all_to_all | solution.py:270
  288.7 103.6 %all-gather.30.cloned.1.call-start = ((), (), s32[]{:S(2)}) async-start(), calls=%async_computation.24 | async-start | bytes 3932160 | tf_op jit(solution)/shard_map/all_gather | solution.py:121
  326.7 32.6 %all-to-all-start.2 = ((bf16[8,96,768]{2,1,0:T(8,128)(2,1)}), bf16[8,96,768]{2,1,0:T(8,128)(2,1)S(1)}, u32[]{:S(2)}, u32[]{:S(2)}) async-start(bf16[8,96,768]{2,1,0:T(8,128)(2,1)} %fusion.56), calls=%async_computation.2 | async-start | bytes 2359296 | tf_op jit(solution)/shard_map/all_to_all | solution.py:294
  330.5 66.1 %all-gather.32.cloned.1.call-start = ((), (), s32[]{:S(2)}) async-start(), calls=%async_computation.25 | async-start | bytes 3932160 | tf_op jit(solution)/shard_map/all_gather | solution.py:122
  359.5 10.1 copy-start.17
  383.1 57.8 %all-to-all-start.3 = ((f32[8,96,768]{2,1,0:T(8,128)}), f32[8,96,768]{2,1,0:T(8,128)}, u32[]{:S(2)}, u32[]{:S(2)}) async-start(f32[8,96,768]{2,1,0:T(8,128)} %bitcast.293), calls=%async_computation.3 | async-start | bytes 4718592 | tf_op jit(solution)/shard_map/all_to_all | solution.py:316
  387.5 203.5 %reduce-scatter.16.cloned.1.call-start = ((), (), s32[]{:S(2)}) async-start(), calls=%async_computation.29 | async-start | bytes 1966080 | tf_op jit(solution)/shard_map/reduce_scatter | solution.py:356
  404.0 45.8 %copy-start.29 = (bf16[768,16]{0,1:T(8,128)(2,1)S(1)}, bf16[768,16]{0,1:T(8,128)(2,1)}, u32[]{:S(2)}) copy-start(bf16[768,16]{0,1:T(8,128)(2,1)} %copy-done.28) | copy-start | bytes 73732
  404.1 45.8 %copy-start.36 = (f32[256]{0:T(256)S(1)}, f32[256]{0:T(256)}, u32[]{:S(2)}) copy-start(f32[256]{0:T(256)} %copy-done.35) | copy-start | bytes 3076
  405.2 47.0 %copy-start.41 = (f32[256]{0:T(256)S(1)}, f32[256]{0:T(256)}, u32[]{:S(2)}) copy-start(f32[256]{0:T(256)} %get-tuple-element.395) | copy-start | bytes 3076
  564.6 57.8 %reduce-scatter.18.cloned.1.call-start = ((), (), s32[]{:S(2)}) async-start(), calls=%async_computation.30 | async-start | bytes 1966080 | tf_op jit(solution)/shard_map/reduce_scatter | solution.py:359
  565.1 103.5 %reduce-scatter.28.cloned.1.call-start = ((), (), s32[]{:S(2)}) async-start(), calls=%async_computation.35 | async-start | bytes 3932160 | tf_op jit(solution)/shard_map/reduce_scatter | solution.py:414
  569.1 135.3 %reduce-scatter.30.cloned.1.call-start = ((), (), s32[]{:S(2)}) async-start(), calls=%async_computation.36 | async-start | bytes 3932160 | tf_op jit(solution)/shard_map/reduce_scatter | solution.py:417
  573.4 171.4 %reduce-scatter.32.cloned.1.call-start = ((), (), s32[]{:S(2)}) async-start(), calls=%async_computation.37 | async-start | bytes 3932160 | tf_op jit(solution)/shard_map/reduce_scatter | solution.py:420
  577.2 190.4 %reduce-scatter.40.cloned.1.call-start = ((), (), s32[]{:S(2)}) async-start(), calls=%async_computation.41 | async-start | bytes 245760
  578.3 13.8 %copy-start.23 = (f32[256,32]{0,1:T(8,128)S(1)}, f32[256,32]{0,1:T(8,128)}, u32[]{:S(2)}) copy-start(f32[256,32]{0,1:T(8,128)} %copy-done.22) | copy-start | bytes 98308
  578.3 13.8 %copy-start.25 = (f32[256,32]{0,1:T(8,128)S(1)}, f32[256,32]{0,1:T(8,128)}, u32[]{:S(2)}) copy-start(f32[256,32]{0,1:T(8,128)} %copy-done.24) | copy-start | bytes 98308
  578.3 217.7 %reduce-scatter.26.cloned.1.call-start = ((), (), s32[]{:S(2)}) async-start(), calls=%async_computation.34 | async-start | bytes 1474560 | tf_op jit(solution)/shard_map/reduce_scatter | solution.py:408
  580.9 13.3 %copy-start.27 = (f32[768]{0:T(1024)S(1)}, f32[768]{0:T(1024)}, u32[]{:S(2)}) copy-start(f32[768]{0:T(1024)} %copy-done.26) | copy-start | bytes 9220
  580.9 13.3 %copy-start.32 = (f32[256]{0:T(256)S(1)}, f32[256]{0:T(256)}, u32[]{:S(2)}) copy-start(f32[256]{0:T(256)} %copy-done.31) | copy-start | bytes 3076
  580.9 243.3 %reduce-scatter.22.cloned.1.call-start = ((), (), s32[]{:S(2)}) async-start(), calls=%async_computation.32 | async-start | bytes 1474560 | tf_op jit(solution)/shard_map/reduce_scatter | solution.py:402
  595.9 257.3 %reduce-scatter.20.cloned.1.call-start = ((), (), s32[]{:S(2)}) async-start(), calls=%async_computation.31 | async-start | bytes 1474560 | tf_op jit(solution)/shard_map/reduce_scatter | solution.py:399
  599.4 282.7 %reduce-scatter.24.cloned.1.call-start = ((), (), s32[]{:S(2)}) async-start(), calls=%async_computation.33 | async-start | bytes 1474560 | tf_op jit(solution)/shard_map/reduce_scatter | solution.py:405
  625.0 535.9 %reduce-scatter.38.cloned.1.call-start = ((), (), s32[]{:S(2)}) async-start(), calls=%async_computation.40 | async-start | bytes 7864320 | tf_op jit(solution)/shard_map/reduce_scatter | solution.py:470
  633.5 530.7 %reduce-scatter.34.cloned.1.call-start = ((), (), s32[]{:S(2)}) async-start(), calls=%async_computation.38 | async-start | bytes 7864320 | tf_op jit(solution)/shard_map/reduce_scatter | solution.py:454
  650.8 516.5 %reduce-scatter.36.cloned.1.call-start = ((), (), s32[]{:S(2)}) async-start(), calls=%async_computation.39 | async-start | bytes 7864320 | tf_op jit(solution)/shard_map/reduce_scatter | solution.py:462
  760.5 37.5 %copy-start.2 = (bf16[768,768]{1,0:T(8,128)(2,1)S(1)}, bf16[768,768]{1,0:T(8,128)(2,1)}, u32[]{:S(2)}) copy-start(bf16[768,768]{1,0:T(8,128)(2,1)} %all-gather.18.cloned.1.call-done) | copy-start | bytes 3538948
  760.5 37.5 %copy-start.8 = (bf16[256,12,64]{0,2,1:T(8,128)(2,1)S(1)}, bf16[256,12,64]{0,2,1:T(8,128)(2,1)}, u32[]{:S(2)}) copy-start(bf16[256,12,64]{0,2,1:T(8,128)(2,1)} %copy-done.7) | copy-start | bytes 1179652
  768.4 30.2 %copy-start.13 = (bf16[256,768]{0,1:T(8,128)(2,1)S(1)}, bf16[256,768]{0,1:T(8,128)(2,1)}, u32[]{:S(2)}) copy-start(bf16[256,768]{0,1:T(8,128)(2,1)} %reduce-scatter.18.cloned.1.call-done) | copy-start | bytes 1179652
  798.6 83.5 %copy-start.20 = (bf16[192,2048]{1,0:T(8,128)(2,1)S(1)}, bf16[192,2048]{1,0:T(8,128)(2,1)}, u32[]{:S(2)}) copy-start(bf16[192,2048]{1,0:T(8,128)(2,1)} %reduce-scatter.28.cloned.1.call-done) | copy-start | bytes 2359300
  799.8 82.3 %copy-start.21 = (bf16[192,2048]{1,0:T(8,128)(2,1)S(1)}, bf16[192,2048]{1,0:T(8,128)(2,1)}, u32[]{:S(2)}) copy-start(bf16[192,2048]{1,0:T(8,128)(2,1)} %reduce-scatter.30.cloned.1.call-done) | copy-start | bytes 2359300
  (27 other events, 97.4 us)
Sparse Core Ops, SparseCore 0:
  9.6 20.1 all-gather.15
  31.3 17.4 all-gather.17
  50.4 17.4 all-gather.21
  69.9 19.9 all-gather.19
  91.8 19.7 all-gather.23
  113.0 17.4 all-gather.25
  132.6 46.4 all-gather.33
  181.2 46.4 all-gather.35
  229.3 46.3 all-gather.37
  277.1 28.7 all-gather.27
  307.4 28.5 all-gather.29
  337.4 28.5 all-gather.31
  564.7 26.2 reduce-scatter.15
  594.1 28.1 reduce-scatter.17
  625.3 37.9 reduce-scatter.27
  666.4 37.9 reduce-scatter.29
  706.8 37.9 reduce-scatter.31
  747.8 19.6 reduce-scatter.39
  770.3 25.6 reduce-scatter.25
  798.4 25.7 reduce-scatter.21
  827.5 25.7 reduce-scatter.19
  856.4 25.6 reduce-scatter.23
  884.8 58.3 reduce-scatter.37
  945.6 58.3 reduce-scatter.33
  1006.7 58.3 reduce-scatter.35
where the time goes:
time: 1190 us; the launch traced here: 1180 us
  waiting for transfers between devices  386 us (32%)
  blocking collectives  339 us (28%)
  matrix products  249 us (21%)
  local copies, waits for them, and re-layouts  115 us (10%)
  other arithmetic  50 us (4%)
  starting transfers between devices  19.2 us (2%)
  between operations  16.7 us (1%)
    psum x1, blocking collectives, shards(): lax.psum((sum_gain_one, sum_query_w, sum_key_w, sum_value_w, sum_out_w, s...  279 us
    dot_general x44, matrix products, contract_cols(): lax.dot_general(left_op, right_op, (((1,), (1,)), ((), ())), preferred_el...  64.9 us
    dot_general x32, matrix products, contract_rows(): lax.dot_general(left_op, right_op, (((0,), (0,)), ((), ())), preferred_el...  60.8 us
    dot_general x32, matrix products, matmul(): return jnp.dot(left_op, right_op, preferred_element_type=jnp.float32)  59.5 us
    all_gather x1, blocking collectives, shards(): all_counts = lax.all_gather(counts[None], ('ep', 'fs'), axis=0, tiled=True)  40.6 us
    reduce_scatter x1, waiting for transfers between devices, shards(): lax.psum_scatter(grad_sdown.astype(jnp.bfloat16), 'fs', scatter_dimension...  40.4 us
    reduce_scatter x1, waiting for transfers between devices, shards(): lax.psum_scatter(grad_sup_w.astype(jnp.bfloat16), 'fs', scatter_dimension...  35.7 us
    all_to_all x1, waiting for transfers between devices, shards(): lax.all_to_all(source_layout(din_rows), 'ep', split_axis=0, concat_axis=0...  35.7 us
  transfers between devices with their start and end apart: 29, of which 17 were waited for; matrix products, arithmetic and copies ran while one was open for 24% of the time, Pallas kernels for 0%

commit v1 on v0

v1 whole, which is shorter than its diff:
```python
import jax
import jax.numpy as jnp
from jax import lax
from jax.sharding import Mesh
from jax.sharding import PartitionSpec as P

HEADS = 12
EXPERTS = 16
MOST = 48

EPS = 1e-06
SCALE = 0.125
NEG = -1e30
LOW = jnp.bfloat16
WIDE = jnp.float32
ALL = ("ep", "fx", "fc")
SEQ = ("fx", "fc")
SWAP = [(0, 1), (1, 0)]


def matmul(left_op, right_op):
    return jnp.dot(left_op, right_op, preferred_element_type=WIDE)


def contract_rows(left_op, right_op):
    return lax.dot_general(left_op, right_op, (((0,), (0,)), ((), ())), preferred_element_type=WIDE)


def contract_cols(left_op, right_op):
    return lax.dot_general(left_op, right_op, (((1,), (1,)), ((), ())), preferred_element_type=WIDE)


def rms_forward(values, gain_vec):
    inverse = lax.rsqrt(jnp.mean(values * values, -1, keepdims=True) + EPS)
    return (values * inverse * gain_vec, inverse)


def rms_backward(upstream, values, inverse, gain_vec):
    scaled = upstream * gain_vec
    return inverse * scaled - values * inverse**3 * jnp.mean(scaled * values, -1, keepdims=True)


def rope_tables(positions, half_size):
    freq = jnp.exp(-jnp.log(10000.0) * jnp.arange(half_size).astype(WIDE) / half_size)
    angle = positions.astype(WIDE)[:, None] * freq[None, :]
    return (jnp.cos(angle), jnp.sin(angle))


def rotate(values, cosine, sine_tab):
    half_size = values.shape[-1] // 2
    first_half, second_half = (values[..., :half_size], values[..., half_size:])
    cosine, sine_tab = (cosine[:, None, :], sine_tab[:, None, :])
    return jnp.concatenate(
        [
            first_half * cosine - second_half * sine_tab,
            second_half * cosine + first_half * sine_tab,
        ],
        -1,
    )


def silu_grad(gate_val):
    sigma = jax.nn.sigmoid(gate_val)
    return (gate_val * sigma, sigma * (1.0 + gate_val * (1.0 - sigma)))


def ordered(own, other, index, axis=0):
    lead = jnp.concatenate([jnp.expand_dims(own, axis), jnp.expand_dims(other, axis)], axis)
    swapped = jnp.concatenate([jnp.expand_dims(other, axis), jnp.expand_dims(own, axis)], axis)
    return jnp.where(index == 0, lead, swapped)


def gather_seq(block):
    far = lax.ppermute(block, "fx", SWAP)
    pair = ordered(block, far, lax.axis_index("fx"))
    near = lax.ppermute(pair, "fc", SWAP)
    quad = ordered(pair, near, lax.axis_index("fc"), 1)
    return quad.reshape((4 * block.shape[0],) + block.shape[1:])


def scatter_seq(total):
    rows = total.shape[0] // 4
    cut = total.reshape((2, 2, rows) + total.shape[1:])
    core, side = (lax.axis_index("fc"), lax.axis_index("fx"))
    keep = lax.dynamic_index_in_dim(cut, core, 1, keepdims=False)
    give = lax.dynamic_index_in_dim(cut, 1 - core, 1, keepdims=False)
    keep = keep + lax.ppermute(give.astype(LOW), "fc", SWAP).astype(WIDE)
    mine = lax.dynamic_index_in_dim(keep, side, 0, keepdims=False)
    give = lax.dynamic_index_in_dim(keep, 1 - side, 0, keepdims=False)
    return mine + lax.ppermute(give.astype(LOW), "fx", SWAP).astype(WIDE)


def exchange(blocks, axes):
    return lax.all_to_all(blocks, axes, split_axis=0, concat_axis=0, tiled=True)


def spread_whole(vector, axes, count):
    return exchange(jnp.broadcast_to(vector[None], (count,) + vector.shape), axes)


def experts_chip(rows_sent, grads_sent, slot_weight, weg, weu, wed):
    width = rows_sent.shape[1]
    axes = ("ep", "fx")
    got_grads = exchange(grads_sent.reshape(EXPERTS, MOST, width), axes).reshape(-1, width)
    gate_mat = jnp.concatenate([weg, lax.ppermute(weg, "fc", SWAP)], 1)
    up_mat = jnp.concatenate([weu, lax.ppermute(weu, "fc", SWAP)], 1)
    down_mat = jnp.concatenate([wed, lax.ppermute(wed, "fc", SWAP)], 0)
    hidden = weg.shape[1]
    grad_hidden = contract_cols(got_grads, down_mat)
    got_weight = exchange(slot_weight.reshape(EXPERTS, MOST), axes).reshape(-1, 1)
    own_rows = exchange(rows_sent.reshape(EXPERTS, MOST, width), axes).reshape(-1, width)
    gate_val = matmul(own_rows, gate_mat)
    up_val = matmul(own_rows, up_mat)
    silu_val, slope_val = silu_grad(gate_val)
    hidden_wide = silu_val * up_val
    hidden_val = hidden_wide.astype(LOW)
    row_dot = jnp.sum(hidden_val.astype(WIDE) * grad_hidden, -1)
    scaled = got_weight * grad_hidden
    grad_gate = (scaled * up_val * slope_val).astype(LOW)
    grad_up = (scaled * silu_val).astype(LOW)
    din_rows = contract_cols(grad_gate, gate_mat) + contract_cols(grad_up, up_mat)
    back_din = exchange(din_rows.astype(LOW).reshape(EXPERTS, MOST, width), axes)
    back_dot = exchange(row_dot.reshape(EXPERTS, MOST), axes)
    out_rows = matmul(hidden_val, down_mat)
    back_out = exchange(out_rows.astype(LOW).reshape(EXPERTS, MOST, width), axes)
    own_grads = (got_weight * got_grads.astype(WIDE)).astype(LOW)

    def finish(full, axis):
        own = lax.slice_in_dim(full, 0, hidden, axis=axis)
        peer = lax.slice_in_dim(full, hidden, 2 * hidden, axis=axis)
        return own + lax.ppermute(peer.astype(LOW), "fc", SWAP).astype(WIDE)

    gate_g = finish(contract_rows(own_rows, grad_gate), 1)
    up_g = finish(contract_rows(own_rows, grad_up), 1)
    down_g = finish(contract_rows(hidden_val, own_grads), 0)
    return (
        back_out.reshape(-1, width),
        back_din.reshape(-1, width),
        back_dot.reshape(-1),
        gate_g,
        up_g,
        down_g,
    )


def experts_spread(rows_sent, grads_sent, slot_weight, weg, weu, wed):
    ep_count = lax.axis_size("ep")
    width = rows_sent.shape[1]
    local_count = max(1, EXPERTS // ep_count)
    replicas = max(1, ep_count // EXPERTS)
    groups = EXPERTS // local_count
    gate_cols, up_cols, down_rows = (
        lax.all_gather(weg, SEQ, axis=1, tiled=True),
        lax.all_gather(weu, SEQ, axis=1, tiled=True),
        lax.all_gather(wed, SEQ, axis=0, tiled=True),
    )
    hidden_part = gate_cols.shape[1] // local_count
    gate_local = gate_cols.reshape(width, local_count, hidden_part).transpose(1, 0, 2)
    up_local = up_cols.reshape(width, local_count, hidden_part).transpose(1, 0, 2)
    down_local = down_rows.reshape(local_count, hidden_part, width)

    def spread(buffer):
        last = buffer.shape[-1]
        wide = buffer.reshape(groups, 1, local_count * MOST, last)
        wide = jnp.broadcast_to(wide, (groups, replicas, local_count * MOST, last))
        return exchange(wide.reshape(ep_count, local_count * MOST, last), "ep")

    def collect(buffer):
        last = buffer.shape[-1]
        return jnp.sum(
            exchange(buffer, "ep").astype(WIDE).reshape(groups, replicas, local_count * MOST, last),
            1,
        ).reshape(EXPERTS * MOST, last)

    def owner_layout(received):
        last = received.shape[-1]
        return (
            received.reshape(ep_count, local_count, MOST, last)
            .transpose(1, 0, 2, 3)
            .reshape(local_count, ep_count * MOST, last)
        )

    def source_layout(owned):
        last = owned.shape[-1]
        return (
            owned.reshape(local_count, ep_count, MOST, last)
            .transpose(1, 0, 2, 3)
            .reshape(ep_count, local_count * MOST, last)
        )

    def batched(spec, left_op, right_op):
        return jnp.einsum(spec, left_op, right_op, preferred_element_type=WIDE)

    own_rows = owner_layout(spread(rows_sent))
    got_grads = owner_layout(spread(grads_sent))
    got_weight = owner_layout(spread(slot_weight[:, None]))
    gate_val = batched("lrd,ldh->lrh", own_rows, gate_local)
    up_val = batched("lrd,ldh->lrh", own_rows, up_local)
    silu_val, slope_val = silu_grad(gate_val)
    hidden_val = (silu_val * up_val).astype(LOW)
    out_rows = batched("lrh,lhd->lrd", hidden_val, down_local)
    back_out = collect(source_layout(out_rows.astype(LOW)))
    grad_hidden = batched("lrd,lhd->lrh", got_grads, down_local)
    row_dot = jnp.sum(hidden_val.astype(WIDE) * grad_hidden, -1, keepdims=True)
    back_dot = collect(source_layout(row_dot))
    scaled = got_weight * grad_hidden
    own_grads = (got_weight * got_grads.astype(WIDE)).astype(LOW)
    grad_gate = (scaled * up_val * slope_val).astype(LOW)
    grad_up = (scaled * silu_val).astype(LOW)
    din_rows = batched("lrh,ldh->lrd", grad_gate, gate_local)
    din_rows = din_rows + batched("lrh,ldh->lrd", grad_up, up_local)
    back_din = collect(source_layout(din_rows.astype(LOW)))
    grad_gate_w = batched("lrd,lrh->ldh", own_rows, grad_gate)
    grad_up_w = batched("lrd,lrh->ldh", own_rows, grad_up)
    grad_down_w = batched("lrh,lrd->lhd", hidden_val, own_grads)

    def share(full, axis):
        return lax.psum_scatter(
            full.astype(LOW), SEQ, scatter_dimension=axis, tiled=True
        ).astype(WIDE)

    return (
        back_out,
        back_din,
        back_dot[:, 0],
        share(grad_gate_w.transpose(1, 0, 2).reshape(width, local_count * hidden_part), 1),
        share(grad_up_w.transpose(1, 0, 2).reshape(width, local_count * hidden_part), 1),
        share(grad_down_w.reshape(local_count * hidden_part, width), 0),
    )


def shards(
    tokens,
    cotangent,
    routes,
    priority,
    gain_attn,
    w_query,
    w_key,
    w_value,
    w_out,
    gain_ffn,
    w_shared_gate,
    w_shared_up,
    w_shared_down,
    w_router,
    w_expert_gate,
    w_expert_up,
    w_expert_down,
):
    tok_rows, width = tokens.shape
    rows_w = w_query.shape[0]
    fs_count = lax.axis_size("fx") * lax.axis_size("fc")
    ep_count = lax.axis_size("ep")
    devices = ep_count * fs_count
    seq_len = tok_rows * fs_count
    head_count = HEADS // fs_count
    head_size = width // HEADS
    fs_index = lax.axis_index("fx") * lax.axis_size("fc") + lax.axis_index("fc")
    my_rank = lax.axis_index("ep") * fs_count + fs_index

    x_all = gather_seq(tokens)
    qkv_cut = jnp.stack([w_query, w_key, w_value]).reshape(3, rows_w, fs_count, rows_w)
    qkv_got = exchange(qkv_cut.transpose(2, 0, 1, 3), SEQ)
    qkv_mat = qkv_got.transpose(1, 0, 2, 3).reshape(3, width, rows_w)
    small = jnp.concatenate([gain_attn[None], gain_ffn[None], w_router.T], 0)
    small_all = gather_seq(small[None]).transpose(1, 0, 2).reshape(2 + EXPERTS, width)
    gain_one, gain_two, router_t = (small_all[0], small_all[1], small_all[2:])
    dy_all = gather_seq(cotangent)
    out_mat = gather_seq(w_out)
    ff_part = w_shared_gate.shape[1] // fs_count
    up_cut = jnp.stack([w_shared_gate, w_shared_up]).reshape(2, rows_w, fs_count, ff_part)
    up_got = exchange(up_cut.transpose(2, 0, 1, 3), SEQ)
    shared_mat = up_got.transpose(1, 0, 2, 3).reshape(2, width, ff_part)
    sgate_mat, sup_mat = (shared_mat[0], shared_mat[1])

    expert_iota = jnp.arange(EXPERTS)
    classes = jnp.stack([priority, 1 - priority], 1)
    route_hits = (routes[:, :, None] == expert_iota).astype(jnp.int32)
    per_class = jnp.stack(
        [
            jnp.sum(route_hits * (classes == class_id)[:, :, None].astype(jnp.int32), 1)
            for class_id in (0, 1)
        ]
    )
    counts = jnp.sum(per_class, 1)
    all_counts = spread_whole(counts, ALL, devices)
    lower = (jnp.arange(tok_rows)[:, None] > jnp.arange(tok_rows)[None, :]).astype(LOW)
    flat_class = per_class.transpose(1, 0, 2).reshape(tok_rows, 2 * EXPERTS)
    before = (
        matmul(lower, flat_class.astype(LOW))
        .astype(jnp.int32)
        .reshape(tok_rows, 2, EXPERTS)
        .transpose(1, 0, 2)
    )
    earlier = (jnp.arange(devices) < my_rank).astype(jnp.int32)
    ahead = jnp.sum(all_counts * earlier[:, None, None], 0)
    zero_row = jnp.zeros((EXPERTS,), jnp.int32)
    global_table = (
        before + (ahead + jnp.stack([zero_row, jnp.sum(all_counts[:, 0, :], 0)]))[:, None, :]
    )
    local_table = before + jnp.stack([zero_row, counts[0]])[:, None, :]

    def pair_value(class_table):
        picked = jnp.where(
            (classes == 0)[:, :, None], class_table[0][:, None, :], class_table[1][:, None, :]
        )
        return jnp.sum(picked * route_hits, -1)

    capacity = 5 * tok_rows * devices // 32
    kept_mask = (pair_value(global_table) < capacity).astype(WIDE)
    flat_slot = routes * MOST + pair_value(local_table)
    slot_iota = jnp.arange(EXPERTS * MOST)
    slot_hit = flat_slot[:, :, None] == slot_iota
    slot_hit_low = slot_hit.astype(LOW)
    dispatch = slot_hit_low[:, 0] + slot_hit_low[:, 1]
    grads_sent = contract_rows(dispatch, cotangent).astype(LOW)

    x_float = x_all.astype(WIDE)
    normed_one, inverse_one = rms_forward(x_float, gain_one)
    attn_input = normed_one.astype(LOW)
    cosine, sine_tab = rope_tables(jnp.arange(seq_len), head_size // 2)
    head_shape = (seq_len, head_count, head_size)
    query_rot = rotate(matmul(attn_input, qkv_mat[0]).reshape(head_shape), cosine, sine_tab)
    key_rot = rotate(matmul(attn_input, qkv_mat[1]).reshape(head_shape), cosine, sine_tab)
    query_heads = query_rot.astype(LOW).transpose(1, 0, 2)
    key_heads = key_rot.astype(LOW).transpose(1, 0, 2)
    value_heads = (
        matmul(attn_input, qkv_mat[2]).astype(LOW).reshape(head_shape).transpose(1, 0, 2)
    )
    causal = jnp.arange(seq_len)[:, None] >= jnp.arange(seq_len)[None, :]

    def head_forward(query_head, key_head, value_head):
        scores = jnp.where(causal, contract_cols(query_head, key_head) * SCALE, NEG)
        row_max = jnp.max(scores, -1, keepdims=True)
        exp_scores = jnp.exp(scores - row_max)
        row_total = jnp.sum(exp_scores, -1, keepdims=True)
        weights = (exp_scores / row_total).astype(LOW)
        return (matmul(weights, value_head).astype(LOW), row_max + jnp.log(row_total))

    fwd = [head_forward(query_heads[h], key_heads[h], value_heads[h]) for h in range(head_count)]
    attended_own = jnp.concatenate([piece[0] for piece in fwd], -1)
    attended_got = exchange(attended_own.reshape(fs_count, tok_rows, rows_w), SEQ)
    attended_low = attended_got.transpose(1, 0, 2).reshape(tok_rows, width)

    residual = tokens.astype(WIDE) + matmul(attended_low, out_mat)
    normed_two, inverse_two = rms_forward(residual, gain_two)
    ffn_input = normed_two.astype(LOW)
    logits = contract_cols(ffn_input, router_t)
    chosen = jnp.sum(route_hits.astype(WIDE) * logits[:, None, :], -1)
    chosen_exp = jnp.exp(chosen - jnp.max(chosen, -1, keepdims=True))
    gates = chosen_exp / jnp.sum(chosen_exp, -1, keepdims=True)
    pair_weight = gates * kept_mask
    slot_weight = jnp.sum(jnp.where(slot_hit, pair_weight[:, :, None], 0.0), (0, 1))
    rows_sent = contract_rows(dispatch, ffn_input).astype(LOW)

    pair_of_cores = EXPERTS == ep_count * lax.axis_size("fx")
    experts = experts_chip if pair_of_cores else experts_spread
    slot_out, slot_din, slot_dot, expert_gate_g, expert_up_g, expert_down_g = experts(
        rows_sent, grads_sent, slot_weight, w_expert_gate, w_expert_up, w_expert_down
    )

    ffn_all = gather_seq(ffn_input)
    shared_gate = matmul(ffn_all, sgate_mat)
    shared_up = matmul(ffn_all, sup_mat)
    shared_silu, shared_slope = silu_grad(shared_gate)
    shared_hidden = (shared_silu * shared_up).astype(LOW)
    grad_shidden = contract_cols(dy_all, w_shared_down)
    grad_sgate = (grad_shidden * shared_up * shared_slope).astype(LOW)
    grad_sup = (grad_shidden * shared_silu).astype(LOW)
    shared_din = scatter_seq(contract_cols(grad_sgate, sgate_mat) + contract_cols(grad_sup, sup_mat))
    shared_out = scatter_seq(matmul(shared_hidden, w_shared_down))
    grad_sdown = contract_rows(shared_hidden, dy_all)
    grad_sgate_w = contract_rows(ffn_all, grad_sgate)
    grad_sup_w = contract_rows(ffn_all, grad_sup)
    turned = jnp.stack([grad_sgate_w, grad_sup_w]).astype(LOW)
    turned = exchange(turned.reshape(2, fs_count, rows_w, ff_part).transpose(1, 0, 2, 3), SEQ)
    turned = turned.transpose(1, 2, 0, 3).reshape(2, rows_w, fs_count * ff_part)

    slot_out_low = slot_out.astype(LOW)
    mixed = sum(
        pair_weight[:, j : j + 1] * matmul(slot_hit_low[:, j], slot_out_low) for j in (0, 1)
    )
    output = (residual + shared_out + mixed).astype(LOW)
    grad_weight = jnp.sum(jnp.where(slot_hit, slot_dot, 0.0), -1) * kept_mask
    grad_chosen = gates * (grad_weight - jnp.sum(gates * grad_weight, -1, keepdims=True))
    grad_logits = jnp.sum(route_hits.astype(WIDE) * grad_chosen[:, :, None], 1).astype(LOW)
    grad_ffn = (
        shared_din + matmul(grad_logits, router_t) + matmul(dispatch, slot_din.astype(LOW))
    )
    grad_resid = cotangent.astype(WIDE) + rms_backward(grad_ffn, residual, inverse_two, gain_two)
    grad_branch = grad_resid.astype(LOW)
    gain_part = jnp.sum(grad_ffn * residual * inverse_two, 0)
    branch_all = gather_seq(grad_branch)
    grad_att = contract_cols(branch_all, w_out).astype(LOW)
    grad_out_w = contract_rows(attended_own, branch_all)
    router_part = contract_rows(grad_logits, ffn_input)

    grad_heads = grad_att.reshape(head_shape).transpose(1, 0, 2)

    def head_backward(query_head, key_head, value_head, grad_head, lse_head):
        scores = jnp.where(causal, contract_cols(query_head, key_head) * SCALE, NEG)
        probs = jnp.exp(scores - lse_head)
        grad_probs = contract_cols(grad_head, value_head)
        inner = jnp.sum(probs * grad_probs, -1, keepdims=True)
        grad_scores = (probs * (grad_probs - inner)).astype(LOW)
        grad_query = matmul(grad_scores, key_head) * SCALE
        grad_keys = contract_rows(grad_scores, query_head) * SCALE
        grad_values = contract_rows(probs.astype(LOW), grad_head)
        return (grad_query, grad_keys, grad_values)

    bwd = [
        head_backward(query_heads[h], key_heads[h], value_heads[h], grad_heads[h], fwd[h][1])
        for h in range(head_count)
    ]
    stack3 = [jnp.stack([piece[i] for piece in bwd], 1) for i in range(3)]
    d_query = rotate(stack3[0], cosine, -sine_tab).reshape(seq_len, rows_w).astype(LOW)
    d_keys = rotate(stack3[1], cosine, -sine_tab).reshape(seq_len, rows_w).astype(LOW)
    d_values = stack3[2].reshape(seq_len, rows_w).astype(LOW)
    d_qkv = (d_query, d_keys, d_values)
    grads_qkv = jnp.stack([contract_rows(attn_input, d_one) for d_one in d_qkv]).astype(LOW)
    grad_in = scatter_seq(sum(contract_cols(d_qkv[i], qkv_mat[i]) for i in range(3)))
    own_float = tokens.astype(WIDE)
    own_inverse = lax.rsqrt(jnp.mean(own_float * own_float, -1, keepdims=True) + EPS)
    grad_tokens = grad_resid + rms_backward(grad_in, own_float, own_inverse, gain_one)

    dense = lax.psum(
        (turned, grad_sdown.astype(LOW), grad_out_w.astype(LOW)), "ep"
    )
    sum_sgate_w, sum_sup_w = (dense[0][0].astype(WIDE), dense[0][1].astype(WIDE))
    sum_sdown, sum_out_w = (dense[1].astype(WIDE), dense[2].astype(WIDE))
    small_sum = lax.psum(jnp.concatenate([gain_part[None], router_part], 0), ALL)
    small_own = lax.dynamic_slice_in_dim(small_sum, fs_index * rows_w, rows_w, 1)
    sum_gain_two, sum_router = (small_own[0], small_own[1:].T)
    strip = rows_w // ep_count
    qkv_blocks = grads_qkv.reshape(3, fs_count, ep_count, strip, rows_w).transpose(2, 1, 0, 3, 4)
    qkv_parts = exchange(qkv_blocks.reshape(devices, 3, strip, rows_w), ALL)
    qkv_parts = qkv_parts.reshape(ep_count, fs_count, 3, strip, rows_w).astype(WIDE)
    qkv_sum = jnp.sum(qkv_parts, 0).transpose(1, 2, 0, 3).reshape(3, strip, width).astype(LOW)
    qkv_whole = spread_whole(qkv_sum, "ep", ep_count)
    qkv_whole = qkv_whole.transpose(1, 0, 2, 3).reshape(3, rows_w, width).astype(WIDE)
    sum_gain_one = (
        sum(
            jnp.sum(qkv_whole[i] * mat.astype(WIDE), -1)
            for i, mat in enumerate((w_query, w_key, w_value))
        )
        / gain_attn.astype(WIDE)
    )
    return (
        output,
        grad_tokens,
        sum_gain_one,
        qkv_whole[0],
        qkv_whole[1],
        qkv_whole[2],
        sum_out_w,
        sum_gain_two,
        sum_sgate_w,
        sum_sup_w,
        sum_sdown,
        sum_router,
        expert_gate_g,
        expert_up_g,
        expert_down_g,
    )


def solution(mesh):
    ep_count, fs_count = mesh.devices.shape
    cut_mesh = Mesh(mesh.devices.reshape(ep_count, fs_count // 2, 2), ALL)
    tok = P(ALL, None)
    row = P(SEQ, None)
    return jax.shard_map(
        shards,
        mesh=cut_mesh,
        in_specs=(
            tok,
            tok,
            tok,
            P(ALL),
            P(SEQ),
            row,
            row,
            row,
            row,
            P(SEQ),
            row,
            row,
            row,
            row,
            P(None, ALL),
            P(None, ALL),
            tok,
        ),
        out_specs=(
            tok,
            tok,
            P(SEQ),
            row,
            row,
            row,
            row,
            P(SEQ),
            row,
            row,
            row,
            row,
            P(None, ALL),
            P(None, ALL),
            tok,
        ),
        check_vma=False,
    )
```

time: 1190 us -> 577 us (0.48)
  blocking collectives: 339 us -> 50.9 us
  waiting for transfers between devices: 386 us -> 122 us
  matrix products: 249 us -> 100 us
  starting transfers between devices: 19.2 us -> 90.3 us
  other arithmetic: 50 us -> 101 us
  local copies, waits for them, and re-layouts: 115 us -> 87.1 us
    psum x1, blocking collectives: 279 us -> 50.9 us  [shards(): lax.psum(jnp.concatenate([gain_part[None], router_part], 0), ALL)]
    reduce_scatter x12 -> x0, waiting for transfers between devices: 207 us -> none  [the longest x1 40.4 us: shards(): lax.psum_scatter(grad_sdown.astype(jnp.bfloat16), 'fs', scatter_dimension...]
    dot_general x41 -> x21, matrix products: 124 us -> 35.4 us  [matmul(): return jnp.dot(left_op, right_op, preferred_element_type=WIDE)]
    all_to_all x4 -> x13, waiting for transfers between devices: 107 us -> 28.1 us  [exchange(): return lax.all_to_all(blocks, axes, split_axis=0, concat_axis=0, tiled=True)]
    psum x0 -> x1, waiting for transfers between devices: none -> 64.5 us  [shards(): lax.psum((turned, grad_sdown.astype(LOW), grad_out_w.astype(LOW)), 'ep')]
    all_gather x12 -> x0, waiting for transfers between devices: 59.2 us -> none  [the longest x1 19.9 us: shards(): lax.all_gather(w_expert_down, 'fs', axis=0, tiled=True)]
    all_to_all x4 -> x13, starting transfers between devices: 17.2 us -> 72.1 us  [exchange(): return lax.all_to_all(blocks, axes, split_axis=0, concat_axis=0, tiled=True)]
    all_gather x2 -> x0, blocking collectives: 45.9 us -> none  [the longest x1 40.6 us: shards(): all_counts = lax.all_gather(counts[None], ('ep', 'fs'), axis=0, tiled=True)]
  transfers between devices with their start and end apart: 29 -> 38, of which waited for: 17 -> 8; matrix products, arithmetic and copies ran while one was open for 24% -> 46% of each run, Pallas kernels for 0% -> 0%
where the time goes in v1:
time: 577 us; the launch traced here: 568 us
  waiting for transfers between devices  122 us (21%)
  other arithmetic  101 us (18%)
  matrix products  100 us (17%)
  starting transfers between devices  90.3 us (16%)
  local copies, waits for them, and re-layouts  87.1 us (15%)
  blocking collectives  50.9 us (9%)
  between operations  16.5 us (3%)
    all_to_all x13, starting transfers between devices, exchange(): return lax.all_to_all(blocks, axes, split_axis=0, concat_axis=0, tiled=True)  72.1 us
    psum x1, waiting for transfers between devices, shards(): lax.psum((turned, grad_sdown.astype(LOW), grad_out_w.astype(LOW)), 'ep')  64.5 us
    psum x1, blocking collectives, shards(): lax.psum(jnp.concatenate([gain_part[None], router_part], 0), ALL)  50.9 us
    dot_general x21, matrix products, matmul(): return jnp.dot(left_op, right_op, preferred_element_type=WIDE)  35.4 us
    dot_general x19, matrix products, contract_rows(): lax.dot_general(left_op, right_op, (((0,), (0,)), ((), ())), preferred_el...  32.4 us
    dot_general x17, matrix products, contract_cols(): lax.dot_general(left_op, right_op, (((1,), (1,)), ((), ())), preferred_el...  32.4 us
    ppermute x6, waiting for transfers between devices, gather_seq(): far = lax.ppermute(block, 'fx', SWAP)  29.6 us
    all_to_all x13, waiting for transfers between devices, exchange(): return lax.all_to_all(blocks, axes, split_axis=0, concat_axis=0, tiled=True)  28.1 us
  transfers between devices with their start and end apart: 38, of which 8 were waited for; matrix products, arithmetic and copies ran while one was open for 46% of the time, Pallas kernels for 0%

profile of v1, /device:TPU:0, one launch (start us, length us, event | category | flops | bytes accessed | tf_op | source)
XLA Modules:
  0.0 567.9 jit_solution(1995298785190414826)
XLA Ops:
  10.0 2.9 collective-permute-start.2
  16.3 6.5 %all-to-all-start.3 = ((s32[32,2,16]{2,1,0:T(2,128)}), s32[32,2,16]{2,1,0:T(2,128)}, u32[]{:S(2)}, u32[]{:S(2)}) async-start(s32[32,2,16]{2,1,0:T(2,128)} %broadcast_in_dim.128), calls=%async_computation.3 | async-start | bytes 65536 | tf_op jit(solution)/shard_map/all_to_all | solution.py:94
  25.6 2.7 constant_dynamic-update-slice_fusion.1
  33.4 2.7 constant_dynamic-update-slice_fusion.5
  48.0 4.3 all-to-all-start
  61.5 12.9 %collective-permute-done.4 = bf16[192,768]{1,0:T(8,128)(2,1)S(1)} collective-permute-done((bf16[192,768]{1,0:T(8,128)(2,1)S(1)}, bf16[192,768]{1,0:T(8,128)(2,1)S(1)}, u32[]{:S(2)}, u32[]{:S(2)}) %collective-permute-start.4) | collective-permute-done | bytes 294944 | tf_op jit(solution)/shard_map/ppermute | solution.py:74
  84.6 4.8 all-to-all-start.2
  102.8 2.8 maximum_select_fusion.4
  119.9 4.1 all-to-all-start.1
  136.0 2.6 convolution_convert_fusion.2
  140.5 5.6 all-to-all-start.4
  156.9 2.7 constant_dynamic-update-slice_fusion.2
  174.3 2.6 fusion.117
  176.9 7.2 %all-to-all-start.6 = ((bf16[16,48,768]{2,1,0:T(8,128)(2,1)}), bf16[16,48,768]{2,1,0:T(8,128)(2,1)}, u32[]{:S(2)}, u32[]{:S(2)}) async-start(bf16[16,48,768]{2,1,0:T(8,128)(2,1)} %bitcast.513), calls=%async_computation.6 | async-start | bytes 2359296 | tf_op jit(solution)/shard_map/all_to_all | solution.py:94
  185.8 2.6 copy.277
  188.4 3.7 fusion.24
  196.0 4.6 fusion.119
  200.5 4.6 fusion.120
  205.1 6.3 %all-to-all-done.6 = bf16[16,48,768]{2,1,0:T(8,128)(2,1)} async-done(((bf16[16,48,768]{2,1,0:T(8,128)(2,1)}), bf16[16,48,768]{2,1,0:T(8,128)(2,1)}, u32[]{:S(2)}, u32[]{:S(2)}) %all-to-all-start.6) | async-done | bytes 1179680 | tf_op jit(solution)/shard_map/all_to_all | solution.py:94
  211.4 13.1 %multiply_reduce_fusion = (f32[768]{0:T(1024)}, bf16[768,2048]{1,0:T(8,128)(2,1)}, f32[768,2048]{1,0:T(8,128)}) fusion(f32[768,2048]{1,0:T(8,128)} %fusion.120, f32[768,2048]{1,0:T(8,128)} %fusion.119, bf16[768,768]{1,0:T(8,128)(2,1)} %bitcast.101, bf16[2048,768]{1,0:T(8,128)(2,1)} %copy-done.77), kind=kOutput, calls=%fused_computation.2 | convolution fusion | flops 2430074112 | bytes 26348544 | tf_op jit(solution)/shard_map/dot_general | solution.py:30
  225.9 7.0 %all-to-all-start.7 = ((f32[16,1,48]{2,1,0:T(1,128)}), f32[16,1,48]{2,1,0:T(1,128)}, u32[]{:S(2)}, u32[]{:S(2)}) async-start(f32[16,1,48]{2,1,0:T(1,128)} %all_to_all.52), calls=%async_computation.7 | async-start | bytes 16384 | tf_op jit(solution)/shard_map/all_to_all | solution.py:94
  235.8 4.3 all-to-all-done.7
  247.1 4.1 all-to-all-start.8
  251.2 6.5 %convolution_convert_fusion.1 = bf16[768,768]{1,0:T(8,128)(2,1)} fusion(bf16[768,2048]{1,0:T(8,128)(2,1)} %get-tuple-element.32, bf16[2048,768]{1,0:T(8,128)(2,1)} %copy-done.77), kind=kOutput, calls=%fused_computation.79 | convolution fusion | flops 2416508928 | bytes 7471104 | tf_op jit(solution)/shard_map/dot_general | solution.py:22
  258.3 6.7 %all-to-all-start.5 = ((bf16[16,48,768]{2,1,0:T(8,128)(2,1)}), bf16[16,48,768]{2,1,0:T(8,128)(2,1)}, u32[]{:S(2)}, u32[]{:S(2)}) async-start(bf16[16,48,768]{2,1,0:T(8,128)(2,1)} %bitcast.516), calls=%async_computation.5 | async-start | bytes 2359296 | tf_op jit(solution)/shard_map/all_to_all | solution.py:94
  268.3 8.6 %multiply_convert_fusion.1 = (bf16[768,2048]{1,0:T(8,128)(2,1)S(1)}, bf16[768,2048]{1,0:T(8,128)(2,1)S(1)}) fusion(f32[768,2048]{1,0:T(8,128)} %fusion.119, f32[768,2048]{1,0:T(8,128)} %fusion.120, f32[768,2048]{1,0:T(8,128)} %get-tuple-element.98, f32[768]{0:T(1024)} %mul.684), kind=kLoop, calls=%fused_computation.1 | loop fusion | flops 22020096 | bytes 25168896 | tf_op jit(solution)/shard_map/convert_element_type | solution.py:119
  276.9 2.6 fusion.122
  281.0 3.7 add_convert_fusion
  284.7 5.3 all-to-all-done.5
  290.0 6.3 %all-to-all-start.9 = ((bf16[16,48,768]{2,1,0:T(8,128)(2,1)}), bf16[16,48,768]{2,1,0:T(8,128)(2,1)}, u32[]{:S(2)}, u32[]{:S(2)}) async-start(bf16[16,48,768]{2,1,0:T(8,128)(2,1)} %bitcast.515), calls=%async_computation.9 | async-start | bytes 2359296 | tf_op jit(solution)/shard_map/all_to_all | solution.py:94
  307.7 2.7 fusion.25
  310.5 11.5 %all-to-all-done.9 = bf16[16,48,768]{2,1,0:T(8,128)(2,1)} async-done(((bf16[16,48,768]{2,1,0:T(8,128)(2,1)}), bf16[16,48,768]{2,1,0:T(8,128)(2,1)}, u32[]{:S(2)}, u32[]{:S(2)}) %all-to-all-start.9) | async-done | bytes 1179680 | tf_op jit(solution)/shard_map/all_to_all | solution.py:94
  322.0 4.5 all-to-all-start.12
  330.9 2.6 fusion.102
  335.4 2.7 fusion.125
  338.1 16.7 %collective-permute-done.17 = bf16[256,768]{1,0:T(8,128)(2,1)S(1)} collective-permute-done((bf16[256,768]{1,0:T(8,128)(2,1)S(1)}, bf16[256,768]{1,0:T(8,128)(2,1)S(1)}, u32[]{:S(2)}, u32[]{:S(2)}) %collective-permute-start.17) | collective-permute-done | bytes 393248 | tf_op jit(solution)/shard_map/ppermute | solution.py:74
  355.0 2.7 fusion.126
  361.9 4.1 fusion.30
  369.6 2.8 copy.288
  400.0 5.5 all-to-all-start.10
  405.6 2.7 convolution_convert_fusion.11
  408.4 4.9 slice_add_fusion.2
  413.4 3.7 slice_add_fusion.1
  421.0 3.4 slice_add_fusion
  424.5 50.9 %psum.29 = f32[17,768]{1,0:T(8,128)S(1)} all-reduce(f32[17,768]{1,0:T(8,128)S(1)} %pad_maximum_fusion.6), channel_id=1, replica_groups=mesh['ep'=8,'fx'=2,'fc'=2] {'ep','fx','fc'}, use_global_device_ids=true, to_apply=%region_35.36 | all-reduce | flops 13056 | bytes 104448 | tf_op jit(solution)/shard_map/psum | solution.py:432
  478.8 5.4 all-to-all-start.11
  486.4 64.5 %all-reduce.5.cloned.1.call-done = (bf16[192,768]{1,0:T(8,128)(2,1)}, bf16[2,192,2048]{2,1,0:T(8,128)(2,1)}, bf16[512,768]{1,0:T(8,128)(2,1)}) async-done(((bf16[192,768]{1,0:T(8,128)(2,1)}, bf16[2,192,2048]{2,1,0:T(8,128)(2,1)}, bf16[512,768]{1,0:T(8,128)(2,1)}), (bf16[192,768]{1,0:T(8,128)(2,1)}, bf16[2,192,2048]{2,1,0:T(8,128)(2,1)}, bf16[512,768]{1,0:T(8,128)(2,1)})) %all-reduce.5.cloned.1.call-update) | async-done | bytes 2654224 | tf_op jit(solution)/shard_map/psum | solution.py:427
  552.8 2.4 convert_element_type.563
  (497 shorter events, 203.1 us)
Async XLA Ops:
  7.2 160.7 %copy-start = (bf16[512,768]{1,0:T(8,128)(2,1)S(1)}, bf16[512,768]{1,0:T(8,128)(2,1)}, u32[]{:S(2)}) copy-start(bf16[512,768]{1,0:T(8,128)(2,1)} %param.29) | copy-start | bytes 2359300
  7.2 21.1 %copy-start.42 = (bf16[768,1024]{1,0:T(8,128)(2,1)S(1)}, bf16[768,1024]{1,0:T(8,128)(2,1)}, u32[]{:S(2)}) copy-start(bf16[768,1024]{1,0:T(8,128)(2,1)} %param.32) | copy-start | bytes 4718596
  10.0 36.3 %collective-permute-start.2 = (bf16[1,18,192]{2,1,0:T(8,128)(2,1)}, bf16[1,18,192]{2,1,0:T(8,128)(2,1)}, u32[]{:S(2)}, u32[]{:S(2)}) collective-permute-start(bf16[1,18,192]{2,1,0:T(8,128)(2,1)} %get-tuple-element.76), channel_id=1, source_target_pairs={{0,2},{2,0},{1,3},{3,1},{4,6},{6,4},{5,7},{7,5},{8,10},{10,8},{9,1... | collective-permute-start | bytes 20744 | tf_op jit(solution)/shard_map/ppermute | solution.py:74
  12.9 63.3 %collective-permute-start = (bf16[256,768]{1,0:T(8,128)(2,1)}, bf16[256,768]{1,0:T(8,128)(2,1)}, u32[]{:S(2)}, u32[]{:S(2)}) collective-permute-start(bf16[256,768]{1,0:T(8,128)(2,1)} %param.17), channel_id=1, source_target_pairs={{0,2},{2,0},{1,3},{3,1},{4,6},{6,4},{5,7},{7,5},{8,10},{10,8},{9,1... | collective-permute-start | bytes 1179656 | tf_op jit(solution)/shard_map/ppermute | solution.py:74
  15.7 13.9 %copy-start.111 = (s32[2,16]{1,0:T(2,128)}, s32[2,16]{1,0:T(2,128)S(1)}, u32[]{:S(2)}) copy-start(s32[2,16]{1,0:T(2,128)S(1)} %get-tuple-element.73) | copy-start | bytes 388
  16.3 31.6 %all-to-all-start.3 = ((s32[32,2,16]{2,1,0:T(2,128)}), s32[32,2,16]{2,1,0:T(2,128)}, u32[]{:S(2)}, u32[]{:S(2)}) async-start(s32[32,2,16]{2,1,0:T(2,128)} %broadcast_in_dim.128), calls=%async_computation.3 | async-start | bytes 65536 | tf_op jit(solution)/shard_map/all_to_all | solution.py:94
  22.8 132.5 %collective-permute-start.10 = (bf16[768,1024]{1,0:T(8,128)(2,1)}, bf16[768,1024]{1,0:T(8,128)(2,1)}, u32[]{:S(2)}, u32[]{:S(2)}) collective-permute-start(bf16[768,1024]{1,0:T(8,128)(2,1)} %param.31), channel_id=1, source_target_pairs={{0,1},{1,0},{2,3},{3,2},{4,5},{5,4},{6,7},{7,6},{8,9},{9,8},{10,11... | collective-permute-start | bytes 4718600 | tf_op jit(solution)/shard_map/ppermute | solution.py:105
  23.1 133.8 %collective-permute-start.11 = (bf16[768,1024]{1,0:T(8,128)(2,1)}, bf16[768,1024]{1,0:T(8,128)(2,1)}, u32[]{:S(2)}, u32[]{:S(2)}) collective-permute-start(bf16[768,1024]{1,0:T(8,128)(2,1)} %param.32), channel_id=1, source_target_pairs={{0,1},{1,0},{2,3},{3,2},{4,5},{5,4},{6,7},{7,6},{8,9},{9,8},{10,11... | collective-permute-start | bytes 4718600 | tf_op jit(solution)/shard_map/ppermute | solution.py:106
  23.4 56.7 %collective-permute-start.13 = (bf16[256,768]{1,0:T(8,128)(2,1)}, bf16[256,768]{1,0:T(8,128)(2,1)}, u32[]{:S(2)}, u32[]{:S(2)}) collective-permute-start(bf16[256,768]{1,0:T(8,128)(2,1)} %param.18), channel_id=1, source_target_pairs={{0,2},{2,0},{1,3},{3,1},{4,6},{6,4},{5,7},{7,5},{8,10},{10,8},{9,1... | collective-permute-start | bytes 1179656 | tf_op jit(solution)/shard_map/ppermute | solution.py:74
  47.1 11.4 %collective-permute-start.3 = (bf16[2,1,18,192]{3,2,1,0:T(8,128)(2,1)S(1)}, bf16[2,1,18,192]{3,2,1,0:T(8,128)(2,1)S(1)}, u32[]{:S(2)}, u32[]{:S(2)}) collective-permute-start(bf16[2,1,18,192]{3,2,1,0:T(8,128)(2,1)S(1)} %maximum_select_fusion.15), channel_id=1, source_target_pairs={{0,1},{1,0},{2,3},{3,2},{4,5},{5,4},{6,7},{7,6},{8,9},{9,8},{10,11... | collective-permute-start | bytes 41480 | tf_op jit(solution)/shard_map/ppermute | solution.py:76
  48.0 36.6 %all-to-all-start = ((bf16[4,3,192,192]{2,3,1,0:T(8,128)(2,1)}), bf16[4,3,192,192]{2,3,1,0:T(8,128)(2,1)}, u32[]{:S(2)}, u32[]{:S(2)}) async-start(bf16[4,3,192,192]{2,3,1,0:T(8,128)(2,1)} %maximum_bitcast_fusion.2), calls=%async_computation | async-start | bytes 2359296 | tf_op jit(solution)/shard_map/all_to_all | solution.py:94
  56.9 19.4 %copy-start.15 = (bf16[256,768]{1,0:T(8,128)(2,1)S(1)}, bf16[256,768]{1,0:T(8,128)(2,1)}, u32[]{:S(2)}) copy-start(bf16[256,768]{1,0:T(8,128)(2,1)} %param.17) | copy-start | bytes 1179652
  58.5 15.9 %collective-permute-start.4 = (bf16[192,768]{1,0:T(8,128)(2,1)S(1)}, bf16[192,768]{1,0:T(8,128)(2,1)S(1)}, u32[]{:S(2)}, u32[]{:S(2)}) collective-permute-start(bf16[192,768]{1,0:T(8,128)(2,1)S(1)} %copy-done.57), channel_id=1, source_target_pairs={{0,2},{2,0},{1,3},{3,1},{4,6},{6,4},{5,7},{7,5},{8,10},{10,8},{9,1... | collective-permute-start | bytes 884744 | tf_op jit(solution)/shard_map/ppermute | solution.py:74
  60.7 58.8 %copy-start.92 = (f32[768]{0:T(1024)}, f32[768]{0:T(1024)S(1)}, u32[]{:S(2)}) copy-start(f32[768]{0:T(1024)S(1)} %reshape.1256) | copy-start | bytes 9220
  75.3 27.0 %collective-permute-start.5 = (bf16[2,192,768]{2,1,0:T(8,128)(2,1)}, bf16[2,192,768]{2,1,0:T(8,128)(2,1)}, u32[]{:S(2)}, u32[]{:S(2)}) collective-permute-start(bf16[2,192,768]{2,1,0:T(8,128)(2,1)} %maximum_select_fusion.12), channel_id=1, source_target_pairs={{0,1},{1,0},{2,3},{3,2},{4,5},{5,4},{6,7},{7,6},{8,9},{9,8},{10,11... | collective-permute-start | bytes 1769480 | tf_op jit(solution)/shard_map/ppermute | solution.py:76
  78.3 27.3 %collective-permute-start.1 = (bf16[2,256,768]{2,1,0:T(8,128)(2,1)}, bf16[2,256,768]{2,1,0:T(8,128)(2,1)S(1)}, u32[]{:S(2)}, u32[]{:S(2)}) collective-permute-start(bf16[2,256,768]{2,1,0:T(8,128)(2,1)} %maximum_select_fusion.5), channel_id=1, source_target_pairs={{0,1},{1,0},{2,3},{3,2},{4,5},{5,4},{6,7},{7,6},{8,9},{9,8},{10,11... | collective-permute-start | bytes 2359304 | tf_op jit(solution)/shard_map/ppermute | solution.py:76
  80.1 79.5 %collective-permute-start.12 = (bf16[1024,768]{1,0:T(8,128)(2,1)}, bf16[1024,768]{1,0:T(8,128)(2,1)}, u32[]{:S(2)}, u32[]{:S(2)}) collective-permute-start(bf16[1024,768]{1,0:T(8,128)(2,1)} %param.33), channel_id=1, source_target_pairs={{0,1},{1,0},{2,3},{3,2},{4,5},{5,4},{6,7},{7,6},{8,9},{9,8},{10,11... | collective-permute-start | bytes 4718600 | tf_op jit(solution)/shard_map/ppermute | solution.py:107
  84.6 35.3 %all-to-all-start.2 = ((bf16[4,2,192,512]{3,2,1,0:T(8,128)(2,1)}), bf16[4,2,192,512]{3,2,1,0:T(8,128)(2,1)}, u32[]{:S(2)}, u32[]{:S(2)}) async-start(bf16[4,2,192,512]{3,2,1,0:T(8,128)(2,1)} %copy.261), calls=%async_computation.2 | async-start | bytes 3145728 | tf_op jit(solution)/shard_map/all_to_all | solution.py:94
  94.0 12.9 %copy-start.27 = (bf16[768,192]{0,1:T(8,128)(2,1)}, bf16[768,192]{0,1:T(8,128)(2,1)S(1)}, u32[]{:S(2)}) copy-start(bf16[768,192]{0,1:T(8,128)(2,1)S(1)} %squeeze.119) | copy-start | bytes 884740
  102.3 21.7 %collective-permute-start.14 = (bf16[2,256,768]{2,1,0:T(8,128)(2,1)}, bf16[2,256,768]{2,1,0:T(8,128)(2,1)}, u32[]{:S(2)}, u32[]{:S(2)}) collective-permute-start(bf16[2,256,768]{2,1,0:T(8,128)(2,1)} %maximum_select_fusion.8), channel_id=1, source_target_pairs={{0,1},{1,0},{2,3},{3,2},{4,5},{5,4},{6,7},{7,6},{8,9},{9,8},{10,11... | collective-permute-start | bytes 2359304 | tf_op jit(solution)/shard_map/ppermute | solution.py:76
  119.9 11.9 %all-to-all-start.1 = ((bf16[4,256,192]{1,2,0:T(8,128)(2,1)}), bf16[4,256,192]{1,2,0:T(8,128)(2,1)}, u32[]{:S(2)}, u32[]{:S(2)}) async-start(bf16[4,256,192]{1,2,0:T(8,128)(2,1)} %bitcast.439), calls=%async_computation.1 | async-start | bytes 786432 | tf_op jit(solution)/shard_map/all_to_all | solution.py:94
  138.6 14.6 %collective-permute-start.6 = (bf16[256,768]{1,0:T(8,128)(2,1)}, bf16[256,768]{1,0:T(8,128)(2,1)}, u32[]{:S(2)}, u32[]{:S(2)}) collective-permute-start(bf16[256,768]{1,0:T(8,128)(2,1)} %multiply_convert_fusion.12), channel_id=1, source_target_pairs={{0,2},{2,0},{1,3},{3,1},{4,6},{6,4},{5,7},{7,5},{8,10},{10,8},{9,1... | collective-permute-start | bytes 1179656 | tf_op jit(solution)/shard_map/ppermute | solution.py:74
  140.5 36.4 %all-to-all-start.4 = ((bf16[16,48,768]{2,1,0:T(8,128)(2,1)}), bf16[16,48,768]{2,1,0:T(8,128)(2,1)S(1)}, u32[]{:S(2)}, u32[]{:S(2)}) async-start(bf16[16,48,768]{2,1,0:T(8,128)(2,1)} %bitcast.514), calls=%async_computation.4 | async-start | bytes 2359296 | tf_op jit(solution)/shard_map/all_to_all | solution.py:94
  154.6 9.5 %collective-permute-start.7 = (bf16[2,256,768]{2,1,0:T(8,128)(2,1)S(1)}, bf16[2,256,768]{2,1,0:T(8,128)(2,1)S(1)}, u32[]{:S(2)}, u32[]{:S(2)}) collective-permute-start(bf16[2,256,768]{2,1,0:T(8,128)(2,1)S(1)} %maximum_select_fusion.7), channel_id=1, source_target_pairs={{0,1},{1,0},{2,3},{3,2},{4,5},{5,4},{6,7},{7,6},{8,9},{9,8},{10,11... | collective-permute-start | bytes 2359304 | tf_op jit(solution)/shard_map/ppermute | solution.py:76
  173.4 123.0 %collective-permute-start.15 = (bf16[2,256,768]{2,1,0:T(8,128)(2,1)}, bf16[2,256,768]{2,1,0:T(8,128)(2,1)}, u32[]{:S(2)}, u32[]{:S(2)}) collective-permute-start(bf16[2,256,768]{2,1,0:T(8,128)(2,1)} %fusion.66), channel_id=1, source_target_pairs={{0,1},{1,0},{2,3},{3,2},{4,5},{5,4},{6,7},{7,6},{8,9},{9,8},{10,11... | collective-permute-start | bytes 2359304 | tf_op jit(solution)/shard_map/ppermute | solution.py:87
  176.9 34.5 %all-to-all-start.6 = ((bf16[16,48,768]{2,1,0:T(8,128)(2,1)}), bf16[16,48,768]{2,1,0:T(8,128)(2,1)}, u32[]{:S(2)}, u32[]{:S(2)}) async-start(bf16[16,48,768]{2,1,0:T(8,128)(2,1)} %bitcast.513), calls=%async_computation.6 | async-start | bytes 2359296 | tf_op jit(solution)/shard_map/all_to_all | solution.py:94
  185.6 115.6 %collective-permute-start.8 = (bf16[2,256,768]{2,1,0:T(8,128)(2,1)S(1)}, bf16[2,256,768]{2,1,0:T(8,128)(2,1)}, u32[]{:S(2)}, u32[]{:S(2)}) collective-permute-start(bf16[2,256,768]{2,1,0:T(8,128)(2,1)S(1)} %fusion.67), channel_id=1, source_target_pairs={{0,1},{1,0},{2,3},{3,2},{4,5},{5,4},{6,7},{7,6},{8,9},{9,8},{10,11... | collective-permute-start | bytes 2359304 | tf_op jit(solution)/shard_map/ppermute | solution.py:87
  225.9 14.1 %all-to-all-start.7 = ((f32[16,1,48]{2,1,0:T(1,128)}), f32[16,1,48]{2,1,0:T(1,128)}, u32[]{:S(2)}, u32[]{:S(2)}) async-start(f32[16,1,48]{2,1,0:T(1,128)} %all_to_all.52), calls=%async_computation.7 | async-start | bytes 16384 | tf_op jit(solution)/shard_map/all_to_all | solution.py:94
  247.1 11.1 %all-to-all-start.8 = ((f32[16,1,48]{2,1,0:T(1,128)}), f32[16,1,48]{2,1,0:T(1,128)}, u32[]{:S(2)}, u32[]{:S(2)}) async-start(f32[16,1,48]{2,1,0:T(1,128)} %all_to_all.54), calls=%async_computation.8 | async-start | bytes 16384 | tf_op jit(solution)/shard_map/all_to_all | solution.py:94
  258.3 31.8 %all-to-all-start.5 = ((bf16[16,48,768]{2,1,0:T(8,128)(2,1)}), bf16[16,48,768]{2,1,0:T(8,128)(2,1)}, u32[]{:S(2)}, u32[]{:S(2)}) async-start(bf16[16,48,768]{2,1,0:T(8,128)(2,1)} %bitcast.516), calls=%async_computation.5 | async-start | bytes 2359296 | tf_op jit(solution)/shard_map/all_to_all | solution.py:94
  290.0 32.0 %all-to-all-start.9 = ((bf16[16,48,768]{2,1,0:T(8,128)(2,1)}), bf16[16,48,768]{2,1,0:T(8,128)(2,1)}, u32[]{:S(2)}, u32[]{:S(2)}) async-start(bf16[16,48,768]{2,1,0:T(8,128)(2,1)} %bitcast.515), calls=%async_computation.9 | async-start | bytes 2359296 | tf_op jit(solution)/shard_map/all_to_all | solution.py:94
  299.2 29.5 %collective-permute-start.16 = (bf16[256,768]{1,0:T(8,128)(2,1)}, bf16[256,768]{1,0:T(8,128)(2,1)}, u32[]{:S(2)}, u32[]{:S(2)}) collective-permute-start(bf16[256,768]{1,0:T(8,128)(2,1)} %fusion.80), channel_id=1, source_target_pairs={{0,2},{2,0},{1,3},{3,1},{4,6},{6,4},{5,7},{7,5},{8,10},{10,8},{9,1... | collective-permute-start | bytes 1179656 | tf_op jit(solution)/shard_map/ppermute | solution.py:90
  303.4 27.4 %collective-permute-start.9 = (bf16[256,768]{1,0:T(8,128)(2,1)}, bf16[256,768]{1,0:T(8,128)(2,1)}, u32[]{:S(2)}, u32[]{:S(2)}) collective-permute-start(bf16[256,768]{1,0:T(8,128)(2,1)} %fusion.79), channel_id=1, source_target_pairs={{0,2},{2,0},{1,3},{3,1},{4,6},{6,4},{5,7},{7,5},{8,10},{10,8},{9,1... | collective-permute-start | bytes 1179656 | tf_op jit(solution)/shard_map/ppermute | solution.py:90
  310.5 18.2 %copy-start.99 = (f32[256]{0:T(256)S(1)}, f32[256]{0:T(256)}, u32[]{:S(2)}) copy-start(f32[256]{0:T(256)} %copy-done.98) | copy-start | bytes 3076
  322.0 47.6 %all-to-all-start.12 = ((bf16[4,2,192,512]{3,2,1,0:T(8,128)(2,1)}), bf16[4,2,192,512]{3,2,1,0:T(8,128)(2,1)}, u32[]{:S(2)}, u32[]{:S(2)}) async-start(bf16[4,2,192,512]{3,2,1,0:T(8,128)(2,1)} %copy.278), calls=%async_computation.12 | async-start | bytes 3145728 | tf_op jit(solution)/shard_map/all_to_all | solution.py:94
  333.4 21.4 %collective-permute-start.17 = (bf16[256,768]{1,0:T(8,128)(2,1)S(1)}, bf16[256,768]{1,0:T(8,128)(2,1)S(1)}, u32[]{:S(2)}, u32[]{:S(2)}) collective-permute-start(bf16[256,768]{1,0:T(8,128)(2,1)S(1)} %get-tuple-element.28), channel_id=1, source_target_pairs={{0,2},{2,0},{1,3},{3,1},{4,6},{6,4},{5,7},{7,5},{8,10},{10,8},{9,1... | collective-permute-start | bytes 1179656 | tf_op jit(solution)/shard_map/ppermute | solution.py:74
  335.4 19.6 %copy-start.12 = (bf16[768,2048]{1,0:T(8,128)(2,1)S(1)}, bf16[768,2048]{1,0:T(8,128)(2,1)}, u32[]{:S(2)}) copy-start(bf16[768,2048]{1,0:T(8,128)(2,1)} %copy-done.11) | copy-start | bytes 9437188
  338.1 19.6 %copy-start.9 = (f32[768,2048]{1,0:T(8,128)}, f32[768,2048]{1,0:T(8,128)S(1)}, u32[]{:S(2)}) copy-start(f32[768,2048]{1,0:T(8,128)S(1)} %fusion.125) | copy-start | bytes 18874372
  355.0 17.6 %collective-permute-start.18 = (bf16[2,256,768]{2,1,0:T(8,128)(2,1)S(1)}, bf16[2,256,768]{2,1,0:T(8,128)(2,1)}, u32[]{:S(2)}, u32[]{:S(2)}) collective-permute-start(bf16[2,256,768]{2,1,0:T(8,128)(2,1)S(1)} %maximum_select_fusion.10), channel_id=1, source_target_pairs={{0,1},{1,0},{2,3},{3,2},{4,5},{5,4},{6,7},{7,6},{8,9},{9,8},{10,11... | collective-permute-start | bytes 2359304 | tf_op jit(solution)/shard_map/ppermute | solution.py:76
  359.1 49.3 %collective-permute-start.21 = (bf16[768,1024]{1,0:T(8,128)(2,1)}, bf16[768,1024]{1,0:T(8,128)(2,1)}, u32[]{:S(2)}, u32[]{:S(2)}) collective-permute-start(bf16[768,1024]{1,0:T(8,128)(2,1)} %slice.381), channel_id=1, source_target_pairs={{0,1},{1,0},{2,3},{3,2},{4,5},{5,4},{6,7},{7,6},{8,9},{9,8},{10,11... | collective-permute-start | bytes 4718600 | tf_op jit(solution)/shard_map/ppermute | solution.py:131
  361.0 52.4 %collective-permute-start.22 = (bf16[768,1024]{1,0:T(8,128)(2,1)}, bf16[768,1024]{1,0:T(8,128)(2,1)}, u32[]{:S(2)}, u32[]{:S(2)}) collective-permute-start(bf16[768,1024]{1,0:T(8,128)(2,1)} %slice.380), channel_id=1, source_target_pairs={{0,1},{1,0},{2,3},{3,2},{4,5},{5,4},{6,7},{7,6},{8,9},{9,8},{10,11... | collective-permute-start | bytes 4718600 | tf_op jit(solution)/shard_map/ppermute | solution.py:131
  369.1 51.9 %collective-permute-start.23 = (bf16[1024,768]{1,0:T(8,128)(2,1)}, bf16[1024,768]{1,0:T(8,128)(2,1)}, u32[]{:S(2)}, u32[]{:S(2)}) collective-permute-start(bf16[1024,768]{1,0:T(8,128)(2,1)} %slice.379), channel_id=1, source_target_pairs={{0,1},{1,0},{2,3},{3,2},{4,5},{5,4},{6,7},{7,6},{8,9},{9,8},{10,11... | collective-permute-start | bytes 4718600 | tf_op jit(solution)/shard_map/ppermute | solution.py:131
  396.4 20.7 %collective-permute-start.19 = (bf16[2,256,768]{2,1,0:T(8,128)(2,1)}, bf16[2,256,768]{2,1,0:T(8,128)(2,1)}, u32[]{:S(2)}, u32[]{:S(2)}) collective-permute-start(bf16[2,256,768]{2,1,0:T(8,128)(2,1)} %fusion.68), channel_id=1, source_target_pairs={{0,1},{1,0},{2,3},{3,2},{4,5},{5,4},{6,7},{7,6},{8,9},{9,8},{10,11... | collective-permute-start | bytes 2359304 | tf_op jit(solution)/shard_map/ppermute | solution.py:87
  400.0 76.1 %all-to-all-start.10 = ((bf16[32,3,24,192]{3,2,1,0:T(8,128)(2,1)}), bf16[32,3,24,192]{3,2,1,0:T(8,128)(2,1)}, u32[]{:S(2)}, u32[]{:S(2)}) async-start(bf16[32,3,24,192]{3,2,1,0:T(8,128)(2,1)} %bitcast.146), calls=%async_computation.10 | async-start | bytes 2359296 | tf_op jit(solution)/shard_map/all_to_all | solution.py:94
  405.5 145.3 %all-reduce.5.cloned.1.call-start = ((), (), s32[]{:S(2)}) async-start(), calls=%async_computation.13 | async-start | bytes 5308416 | tf_op jit(solution)/shard_map/psum | solution.py:427
  408.4 12.6 %slice-start.2 = ((s8[6291456]{0:T(1024)(128)(4,1)}), s8[4194304]{0:T(1024)(128)(4,1)S(1)}, s32[]{:S(2)}) async-start(s8[6291456]{0:T(1024)(128)(4,1)} %bitcast.472), calls=%async_computation.16 | async-start | bytes 8388608
  419.4 65.5 %collective-permute-start.20 = (bf16[256,768]{1,0:T(8,128)(2,1)}, bf16[256,768]{1,0:T(8,128)(2,1)S(1)}, u32[]{:S(2)}, u32[]{:S(2)}) collective-permute-start(bf16[256,768]{1,0:T(8,128)(2,1)} %fusion.81), channel_id=1, source_target_pairs={{0,2},{2,0},{1,3},{3,1},{4,6},{6,4},{5,7},{7,5},{8,10},{10,8},{9,1... | collective-permute-start | bytes 1179656 | tf_op jit(solution)/shard_map/ppermute | solution.py:90
  478.8 78.4 %all-to-all-start.11 = ((bf16[8,3,24,768]{3,2,1,0:T(8,128)(2,1)}), bf16[8,3,24,768]{3,2,1,0:T(8,128)(2,1)}, u32[]{:S(2)}, u32[]{:S(2)}) async-start(bf16[8,3,24,768]{3,2,1,0:T(8,128)(2,1)} %broadcast_in_dim.253), calls=%async_computation.11 | async-start | bytes 1769472 | tf_op jit(solution)/shard_map/all_to_all | solution.py:94
  (110 other events, 390.8 us)
Sparse Core Ops, SparseCore 0:
  411.5 139.3 all-reduce.4

commit v2 on v1

v2 whole, which is shorter than its diff:
```python
import jax
import jax.numpy as jnp
import numpy as np
from jax import lax
from jax.experimental import pallas as pl
from jax.experimental.pallas import tpu as pltpu
from jax.sharding import Mesh
from jax.sharding import PartitionSpec as P

HEADS = 12
EXPERTS = 16
MOST = 48
EXTRA = 2 * EXPERTS

EPS = 1e-06
NEG = -1e30
LOW = jnp.bfloat16
WIDE = jnp.float32
ALL = ("ep", "fx", "fc")
SEQ = ("fx", "fc")
SWAP = [(0, 1), (1, 0)]
VMEM = pl.BlockSpec(memory_space=pltpu.VMEM)
SMEM = pl.BlockSpec(memory_space=pltpu.SMEM)


def matmul(left_op, right_op):
    return jnp.dot(left_op, right_op, preferred_element_type=WIDE)


def contract_rows(left_op, right_op):
    return lax.dot_general(left_op, right_op, (((0,), (0,)), ((), ())), preferred_element_type=WIDE)


def contract_cols(left_op, right_op):
    return lax.dot_general(left_op, right_op, (((1,), (1,)), ((), ())), preferred_element_type=WIDE)


def inverse_rms(values):
    return lax.rsqrt(jnp.mean(values * values, -1, keepdims=True) + EPS)


def rms_backward(upstream, values, inverse, gain_vec):
    scaled = upstream * gain_vec
    return inverse * scaled - values * inverse**3 * jnp.mean(scaled * values, -1, keepdims=True)


def silu_grad(gate_val):
    sigma = jax.nn.sigmoid(gate_val)
    return (gate_val * sigma, sigma * (1.0 + gate_val * (1.0 - sigma)))


def far_of(block):
    return lax.ppermute(block, "fx", SWAP)


def near_of(block):
    return lax.ppermute(block, "fc", SWAP)


def after(value, *others):
    return lax.optimization_barrier((value, *others))[0]


def exchange(blocks, axes):
    return lax.all_to_all(blocks, axes, split_axis=0, concat_axis=0, tiled=True)


def halve(parts):
    index = lax.axis_index("ep")
    count = parts.shape[0]
    size = count
    while size > 1:
        bit = count // size
        cut = parts.reshape((size // 2, 2) + parts.shape[1:])
        mine = lax.rem(index // bit, 2)
        give = lax.dynamic_index_in_dim(cut, 1 - mine, 1, keepdims=False)
        keep = lax.dynamic_index_in_dim(cut, mine, 1, keepdims=False)
        got = lax.ppermute(give, "ep", [(i, i ^ bit) for i in range(count)])
        parts = (keep.astype(WIDE) + got.astype(WIDE)).astype(LOW)
        size //= 2
    return parts[0]


def shape_of(dims, kind):
    return jax.ShapeDtypeStruct(dims, kind)


def run_kernel(body, outs, args, specs=None, out_specs=None, scratch=(), grid=None, flops=0, move=0):
    options = {} if grid is None else {"grid": grid}
    return pl.pallas_call(
        body,
        out_shape=outs,
        in_specs=specs if specs is not None else [VMEM] * len(args),
        out_specs=out_specs if out_specs is not None else [VMEM] * len(outs),
        scratch_shapes=list(scratch),
        compiler_params=pltpu.CompilerParams(vmem_limit_bytes=52 * 2**20),
        cost_estimate=pl.CostEstimate(flops=flops, bytes_accessed=move, transcendentals=0),
        **options,
    )(*args)


def pick_rows(first_iota, second_iota, source):
    return (first_iota == source(second_iota)).astype(LOW)


def rope_constants(length, half):
    freq = np.exp(-np.log(np.float32(10000.0)) * np.arange(half, dtype=np.float32) / np.float32(half))
    angle = np.arange(length, dtype=np.float32)[:, None] * freq.astype(np.float32)[None, :]
    cosine, sine = (np.cos(angle), np.sin(angle))
    return (
        np.concatenate([cosine, cosine, sine, sine], 1).astype(np.float32),
        np.concatenate([cosine] * 4, 1).astype(np.float32),
        np.concatenate([sine, -sine, sine, -sine], 1).astype(np.float32),
    )


def attention_forward(ids, x_parts, w_parts, table):
    full, width = x_parts[0].shape
    rows = full - EXTRA
    block = w_parts[0].shape[1]
    length = 4 * rows
    heads = block // 64
    size = heads * 128

    def body(ids_ref, *refs):
        x_refs, w_refs, table_ref = (refs[:4], refs[4:8], refs[8])
        ain_ref, own_ref, q_ref, k_ref, v_ref, lse_ref = refs[9:15]
        att_refs, small_ref = (refs[15:19], refs[19])
        att_scr = refs[20]
        first = lax.broadcasted_iota(jnp.int32, (block, width), 0)
        lane = lax.broadcasted_iota(jnp.int32, (block, width), 1)
        small = jnp.zeros((EXTRA, width), WIDE)
        for k in range(4):
            place = jnp.where(lane == first + ids_ref[1 + k] * block, 1.0, 0.0).astype(LOW)
            small = small + matmul(x_refs[k][rows:, :block], place)
        small_ref[...] = small.astype(LOW)
        gain = small[EXPERTS : EXPERTS + 1, :]
        for k in range(4):
            place = ids_ref[1 + k]
            piece = x_refs[k][:rows, :].astype(WIDE)
            ain_ref[pl.ds(place * rows, rows), :] = (piece * inverse_rms(piece) * gain).astype(LOW)
            for m in range(3):
                own_ref[m, pl.ds(place * block, block), :] = w_refs[k][m]
        first = lax.broadcasted_iota(jnp.int32, (block, size), 0)
        lane = lax.broadcasted_iota(jnp.int32, (block, size), 1)
        head, inner = (lane // 128, lane % 128)
        low = inner % 64
        swapped = jnp.where(low < 32, low + 32, low - 32)
        source = 64 * head + jnp.where(inner < 64, low, swapped)
        sign = jnp.where((inner >= 64) & (low < 32), -1.0, 1.0)
        turn = jnp.where(first == source, sign, 0.0).astype(LOW)
        keep = (inner // 64 == head % 2) & (first == 64 * head + low)
        place_v = jnp.where(keep, 1.0, 0.0).astype(LOW)
        w_q = matmul(own_ref[0], turn).astype(LOW)
        w_k = matmul(own_ref[1], turn).astype(LOW)
        w_v = matmul(own_ref[2], place_v).astype(LOW)
        half = lax.broadcasted_iota(jnp.int32, (rows, 128), 1) < 64
        for i in range(4):
            span = slice(i * rows, (i + 1) * rows)
            ain = ain_ref[span, :]
            y_q, y_k, y_v = (matmul(ain, w_q), matmul(ain, w_k), matmul(ain, w_v))
            tab = table_ref[span, :]
            for h in range(heads):
                cols = slice(128 * h, 128 * h + 128)
                turned = y_q[:, cols] * tab
                turned = (turned + pltpu.roll(turned, 64, 1)).astype(LOW).astype(WIDE)
                q_ref[h, span, :] = jnp.where(half, turned * 0.125, 0.0).astype(LOW)
                turned = y_k[:, cols] * tab
                k_ref[h, span, :] = (turned + pltpu.roll(turned, 64, 1)).astype(LOW)
                v_ref[h, span, :] = y_v[:, cols].astype(LOW)
        tri = lax.broadcasted_iota(jnp.int32, (rows, rows), 0) >= lax.broadcasted_iota(
            jnp.int32, (rows, rows), 1
        )
        for i in range(4):
            span = slice(i * rows, (i + 1) * rows)
            done = slice(0, i * rows)
            tiles = []
            for h in range(heads):
                query = q_ref[h, span, :]
                diag = jnp.where(tri, contract_cols(query, k_ref[h, span, :]), NEG)
                top = jnp.max(diag, -1, keepdims=True)
                if i:
                    past = contract_cols(query, k_ref[h, done, :])
                    top = jnp.maximum(top, jnp.max(past, -1, keepdims=True))
                diag = jnp.exp(diag - top)
                total = jnp.sum(diag, -1, keepdims=True)
                if i:
                    past = jnp.exp(past - top)
                    total = total + jnp.sum(past, -1, keepdims=True)
                scale = 1.0 / total
                out = matmul((diag * scale).astype(LOW), v_ref[h, span, :])
                if i:
                    out = out + matmul((past * scale).astype(LOW), v_ref[h, done, :])
                lse_ref[h, span, :] = top + jnp.log(total)
                tiles.append(out)
            for t in range((heads + 1) // 2):
                pair = tiles[2 * t] + (tiles[2 * t + 1] if 2 * t + 1 < heads else 0.0)
                wide = min(128, block - 128 * t)
                att_scr[span, 128 * t : 128 * t + wide] = pair[:, :wide].astype(LOW)
        for k in range(4):
            att_refs[k][...] = att_scr[pl.ds(ids_ref[1 + k] * rows, rows), :]

    outs = (
        [shape_of((length, width), LOW), shape_of((3, width, block), LOW)]
        + [shape_of((heads, length, 128), LOW)] * 3
        + [shape_of((heads, length, 1), WIDE)]
        + [shape_of((rows, block), LOW)] * 4
        + [shape_of((EXTRA, width), LOW)]
    )
    args = [ids, *x_parts, *w_parts, table]
    got = run_kernel(
        body,
        outs,
        args,
        specs=[SMEM] + [VMEM] * (len(args) - 1),
        scratch=[pltpu.VMEM((length, block), LOW)],
        flops=8 * 10**9,
        move=12 * 10**6,
    )
    return (got[0], got[1], got[2:5], got[5], got[6:10], got[10])


def after_attention(att_parts, out_parts, tokens, small, dispatch):
    rows, width = tokens.shape

    def body(*refs):
        att_refs, out_refs = (refs[:4], refs[4:8])
        tok_ref, small_ref, disp_ref, res_ref, ffn_ref, sent_ref = refs[8:]
        total = tok_ref[...].astype(WIDE)
        for k in range(4):
            total = total + matmul(att_refs[k][...], out_refs[k][...])
        res_ref[...] = total
        gain = small_ref[EXPERTS + 1 : EXPERTS + 2, :].astype(WIDE)
        ffn = (total * inverse_rms(total) * gain).astype(LOW)
        ffn_ref[...] = ffn
        sent_ref[...] = contract_rows(disp_ref[...], ffn).astype(LOW)

    slots = dispatch.shape[1]
    outs = [shape_of((rows, width), WIDE), shape_of((rows, width), LOW), shape_of((slots, width), LOW)]
    args = [*att_parts, *out_parts, tokens, small, dispatch]
    return run_kernel(body, outs, args, flops=6 * 10**8, move=4 * 10**6)


def shared_branch(ids, ffn_parts, dy_parts, w_parts, down, chunks):
    rows, width = ffn_parts[0].shape
    block, hidden = w_parts[0].shape[1:]

    def body(ids_ref, *refs):
        ffn_refs, dy_refs, w_refs = (refs[:4], refs[4:8], refs[8:12])
        down_ref = refs[12]
        mine_ref, near_ref, mid_ref = refs[13:16]
        grad_refs = refs[16:-3]
        w_scr, g_scr, d_scr = refs[-3:]
        for k in range(4):
            for m in range(2):
                w_scr[m, pl.ds(ids_ref[1 + k] * block, block), :] = w_refs[k][m]
        for k in range(4):
            ffn, dy = (ffn_refs[k][...], dy_refs[k][...])
            gate, up = (matmul(ffn, w_scr[0]), matmul(ffn, w_scr[1]))
            silu, slope = silu_grad(gate)
            hid = (silu * up).astype(LOW)
            back = contract_cols(dy, down_ref[...])
            d_gate = (back * up * slope).astype(LOW)
            d_up = (back * silu).astype(LOW)
            din = (contract_cols(d_gate, w_scr[0]) + contract_cols(d_up, w_scr[1])).astype(LOW)
            out = matmul(hid, down_ref[...]).astype(LOW)
            if k % 2 == 0:
                target = mine_ref if k == 0 else mid_ref
                target[0], target[1] = (din, out)
            else:
                near_ref[k // 2, 0], near_ref[k // 2, 1] = (din, out)
            parts = (contract_rows(ffn, d_gate), contract_rows(ffn, d_up), contract_rows(hid, dy))
            if k == 0:
                g_scr[0], g_scr[1], d_scr[...] = parts
            else:
                g_scr[0] += parts[0]
                g_scr[1] += parts[1]
                d_scr[...] += parts[2]
        if chunks:
            per = chunks // 2
            cut, line = (block // per, hidden // chunks)
            for r in range(chunks):
                part = ids_ref[6] ^ r
                target = grad_refs[r % 2]
                which, low = (part // per, part % per)
                for k in range(4):
                    start = ids_ref[1 + k] * block + low * cut
                    target[r // 2, k * cut : (k + 1) * cut, :] = g_scr[
                        which, pl.ds(pl.multiple_of(start, 16), cut), :
                    ].astype(LOW)
                start = pl.multiple_of(part * line, 16)
                piece = d_scr[pl.ds(start, line), :].astype(LOW)
                base = 4 * cut
                target[r // 2, base : base + line, :] = piece[:, :hidden]
                target[r // 2, base + line :, : hidden // 2] = piece[: line // 2, hidden:]
                target[r // 2, base + line :, hidden // 2 :] = piece[line // 2 :, hidden:]
        else:
            for k in range(4):
                for m in range(2):
                    grad_refs[k][m] = g_scr[m, pl.ds(ids_ref[1 + k] * block, block), :].astype(LOW)
            grad_refs[4][...] = d_scr[...].astype(LOW)

    if chunks:
        lines = 4 * block * 2 // chunks + 3 * hidden // chunks // 2
        grad_outs = [shape_of((chunks // 2, lines, hidden), LOW)] * 2
    else:
        grad_outs = [shape_of((2, block, hidden), LOW)] * 4 + [shape_of((hidden, width), LOW)]
    outs = [
        shape_of((2, rows, width), LOW),
        shape_of((2, 2, rows, width), LOW),
        shape_of((2, rows, width), LOW),
    ] + grad_outs
    args = [ids, *ffn_parts, *dy_parts, *w_parts, down]
    got = run_kernel(
        body,
        outs,
        args,
        specs=[SMEM] + [VMEM] * (len(args) - 1),
        scratch=[
            pltpu.VMEM((2, width, hidden), LOW),
            pltpu.VMEM((2, width, hidden), WIDE),
            pltpu.VMEM((hidden, width), WIDE),
        ],
        flops=7 * 10**9,
        move=14 * 10**6,
    )
    return (got[0:3], got[3:])


def place_shared(ids, groups, block, width):
    per_group, lines, hidden = groups[0].shape
    chunks = per_group * len(groups)
    per = chunks // 2
    cut, line = (block // per, hidden // chunks)
    order = (0, 4, 2, 6, 1, 5, 3, 7)

    def body(ids_ref, *refs):
        up_ref, down_ref = refs[-2:]
        for n in range(chunks):
            part = ids_ref[6] ^ order[n]
            which, low = (part // per, part % per)
            piece = refs[n // per_group][n % per_group].astype(WIDE)
            for k in range(4):
                lane = pl.multiple_of(ids_ref[1 + k] * hidden, 128)
                up_ref[which, pl.ds(low * cut, cut), pl.ds(lane, hidden)] = piece[
                    k * cut : (k + 1) * cut, :
                ]
            base = 4 * cut
            start = pl.multiple_of(part * line, 16)
            down_ref[pl.ds(start, line), :hidden] = piece[base : base + line, :]
            tail = piece[base + line :, :]
            down_ref[pl.ds(start, line // 2), hidden:] = tail[:, : hidden // 2]
            down_ref[pl.ds(start + line // 2, line // 2), hidden:] = tail[:, hidden // 2 :]

    return run_kernel(
        body,
        [shape_of((2, block, 4 * hidden), WIDE), shape_of((hidden, width), WIDE)],
        [ids, *groups],
        specs=[SMEM] + [VMEM] * len(groups),
        move=8 * 10**6,
    )


def expert_main(ids, rows_in, dy_in, mats, other, router_t):
    count, width = rows_in.shape
    own_hidden = mats[0].shape[1]
    tile = 512
    steps = 2 * own_hidden // tile
    half = steps // 2
    chunk = 256

    def body(ids_ref, rows_ref, dy_ref, *refs):
        own, peer = (refs[0:3], refs[3:6])
        other_ref, router_ref = refs[6:8]
        din_ref, hid_ref, dg_ref, du_ref, dyw_ref, w_ref, part_ref = refs[8:15]
        acc, dot_scr = refs[15:17]
        step = pl.program_id(0)
        expert = ids_ref[5]

        @pl.when(step == 0)
        def start():
            for r in range(0, count, chunk):
                span = slice(r, r + chunk)
                logits = contract_cols(rows_ref[span, :], router_ref[...])
                lane = lax.broadcasted_iota(jnp.int32, logits.shape, 1)
                mine = jnp.sum(jnp.where(lane == expert, logits, 0.0), -1, keepdims=True)
                rest = jnp.sum(jnp.where(lane == other_ref[span, :], logits, 0.0), -1, keepdims=True)
                weight = jax.nn.sigmoid(mine - rest)
                w_ref[span, :] = weight
                dyw_ref[span, :] = (weight * dy_ref[span, :].astype(WIDE)).astype(LOW)
                dot_scr[span, :] = jnp.zeros((chunk, 1), WIDE)
                acc[span, :] = jnp.zeros((chunk, width), WIDE)

        def work(gate_ref, up_ref, down_ref):
            for r in range(0, count, chunk):
                span = slice(r, r + chunk)
                rows = rows_ref[span, :]
                gate, up = (matmul(rows, gate_ref[...]), matmul(rows, up_ref[...]))
                back = contract_cols(dy_ref[span, :], down_ref[...])
                silu, slope = silu_grad(gate)
                hid = (silu * up).astype(LOW)
                hid_ref[span, :] = hid
                dot_scr[span, :] += jnp.sum(hid.astype(WIDE) * back, -1, keepdims=True)
                scaled = w_ref[span, :] * back
                d_gate = (scaled * up * slope).astype(LOW)
                d_up = (scaled * silu).astype(LOW)
                dg_ref[span, :] = d_gate
                du_ref[span, :] = d_up
                acc[span, :] += contract_cols(d_gate, gate_ref[...]) + contract_cols(
                    d_up, up_ref[...]
                )

        @pl.when(step < half)
        def first():
            work(*own)

        @pl.when(step >= half)
        def second():
            work(*peer)

        @pl.when(step == steps - 1)
        def finish():
            for r in range(0, count, chunk):
                span = slice(r, r + chunk)
                weight = w_ref[span, :]
                amount = weight * (1.0 - weight) * dot_scr[span, :]
                lane = lax.broadcasted_iota(jnp.int32, (chunk, EXTRA), 1)
                signs = jnp.where(lane == expert, 1.0, 0.0) - jnp.where(
                    lane == other_ref[span, :], 1.0, 0.0
                )
                d_logit = (amount * signs).astype(LOW)
                din_ref[span, :] = (acc[span, :] + matmul(d_logit, router_ref[...])).astype(LOW)
                part = contract_rows(d_logit, rows_ref[span, :])
                part_ref[...] = part if r == 0 else part_ref[...] + part

    def fixed(dims):
        return pl.BlockSpec(dims, lambda j: (0,) * len(dims))

    def near(j):
        return jnp.minimum(j, half - 1)

    def late(j):
        return jnp.maximum(j - half, 0)

    cols = (width, tile)
    specs = [SMEM, fixed((count, width)), fixed((count, width))]
    for place in (near, late):
        specs += [
            pl.BlockSpec(cols, lambda j, place=place: (0, place(j))),
            pl.BlockSpec(cols, lambda j, place=place: (0, place(j))),
            pl.BlockSpec((tile, width), lambda j, place=place: (place(j), 0)),
        ]
    specs += [fixed((count, 1)), fixed(router_t.shape)]
    tiles = pl.BlockSpec((count, tile), lambda j: (0, j))
    outs = (
        [shape_of((count, width), LOW)]
        + [shape_of((count, 2 * own_hidden), LOW)] * 3
        + [shape_of((count, width), LOW), shape_of((count, 1), WIDE), shape_of(router_t.shape, WIDE)]
    )
    out_specs = [
        fixed((count, width)),
        tiles,
        tiles,
        tiles,
        fixed((count, width)),
        fixed((count, 1)),
        fixed(router_t.shape),
    ]
    return run_kernel(
        body,
        outs,
        [ids, rows_in, dy_in, *mats, other, router_t],
        specs=specs,
        out_specs=out_specs,
        scratch=[pltpu.VMEM((count, width), WIDE), pltpu.VMEM((count, 1), WIDE)],
        grid=(steps,),
        flops=12 * 10**9,
        move=22 * 10**6,
    )


def expert_out(hid, weight, down_own, down_peer):
    count, hidden = hid.shape
    width = down_own.shape[1]
    half = hidden // 2
    chunk = 256

    def body(hid_ref, w_ref, own_ref, peer_ref, out_ref):
        for r in range(0, count, chunk):
            span = slice(r, r + chunk)
            total = matmul(hid_ref[span, :half], own_ref[...])
            total = total + matmul(hid_ref[span, half:], peer_ref[...])
            out_ref[span, :] = (w_ref[span, :] * total).astype(LOW)

    return run_kernel(
        body,
        [shape_of((count, width), LOW)],
        [hid, weight, down_own, down_peer],
        flops=2 * 10**9,
        move=8 * 10**6,
    )[0]


def expert_weight_grads(rows_in, dyw, hid, d_gate, d_up, peer, add=None):
    count, width = rows_in.shape
    half = hid.shape[1] // 2
    tile = 512
    steps = half // tile
    offset = steps if peer else 0
    kind = LOW if add is None else WIDE

    def body(rows_ref, dyw_ref, hid_ref, dg_ref, du_ref, *refs):
        outs = refs[-3:]
        grads = (
            contract_rows(rows_ref[...], dg_ref[...]),
            contract_rows(rows_ref[...], du_ref[...]),
            contract_rows(hid_ref[...], dyw_ref[...]),
        )
        for i in range(3):
            value = grads[i] if add is None else grads[i] + refs[i][...].astype(WIDE)
            outs[i][...] = value.astype(kind)

    def fixed(dims):
        return pl.BlockSpec(dims, lambda j: (0,) * len(dims))

    tiles = pl.BlockSpec((count, tile), lambda j: (0, j + offset))
    cols = pl.BlockSpec((width, tile), lambda j: (0, j))
    lines = pl.BlockSpec((tile, width), lambda j: (j, 0))
    specs = [fixed((count, width)), fixed((count, width)), tiles, tiles, tiles]
    extra = [] if add is None else list(add)
    return run_kernel(
        body,
        [shape_of((width, half), kind), shape_of((width, half), kind), shape_of((half, width), kind)],
        [rows_in, dyw, hid, d_gate, d_up, *extra],
        specs=specs + ([] if add is None else [cols, cols, lines]),
        out_specs=[cols, cols, lines],
        grid=(steps,),
        flops=37 * 10**8,
        move=14 * 10**6,
    )


def back_at_tokens(fold, back_din, dispatch, residual, small, cotangent, router_part):
    rows, width = residual.shape

    def body(one_ref, two_ref, last_ref, back_ref, disp_ref, res_ref, small_ref, dy_ref, part_ref, dres_ref, br_ref):
        d_ffn = one_ref[0].astype(WIDE) + two_ref[0, 0].astype(WIDE) + last_ref[0].astype(WIDE)
        d_ffn = d_ffn + matmul(disp_ref[...], back_ref[...])
        residual_val = res_ref[...]
        inverse = inverse_rms(residual_val)
        gain = small_ref[EXPERTS + 1 : EXPERTS + 2, :].astype(WIDE)
        d_res = dy_ref[...].astype(WIDE) + rms_backward(d_ffn, residual_val, inverse, gain)
        dres_ref[...] = d_res
        br_ref[0:rows, :] = d_res.astype(LOW)
        gain_part = jnp.sum(d_ffn * residual_val * inverse, 0, keepdims=True)
        line = lax.broadcasted_iota(jnp.int32, (EXTRA, width), 0)
        extra = jnp.where(line == EXPERTS, gain_part, part_ref[...])
        br_ref[rows:, :] = extra.astype(LOW)

    return run_kernel(
        body,
        [shape_of((rows, width), WIDE), shape_of((rows + EXTRA, width), LOW)],
        [*fold, back_din, dispatch, residual, small, cotangent, router_part],
        flops=3 * 10**8,
        move=5 * 10**6,
    )


def finish_output(residual, fold, back_out, dispatch):
    rows, width = residual.shape

    def body(res_ref, one_ref, two_ref, last_ref, back_ref, disp_ref, out_ref):
        total = res_ref[...] + one_ref[1].astype(WIDE) + two_ref[0, 1].astype(WIDE)
        total = total + last_ref[1].astype(WIDE)
        out_ref[...] = (total + matmul(disp_ref[...], back_ref[...])).astype(LOW)

    return run_kernel(
        body,
        [shape_of((rows, width), LOW)],
        [residual, *fold, back_out, dispatch],
        flops=3 * 10**8,
        move=4 * 10**6,
    )[0]


def attention_backward(ids, branch, w_out, queries, keys, values, lse, ain, tables):
    heads, length, _ = queries.shape
    rows = length // 4
    block, width = w_out.shape
    tiles = (heads + 1) // 2

    def body(ids_ref, *refs):
        br_refs = refs[:4]
        wo_ref, q_ref, k_ref, v_ref, lse_ref, ain_ref, cc_ref, ss_ref = refs[4:12]
        d_ref, g_ref = refs[12:14]
        da_scr, dk_scr, dv_scr = refs[14:17]
        zero = jnp.zeros((rows, 128), WIDE)
        for k in range(4):
            d_att = contract_cols(br_refs[k][0:rows, :], wo_ref[...]).astype(LOW)
            place = ids_ref[1 + k] * rows
            for t in range(tiles):
                wide = min(128, block - 128 * t)
                if wide < 128:
                    da_scr[t, pl.ds(place, rows), :] = zero.astype(LOW)
                da_scr[t, pl.ds(place, rows), 0:wide] = d_att[:, 128 * t : 128 * t + wide]
        half = lax.broadcasted_iota(jnp.int32, (rows, 128), 1) < 64
        tri = lax.broadcasted_iota(jnp.int32, (rows, rows), 0) >= lax.broadcasted_iota(
            jnp.int32, (rows, rows), 1
        )

        def place_tile(m, span, h, value):
            t = h // 2
            wide = min(128, block - 128 * t)
            if h % 2 == 0:
                d_ref[m, span, 128 * t : 128 * t + wide] = value[:, :wide].astype(LOW)
            else:
                kept = d_ref[m, span, 128 * t : 128 * t + 128].astype(WIDE)
                d_ref[m, span, 128 * t : 128 * t + 128] = jnp.where(half, kept, value).astype(LOW)

        def unturn(value, span):
            return value * cc_ref[span, :] + pltpu.roll(value, 32, 1) * ss_ref[span, :]

        for h in range(heads):
            for i in range(4):
                span = slice(i * rows, (i + 1) * rows)
                done = slice(0, i * rows)
                query = q_ref[h, span, :]
                d_att = da_scr[h // 2, span, :]
                level = lse_ref[h, span, :]
                diag = contract_cols(query, k_ref[h, span, :]) - level
                diag = jnp.exp(jnp.where(tri, diag, NEG))
                d_diag = contract_cols(d_att, v_ref[h, span, :])
                inner = jnp.sum(diag * d_diag, -1, keepdims=True)
                if i:
                    past = jnp.exp(contract_cols(query, k_ref[h, done, :]) - level)
                    d_past = contract_cols(d_att, v_ref[h, done, :])
                    inner = inner + jnp.sum(past * d_past, -1, keepdims=True)
                d_diag = (diag * (d_diag - inner)).astype(LOW)
                d_query = matmul(d_diag, k_ref[h, span, :])
                dk_scr[span, :] = contract_rows(d_diag, query)
                dv_scr[span, :] = contract_rows(diag.astype(LOW), d_att)
                if i:
                    d_past = (past * (d_past - inner)).astype(LOW)
                    d_query = d_query + matmul(d_past, k_ref[h, done, :])
                    dk_scr[done, :] += contract_rows(d_past, query)
                    dv_scr[done, :] += contract_rows(past.astype(LOW), d_att)
                place_tile(0, span, h, unturn(d_query * 0.125, span))
            for i in range(4):
                span = slice(i * rows, (i + 1) * rows)
                d_key = dk_scr[span, :]
                place_tile(1, span, h, unturn(d_key + pltpu.roll(d_key, 64, 1), span))
                place_tile(2, span, h, dv_scr[span, :])
        for m in range(3):
            g_ref[m] = contract_rows(ain_ref[...], d_ref[m]).astype(LOW)

    args = [ids, *branch, w_out, queries, keys, values, lse, ain, *tables]
    return run_kernel(
        body,
        [shape_of((3, length, block), LOW), shape_of((3, width, block), LOW)],
        args,
        specs=[SMEM] + [VMEM] * (len(args) - 1),
        scratch=[
            pltpu.VMEM((tiles, length, 128), LOW),
            pltpu.VMEM((length, 128), WIDE),
            pltpu.VMEM((length, 128), WIDE),
        ],
        flops=16 * 10**9,
        move=12 * 10**6,
    )


def late_grads(ids, d_qkv, own_mats, att_parts, branch):
    length, block = d_qkv.shape[1:]
    rows = length // 4
    width = own_mats.shape[1]
    extra = branch[0].shape[0] - rows

    def body(ids_ref, d_ref, w_ref, *refs):
        att_refs, br_refs = (refs[:4], refs[4:8])
        mine_ref, near_ref, mid_ref, gout_ref = refs[8:12]
        for k in range(4):
            span = pl.ds(ids_ref[1 + k] * rows, rows)
            total = contract_cols(d_ref[0, span, :], w_ref[0])
            for m in range(1, 3):
                total = total + contract_cols(d_ref[m, span, :], w_ref[m])
            if k % 2 == 0:
                target = mine_ref if k == 0 else mid_ref
                target[...] = total.astype(LOW)
            else:
                near_ref[k // 2] = total.astype(LOW)
        gout = contract_rows(att_refs[0][...], br_refs[0][0:rows, :])
        small = br_refs[0][rows:, :].astype(WIDE)
        for k in range(1, 4):
            gout = gout + contract_rows(att_refs[k][...], br_refs[k][0:rows, :])
            small = small + br_refs[k][rows:, :].astype(WIDE)
        gout_ref[0:block, :] = gout.astype(LOW)
        gout_ref[block:, :] = small.astype(LOW)

    args = [ids, d_qkv, own_mats, *att_parts, *branch]
    got = run_kernel(
        body,
        [
            shape_of((rows, width), LOW),
            shape_of((2, rows, width), LOW),
            shape_of((rows, width), LOW),
            shape_of((block + extra, width), LOW),
        ],
        args,
        specs=[SMEM] + [VMEM] * (len(args) - 1),
        flops=12 * 10**8,
        move=7 * 10**6,
    )
    return (got[:3], got[3])


def experts_chip(ids, rows_sent, got_dy, other, small, weights, peers):
    width = rows_sent.shape[1]
    axes = ("ep", "fx")
    own_rows = exchange(rows_sent.reshape(EXPERTS, MOST, width), axes).reshape(-1, width)
    din, hid, d_gate, d_up, dyw, weight, part = expert_main(
        ids, own_rows, got_dy, [*weights, *peers], other, small
    )
    back_din = exchange(din.reshape(EXPERTS, MOST, width), axes).reshape(-1, width)

    def middle(start):
        out = expert_out(after(hid, start), weight, weights[2], peers[2])
        given = expert_weight_grads(after(own_rows, out), dyw, hid, d_gate, d_up, True)
        return (out, [near_of(piece) for piece in given])

    def outward(out):
        return exchange(out.reshape(EXPERTS, MOST, width), axes).reshape(-1, width)

    def finish(start, received):
        return expert_weight_grads(
            after(own_rows, start), dyw, hid, d_gate, d_up, False, received
        )

    return (back_din, part, din, middle, outward, finish)


def experts_spread(rows_sent, grads_sent, other, router_t, weights):
    ep_count = lax.axis_size("ep")
    weg, weu, wed = weights
    width = rows_sent.shape[1]
    local_count = max(1, EXPERTS // ep_count)
    replicas = max(1, ep_count // EXPERTS)
    groups = EXPERTS // local_count
    gate_cols, up_cols, down_rows = (
        lax.all_gather(weg, SEQ, axis=1, tiled=True),
        lax.all_gather(weu, SEQ, axis=1, tiled=True),
        lax.all_gather(wed, SEQ, axis=0, tiled=True),
    )
    hidden_part = gate_cols.shape[1] // local_count
    gate_local = gate_cols.reshape(width, local_count, hidden_part).transpose(1, 0, 2)
    up_local = up_cols.reshape(width, local_count, hidden_part).transpose(1, 0, 2)
    down_local = down_rows.reshape(local_count, hidden_part, width)

    def spread(buffer):
        last = buffer.shape[-1]
        wide = buffer.reshape(groups, 1, local_count * MOST, last)
        wide = jnp.broadcast_to(wide, (groups, replicas, local_count * MOST, last))
        return exchange(wide.reshape(ep_count, local_count * MOST, last), "ep")

    def collect(buffer):
        last = buffer.shape[-1]
        return jnp.sum(
            exchange(buffer, "ep").astype(WIDE).reshape(groups, replicas, local_count * MOST, last),
            1,
        ).reshape(EXPERTS * MOST, last)

    def owner_layout(received):
        last = received.shape[-1]
        return (
            received.reshape(ep_count, local_count, MOST, last)
            .transpose(1, 0, 2, 3)
            .reshape(local_count, ep_count * MOST, last)
        )

    def source_layout(owned):
        last = owned.shape[-1]
        return (
            owned.reshape(local_count, ep_count, MOST, last)
            .transpose(1, 0, 2, 3)
            .reshape(ep_count, local_count * MOST, last)
        )

    def batched(spec, left_op, right_op):
        return jnp.einsum(spec, left_op, right_op, preferred_element_type=WIDE)

    own_rows = owner_layout(spread(rows_sent))
    got_grads = owner_layout(spread(grads_sent))
    got_other = owner_layout(spread(other[:, None]))
    first = lax.axis_index("ep") // replicas * local_count
    mine = first + jnp.arange(local_count)[:, None, None]
    lane = jnp.arange(EXPERTS)
    logits = batched("lrd,ed->lre", own_rows, router_t)
    hit_mine, hit_other = ((lane == mine).astype(WIDE), (lane == got_other).astype(WIDE))
    got_weight = jax.nn.sigmoid(jnp.sum(logits * (hit_mine - hit_other), -1, keepdims=True))
    gate_val = batched("lrd,ldh->lrh", own_rows, gate_local)
    up_val = batched("lrd,ldh->lrh", own_rows, up_local)
    silu_val, slope_val = silu_grad(gate_val)
    hidden_val = (silu_val * up_val).astype(LOW)
    out_rows = batched("lrh,lhd->lrd", hidden_val, down_local)
    back_out = collect(source_layout((got_weight * out_rows).astype(LOW)))
    grad_hidden = batched("lrd,lhd->lrh", got_grads, down_local)
    row_dot = jnp.sum(hidden_val.astype(WIDE) * grad_hidden, -1, keepdims=True)
    amount = got_weight * (1.0 - got_weight) * row_dot
    d_logits = (amount * (hit_mine - hit_other)).astype(LOW)
    part = jnp.sum(batched("lre,lrd->led", d_logits, own_rows), 0)
    scaled = got_weight * grad_hidden
    own_grads = (got_weight * got_grads.astype(WIDE)).astype(LOW)
    grad_gate = (scaled * up_val * slope_val).astype(LOW)
    grad_up = (scaled * silu_val).astype(LOW)
    din_rows = batched("lrh,ldh->lrd", grad_gate, gate_local)
    din_rows = din_rows + batched("lrh,ldh->lrd", grad_up, up_local)
    din_rows = din_rows + batched("lre,ed->lrd", d_logits, router_t)
    back_din = collect(source_layout(din_rows.astype(LOW)))
    grad_gate_w = batched("lrd,lrh->ldh", own_rows, grad_gate)
    grad_up_w = batched("lrd,lrh->ldh", own_rows, grad_up)
    grad_down_w = batched("lrh,lrd->lhd", hidden_val, own_grads)

    def share(full, axis):
        return lax.psum_scatter(
            full.astype(LOW), SEQ, scatter_dimension=axis, tiled=True
        ).astype(WIDE)

    return (
        back_out.astype(LOW),
        back_din.astype(LOW),
        jnp.pad(part, ((0, EXTRA - EXPERTS), (0, 0))),
        lambda start: (
            share(grad_gate_w.transpose(1, 0, 2).reshape(width, local_count * hidden_part), 1),
            share(grad_up_w.transpose(1, 0, 2).reshape(width, local_count * hidden_part), 1),
            share(grad_down_w.reshape(local_count * hidden_part, width), 0),
        ),
    )


def shards(
    tokens,
    cotangent,
    routes,
    priority,
    gain_attn,
    w_query,
    w_key,
    w_value,
    w_out,
    gain_ffn,
    w_shared_gate,
    w_shared_up,
    w_shared_down,
    w_router,
    w_expert_gate,
    w_expert_up,
    w_expert_down,
):
    tok_rows, width = tokens.shape
    rows_w = w_query.shape[0]
    fs_count = lax.axis_size("fx") * lax.axis_size("fc")
    ep_count = lax.axis_size("ep")
    devices = ep_count * fs_count
    seq_len = tok_rows * fs_count
    head_size = width // HEADS
    side, core = (lax.axis_index("fx"), lax.axis_index("fc"))
    fs_index = side * lax.axis_size("fc") + core
    my_rank = lax.axis_index("ep") * fs_count + fs_index
    my_expert = lax.axis_index("ep") * lax.axis_size("fx") + side
    ids = [core] + [fs_index ^ k for k in range(4)] + [my_expert, lax.axis_index("ep")]
    ids = jnp.stack(ids).astype(jnp.int32)

    small_own = jnp.concatenate([w_router.T, gain_attn[None], gain_ffn[None]], 0)
    small_own = jnp.pad(small_own, ((0, EXTRA - EXPERTS - 2), (0, width - rows_w)))
    pack = jnp.concatenate([tokens, small_own])
    pack_far = far_of(pack)
    qkv_stack = jnp.stack([w_query, w_key, w_value])
    qkv_cut = [
        lax.dynamic_slice_in_dim(qkv_stack, (fs_index ^ k) * rows_w, rows_w, 2) for k in range(4)
    ]

    def to_place(parts):
        got = [
            lax.ppermute(parts[k], SEQ, [(i, i ^ k) for i in range(fs_count)]) for k in (2, 3, 1)
        ]
        return (parts[0], got[2], got[0], got[1])

    w_parts = to_place(qkv_cut)
    x_parts = (pack, near_of(pack), pack_far, near_of(pack_far))

    lane = jnp.arange(2 * EXPERTS)
    classes = jnp.stack([priority, 1 - priority], 1)
    named = routes + EXPERTS * classes
    hits = [(named[:, j : j + 1] == lane).astype(WIDE) for j in (0, 1)]
    both = hits[0] + hits[1]
    lower = (jnp.arange(tok_rows)[:, None] > jnp.arange(tok_rows)[None, :]).astype(LOW)
    before = matmul(lower, both.astype(LOW))
    counts = jnp.sum(both, 0)
    zero_row = jnp.zeros((EXPERTS,), WIDE)
    local_table = before + jnp.concatenate([zero_row, counts[:EXPERTS]])
    slot_iota = jnp.arange(EXPERTS * MOST)
    slot_hit = []
    for j in (0, 1):
        rank = jnp.sum(local_table * hits[j], -1).astype(jnp.int32)
        slot_hit.append(((routes[:, j] * MOST + rank)[:, None] == slot_iota).astype(LOW))
    dispatch = slot_hit[0] + slot_hit[1]
    others = jnp.stack([routes[:, 1], routes[:, 0]]).astype(LOW)
    other_sent = matmul(others[0:1], slot_hit[0]) + matmul(others[1:2], slot_hit[1])
    other_sent = other_sent.reshape(EXPERTS, MOST)
    pair_of_cores = EXPERTS == ep_count * lax.axis_size("fx")
    if pair_of_cores:
        tiny = jnp.concatenate(
            [jnp.broadcast_to(counts[None], (EXPERTS, 2 * EXPERTS)), other_sent], 1
        )
        tiny = jnp.pad(tiny, ((0, 0), (0, 128 - tiny.shape[1]))).astype(jnp.int32)
        tiny = jnp.broadcast_to(tiny[:, None], (EXPERTS, 2, 128)).reshape(devices, 1, 128)
        tiny_got = exchange(tiny, ALL)
        dy_sent = contract_rows(dispatch, cotangent).astype(LOW)
        dy_sent = after(dy_sent, tiny_got, pack_far, *w_parts[2:])
        got_dy = exchange(dy_sent.reshape(EXPERTS, MOST, width), ("ep", "fx"))
        got_dy = got_dy.reshape(-1, width)
        all_counts = tiny_got[:, 0, : 2 * EXPERTS].astype(WIDE)
        other = lax.dynamic_index_in_dim(tiny_got.reshape(EXPERTS, 2, 128), core, 1, keepdims=False)
        other = other[:, 2 * EXPERTS : 2 * EXPERTS + MOST].reshape(EXPERTS * MOST, 1)
    else:
        spread_counts = jnp.broadcast_to(counts.astype(jnp.int32), (devices, 2 * EXPERTS))
        all_counts = exchange(spread_counts, ALL).astype(WIDE)
    earlier = (jnp.arange(devices) < my_rank).astype(WIDE)
    base = jnp.sum(all_counts * earlier[:, None], 0)
    base = base + jnp.concatenate([zero_row, jnp.sum(all_counts[:, :EXPERTS], 0)])
    capacity = 5 * tok_rows * devices // 32
    kept = [(jnp.sum((before + base) * hits[j], -1) < capacity).astype(LOW) for j in (0, 1)]
    dispatch_kept = slot_hit[0] * kept[0][:, None] + slot_hit[1] * kept[1][:, None]

    forward_table, cos_table, sin_table = rope_constants(seq_len, head_size // 2)
    ain, own_mats, (queries, keys, values), lse, att_own, small = attention_forward(
        ids, x_parts, w_parts, jnp.asarray(forward_table)
    )
    out_far = far_of(after(w_out, pack_far, *w_parts[2:]))
    out_parts = (w_out, near_of(after(w_out, pack_far)), out_far, near_of(out_far))
    att_parts = to_place(att_own)
    residual, ffn_input, rows_sent = after_attention(
        att_parts, out_parts, tokens, small, dispatch_kept
    )

    ffn_far = far_of(ffn_input)
    dy_far = far_of(after(cotangent, ffn_far))
    up_stack = jnp.stack([w_shared_gate, w_shared_up])
    ff_part = w_shared_gate.shape[1] // fs_count
    up_own = lax.dynamic_slice_in_dim(up_stack, side * 2 * ff_part, 2 * ff_part, 2)
    up_give = lax.dynamic_slice_in_dim(up_stack, (1 - side) * 2 * ff_part, 2 * ff_part, 2)
    up_far = far_of(after(up_give, dy_far))

    def core_cut(piece, which):
        return lax.dynamic_slice_in_dim(piece, which * ff_part, ff_part, 2)

    up_parts = (
        core_cut(up_own, core),
        near_of(after(core_cut(up_own, 1 - core), ffn_far)),
        core_cut(up_far, core),
        near_of(core_cut(up_far, 1 - core)),
    )
    dy_parts = (cotangent, near_of(after(cotangent, ffn_far)), dy_far, near_of(dy_far))
    ffn_parts = (ffn_input, near_of(ffn_input), ffn_far, near_of(ffn_far))

    def fold(parts):
        mine, give, mid = parts
        got = near_of(give)
        return (mine, got, far_of((mid.astype(WIDE) + got[1].astype(WIDE)).astype(LOW)))

    def shared(start):
        sums, grads = shared_branch(
            ids,
            (after(ffn_parts[0], start), *ffn_parts[1:]),
            dy_parts,
            up_parts,
            w_shared_down,
            ep_count if pair_of_cores else 0,
        )
        return (fold(sums), grads, sums[0])

    def ep_step(block, bit):
        return lax.ppermute(block, "ep", [(i, i ^ bit) for i in range(ep_count)])

    def added(first, second):
        return (first.astype(WIDE) + second.astype(WIDE)).astype(LOW)

    weights = (w_expert_gate, w_expert_up, w_expert_down)
    if pair_of_cores:
        peers = [near_of(after(piece, out_far)) for piece in weights]
        back_din, router_part, din_sent, middle, outward, last = experts_chip(
            ids, rows_sent, got_dy, other, small, weights, peers
        )
        folded, (grads_keep, grads_give), shared_done = shared(din_sent)
        grads_got = ep_step(grads_give, 1)
        expert_out_rows, received = middle(shared_done)
    else:
        dy_sent = contract_rows(dispatch, cotangent).astype(LOW)
        back_out, back_din, router_part, expert_grads = experts_spread(
            rows_sent, dy_sent, other_sent.reshape(-1), small[:EXPERTS], weights
        )
        folded, grads_rest, _ = shared(back_din)

    grad_resid, branch = back_at_tokens(
        folded, back_din, dispatch, residual, small, cotangent, router_part
    )
    branch_far = far_of(branch)
    branch_parts = (branch, near_of(branch), branch_far, near_of(branch_far))
    if pair_of_cores:
        back_out = outward(after(expert_out_rows, branch))
        half = added(grads_keep, after(grads_got, branch))
        half_got = ep_step(half[1::2], 2)
        quarter = added(half[0::2], after(half_got, branch_parts[3]))
        quarter_got = ep_step(quarter[1:2], 4)
    output = finish_output(residual, folded, back_out, dispatch)

    d_qkv, grads_qkv = attention_backward(
        ids, branch_parts, w_out, queries, keys, values, lse, ain, (cos_table, sin_table)
    )
    din_parts, grad_out_w = late_grads(ids, d_qkv, own_mats, att_own, branch_parts)
    in_fold = fold(din_parts)
    own_float = tokens.astype(WIDE)
    grad_in = in_fold[0].astype(WIDE) + in_fold[1][0].astype(WIDE) + in_fold[2].astype(WIDE)
    gain_one = small[EXPERTS : EXPERTS + 1].astype(WIDE)
    grad_tokens = grad_resid + rms_backward(grad_in, own_float, inverse_rms(own_float), gain_one)

    strip = rows_w // ep_count
    grads_qkv = after(grads_qkv, back_out)
    qkv_blocks = grads_qkv.reshape(3, fs_count, ep_count, strip, rows_w).transpose(2, 1, 0, 3, 4)
    qkv_got = exchange(qkv_blocks.reshape(devices, 3, strip, rows_w), ALL)
    qkv_got = qkv_got.reshape(ep_count, fs_count, 3, strip, rows_w).astype(WIDE)
    qkv_sum = jnp.sum(qkv_got, 0).transpose(1, 2, 0, 3).reshape(3 * strip, width).astype(LOW)
    small_part = lax.dynamic_slice_in_dim(grad_out_w[rows_w:], fs_index * rows_w, rows_w, 1)
    if pair_of_cores:
        lines = EXTRA * rows_w // (ep_count * width)
        parts = jnp.concatenate(
            [
                grad_out_w[:rows_w].reshape(ep_count, strip, width),
                small_part.reshape(ep_count, lines, width),
            ],
            1,
        )
        out_sum = halve(parts)
    else:
        lines = 0
        out_whole = lax.psum((grad_out_w[:rows_w], small_part), "ep")
        out_sum = jnp.zeros((0, width), LOW)
    sums = jnp.concatenate([qkv_sum, out_sum])
    sums = exchange(jnp.broadcast_to(sums[None], (ep_count,) + sums.shape), "ep").astype(WIDE)
    qkv_all = sums[:, : 3 * strip].reshape(ep_count, 3, strip, width)
    qkv_all = qkv_all.transpose(1, 0, 2, 3).reshape(3, rows_w, width)
    if pair_of_cores:
        sum_out_w = sums[:, 3 * strip : 4 * strip].reshape(rows_w, width)
        sum_small = sums[:, 4 * strip :].reshape(EXTRA, rows_w)
    else:
        sum_out_w, sum_small = (piece.astype(WIDE) for piece in out_whole)
    sum_gain_one = (
        sum(
            jnp.sum(qkv_all[i] * mat.astype(WIDE), -1)
            for i, mat in enumerate((w_query, w_key, w_value))
        )
        / gain_attn.astype(WIDE)
    )
    sum_router, sum_gain_two = (sum_small[:EXPERTS].T, sum_small[EXPERTS])
    if pair_of_cores:
        expert_grads = last(qkv_blocks, received)
        own_chunk = added(quarter[0:1], after(quarter_got, grads_qkv))
        cut = 2 * rows_w // ep_count
        turned = to_place([own_chunk[0, k * cut : (k + 1) * cut] for k in range(4)])
        own_chunk = jnp.concatenate([*turned, own_chunk[0, 4 * cut :]])[None]
        whole = [own_chunk, ep_step(own_chunk, 4)]
        whole = [jnp.concatenate(whole)]
        whole = [jnp.concatenate([whole[0], ep_step(whole[0], 2)])]
        whole = [whole[0], ep_step(whole[0], 1)]
        wide_all, sum_sdown = place_shared(ids, whole, rows_w, width)
    else:
        expert_grads = expert_grads(grads_qkv)
        dense = lax.psum((*to_place(grads_rest[:4]), grads_rest[4]), "ep")
        sum_sdown = dense[4].astype(WIDE)
        wide_rel = jnp.stack([piece.astype(WIDE) for piece in dense[:4]])
        wide_all = jnp.concatenate(
            [
                lax.dynamic_index_in_dim(wide_rel, fs_index ^ k, 0, keepdims=False)
                for k in range(4)
            ],
            2,
        )
    return (
        output,
        grad_tokens,
        sum_gain_one,
        qkv_all[0],
        qkv_all[1],
        qkv_all[2],
        sum_out_w,
        sum_gain_two,
        wide_all[0],
        wide_all[1],
        sum_sdown,
        sum_router,
        *expert_grads,
    )


def solution(mesh):
    ep_count, fs_count = mesh.devices.shape
    cut_mesh = Mesh(mesh.devices.reshape(ep_count, fs_count // 2, 2), ALL)
    tok = P(ALL, None)
    row = P(SEQ, None)
    return jax.shard_map(
        shards,
        mesh=cut_mesh,
        in_specs=(
            tok,
            tok,
            tok,
            P(ALL),
            P(SEQ),
            row,
            row,
            row,
            row,
            P(SEQ),
            row,
            row,
            row,
            row,
            P(None, ALL),
            P(None, ALL),
            tok,
        ),
        out_specs=(
            tok,
            tok,
            P(SEQ),
            row,
            row,
            row,
            row,
            P(SEQ),
            row,
            row,
            row,
            row,
            P(None, ALL),
            P(None, ALL),
            tok,
        ),
        check_vma=False,
    )
```

time: 577 us -> 439 us (0.76)
  Pallas kernels: 0 us -> 107 us
  matrix products: 100 us -> 3.86 us
  other arithmetic: 101 us -> 28.7 us
  waiting for transfers between devices: 122 us -> 191 us
  local copies, waits for them, and re-layouts: 87.1 us -> 26.8 us
  blocking collectives: 50.9 us -> 0 us
  between operations: 16.5 us -> 1.9 us
  starting transfers between devices: 90.3 us -> 75.8 us
    ppermute x24 -> x46, waiting for transfers between devices: 29.7 us -> 169 us  [the longest x8 65.1 us: far_of(): return lax.ppermute(block, 'fx', SWAP)]
    pallas_call x0 -> x12, Pallas kernels: none -> 107 us  [run_kernel(): pl.pallas_call(body, out_shape=outs, in_specs=specs if specs is not None...]
    psum x1 -> x0, waiting for transfers between devices: 64.5 us -> none  [shards(): lax.psum((turned, grad_sdown.astype(LOW), grad_out_w.astype(LOW)), 'ep')]
    psum x1 -> x0, blocking collectives: 50.9 us -> none  [shards(): lax.psum(jnp.concatenate([gain_part[None], router_part], 0), ALL)]
    dot_general x21 -> x3, matrix products: 35.4 us -> 2.18 us  [matmul(): return jnp.dot(left_op, right_op, preferred_element_type=WIDE)]
    dot_general x17 -> x0, matrix products: 32.4 us -> none  [contract_cols(): lax.dot_general(left_op, right_op, (((1,), (1,)), ((), ())), preferred_el...]
    dot_general x19 -> x1, matrix products: 32.4 us -> 1.68 us  [contract_rows(): lax.dot_general(left_op, right_op, (((0,), (0,)), ((), ())), preferred_el...]
    all_to_all x13 -> x7, starting transfers between devices: 72.1 us -> 42.2 us  [exchange(): return lax.all_to_all(blocks, axes, split_axis=0, concat_axis=0, tiled=True)]
  transfers between devices with their start and end apart: 38 -> 53, of which waited for: 8 -> 21; matrix products, arithmetic and copies ran while one was open for 46% -> 9% of each run, Pallas kernels for 0% -> 22%
where the time goes in v2:
time: 439 us; the launch traced here: 435 us
  waiting for transfers between devices  191 us (44%)
  Pallas kernels  107 us (24%)
  starting transfers between devices  75.8 us (17%)
  other arithmetic  28.7 us (7%)
  local copies, waits for them, and re-layouts  26.8 us (6%)
    pallas_call x12, Pallas kernels, run_kernel(): pl.pallas_call(body, out_shape=outs, in_specs=specs if specs is not None...  107 us
    ppermute x8, waiting for transfers between devices, far_of(): return lax.ppermute(block, 'fx', SWAP)  65.1 us
    ppermute x6, waiting for transfers between devices, ep_step(): return lax.ppermute(block, 'ep', [(i, i ^ bit) for i in range(ep_count)])  56.4 us
    all_to_all x7, starting transfers between devices, exchange(): return lax.all_to_all(blocks, axes, split_axis=0, concat_axis=0, tiled=True)  42.2 us
    ppermute x9, waiting for transfers between devices, to_place(): lax.ppermute(parts[k], SEQ, [(i, i ^ k) for i in range(fs_count)])  37.1 us
    all_to_all x7, waiting for transfers between devices, exchange(): return lax.all_to_all(blocks, axes, split_axis=0, concat_axis=0, tiled=True)  21.3 us
    ppermute x8, starting transfers between devices, far_of(): return lax.ppermute(block, 'fx', SWAP)  11.2 us
    ppermute x6, starting transfers between devices, ep_step(): return lax.ppermute(block, 'ep', [(i, i ^ bit) for i in range(ep_count)])  11.1 us
  transfers between devices with their start and end apart: 53, of which 21 were waited for; matrix products, arithmetic and copies ran while one was open for 9% of the time, Pallas kernels for 22%

profile of v2, /device:TPU:0, one launch (start us, length us, event | category | flops | bytes accessed | tf_op | source)
XLA Modules:
  0.0 434.6 jit_solution(13120786620051762088)
XLA Ops:
  6.1 7.3 %all-to-all-start = ((s32[32,1,128]{2,1,0:T(1,128)}), s32[32,1,128]{2,1,0:T(1,128)S(1)}, u32[]{:S(2)}, u32[]{:S(2)}) async-start(s32[32,1,128]{2,1,0:T(1,128)} %bitcast.19), calls=%async_computation | async-start | bytes 32768 | tf_op jit(solution)/shard_map/all_to_all | solution.py:65
  22.9 12.3 %collective-permute-done.5.refs_7_ = bf16[3,192,192]{2,1,0:T(8,128)(2,1)S(1)} collective-permute-done((bf16[3,192,192]{2,1,0:T(8,128)(2,1)S(1)}, bf16[3,192,192]{2,1,0:T(8,128)(2,1)S(1)}, u32[]{:S(2)}, u32[]{:S(2)}) %collective-permute-start.5) | collective-permute-done | bytes 221216 | tf_op jit(solution)/shard_map/ppermute | solution.py:883
  35.2 6.4 %collective-permute-done.4.refs_6_ = bf16[3,192,192]{2,1,0:T(8,128)(2,1)S(1)} collective-permute-done((bf16[3,192,192]{2,1,0:T(8,128)(2,1)S(1)}, bf16[3,192,192]{2,1,0:T(8,128)(2,1)S(1)}, u32[]{:S(2)}, u32[]{:S(2)}) %collective-permute-start.4) | collective-permute-done | bytes 221216 | tf_op jit(solution)/shard_map/ppermute | solution.py:883
  41.6 7.0 %all-to-all-start.2 = ((bf16[16,48,768]{2,1,0:T(8,128)(2,1)}), bf16[16,48,768]{2,1,0:T(8,128)(2,1)}, u32[]{:S(2)}, u32[]{:S(2)}) async-start(bf16[16,48,768]{2,1,0:T(8,128)(2,1)} %bitcast.123), calls=%async_computation.2 | async-start | bytes 2359296 | tf_op jit(solution)/shard_map/all_to_all | solution.py:65
  51.9 10.6 %collective-permute-done.10.refs_6_ = bf16[192,768]{1,0:T(8,128)(2,1)S(1)} collective-permute-done((bf16[192,768]{1,0:T(8,128)(2,1)S(1)}, bf16[192,768]{1,0:T(8,128)(2,1)S(1)}, u32[]{:S(2)}, u32[]{:S(2)}) %collective-permute-start.10) | collective-permute-done | bytes 294944 | tf_op jit(solution)/shard_map/ppermute | solution.py:53
  65.0 12.8 %shard_map.307 = (bf16[1024,768]{1,0:T(8,128)(2,1)}, bf16[3,768,192]{2,1,0:T(8,128)(2,1)}, bf16[3,1024,128]{2,1,0:T(8,128)(2,1)}, bf16[3,1024,128]{2,1,0:T(8,128...) custom-call(s32[7]{0:T(128)S(1)} %stack.63.ids_ref, ...), custom_call_target="tpu_custom_call" | custom-call | flops 8000000000 | bytes 12000000 | tf_op jit(solution)/shard_map/pallas_call | solution.py:90
  81.1 3.5 collective-permute-done.7.refs_2_
  85.8 3.4 shard_map.308
  89.3 7.5 %all-to-all-start.1 = ((bf16[16,48,768]{2,1,0:T(8,128)(2,1)}), bf16[16,48,768]{2,1,0:T(8,128)(2,1)S(1)}, u32[]{:S(2)}, u32[]{:S(2)}) async-start(bf16[16,48,768]{2,1,0:T(8,128)(2,1)} %bitcast.124), calls=%async_computation.1 | async-start | bytes 2359296 | tf_op jit(solution)/shard_map/all_to_all | solution.py:65
  96.8 2.1 collective-permute-start.16
  99.4 18.6 %collective-permute-done.16.refs_2_ = bf16[256,768]{1,0:T(8,128)(2,1)} collective-permute-done((bf16[256,768]{1,0:T(8,128)(2,1)S(1)}, bf16[256,768]{1,0:T(8,128)(2,1)}, u32[]{:S(2)}, u32[]{:S(2)}) %collective-permute-start.16) | collective-permute-done | bytes 393248 | tf_op jit(solution)/shard_map/ppermute | solution.py:53
  118.3 2.0 fusion.6
  120.3 11.6 %collective-permute-done.19.refs_6_ = bf16[256,768]{1,0:T(8,128)(2,1)} collective-permute-done((bf16[256,768]{1,0:T(8,128)(2,1)S(1)}, bf16[256,768]{1,0:T(8,128)(2,1)}, u32[]{:S(2)}, u32[]{:S(2)}) %collective-permute-start.19) | collective-permute-done | bytes 393248 | tf_op jit(solution)/shard_map/ppermute | solution.py:53
  132.4 2.5 fusion.17
  135.2 15.9 %collective-permute-done.22 = bf16[2,192,1024]{2,1,0:T(8,128)(2,1)} collective-permute-done((bf16[2,192,1024]{2,1,0:T(8,128)(2,1)}, bf16[2,192,1024]{2,1,0:T(8,128)(2,1)}, u32[]{:S(2)}, u32[]{:S(2)}) %collective-permute-start.22) | collective-permute-done | bytes 786464 | tf_op jit(solution)/shard_map/ppermute | solution.py:53
  151.1 2.1 constant_dynamic-slice_fusion.4
  156.1 22.7 %shard_map.309 = (bf16[768,768]{1,0:T(8,128)(2,1)}, bf16[768,2048]{1,0:T(8,128)(2,1)}, bf16[768,2048]{1,0:T(8,128)(2,1)}, bf16[768,2048]{1,0:T(8,128)(2,1)}, bf1...) custom-call(s32[7]{0:T(128)S(1)} %stack.63.ids_ref, bf16[768,768]{1,0:T(8,128)(2,1)} %bitcast.104, ...), custom_call_target="tpu_custom_call" | custom-call | flops 12000000000 | bytes 22000000 | tf_op jit(solution)/shard_map/pallas_call | solution.py:90
  178.9 12.8 %shard_map.310 = (bf16[2,256,768]{2,1,0:T(8,128)(2,1)}, bf16[2,2,256,768]{3,2,1,0:T(8,128)(2,1)}, bf16[2,256,768]{2,1,0:T(8,128)(2,1)}, bf16[4,288,512]{2,1,0:T(8,128)(2,1)}, bf16[4,288,512]{2,1,0:T(8,128)(2,1)}) custom-call(s32[7]{0:T(128)S(1)} %stack.63.ids_ref, bf16[256,768]{1,0:T(8,128)(2,1)S(1)} %copy-done.18, bf16[256,768]{1,0:T(8,128)(2,1)S(1)} %copy-done.20, ...), custom_call_target="tpu_custom_call" | custom-call | flops 7000000000 | bytes 14000000 | tf_op jit(solution)/shard_map/pallas_call | solution.py:90
  192.1 5.9 %all-to-all-start.3 = ((bf16[16,48,768]{2,1,0:T(8,128)(2,1)}), bf16[16,48,768]{2,1,0:T(8,128)(2,1)S(1)}, u32[]{:S(2)}, u32[]{:S(2)}) async-start(bf16[16,48,768]{2,1,0:T(8,128)(2,1)} %bitcast.126), calls=%async_computation.3 | async-start | bytes 2359296 | tf_op jit(solution)/shard_map/all_to_all | solution.py:65
  198.1 2.4 fusion
  203.9 21.3 %all-to-all-done.3 = bf16[16,48,768]{2,1,0:T(8,128)(2,1)S(1)} async-done(((bf16[16,48,768]{2,1,0:T(8,128)(2,1)}), bf16[16,48,768]{2,1,0:T(8,128)(2,1)S(1)}, u32[]{:S(2)}, u32[]{:S(2)}) %all-to-all-start.3) | async-done | bytes 1179680 | tf_op jit(solution)/shard_map/all_to_all | solution.py:65
  225.1 5.0 %collective-permute-done.25.last_ref = bf16[2,256,768]{2,1,0:T(8,128)(2,1)} collective-permute-done((bf16[2,256,768]{2,1,0:T(8,128)(2,1)}, bf16[2,256,768]{2,1,0:T(8,128)(2,1)}, u32[]{:S(2)}, u32[]{:S(2)}) %collective-permute-start.25) | collective-permute-done | bytes 786464 | tf_op jit(solution)/shard_map/ppermute | solution.py:53
  230.1 4.1 shard_map.312
  235.9 6.6 %shard_map.311 = bf16[768,768]{1,0:T(8,128)(2,1)} custom-call(bf16[768,2048]{1,0:T(8,128)(2,1)} %get-tuple-element.98.hid_ref, f32[768,1]{1,0:T(8,128)S(1)} %get-tuple-element.99.w_ref, bf16[1024,768]{1,0:T(8,128)(2,1)} %own_ref.1, bf16[1024,768]{1,0:T(8,128)(2,1)} %collective-permute-done.14.refs_5_.peer_ref), custom_call_target="tpu_custom_call" | custom-call | flops 2000000000 | bytes 8000000 | tf_op jit(solution)/shard_map/pallas_call | solution.py:90
  242.5 3.3 collective-permute-done.27.refs_2_.refs_6_
  245.8 7.4 %shard_map.317 = (bf16[768,1024]{1,0:T(8,128)(2,1)}, bf16[768,1024]{1,0:T(8,128)(2,1)}, bf16[1024,768]{1,0:T(8,128)(2,1)}) custom-call(bf16[768,768]{1,0:T(8,128)(2,1)S(1)} %bitcast.105, bf16[768,768]{1,0:T(8,128)(2,1)} %get-tuple-element.125.dyw_ref, bf16[768,2048]{1,0:T(8,128)(2,1)} %get-tuple-element.98.hid_ref, ...), custom_call_target="tpu_custom_call" | custom-call | flops 3700000000 | bytes 14000000 | tf_op jit(solution)/shard_map/pallas_call | solution.py:90
  254.1 5.5 %all-to-all-start.4 = ((bf16[16,48,768]{2,1,0:T(8,128)(2,1)}), bf16[16,48,768]{2,1,0:T(8,128)(2,1)}, u32[]{:S(2)}, u32[]{:S(2)}) async-start(bf16[16,48,768]{2,1,0:T(8,128)(2,1)} %bitcast.32), calls=%async_computation.4 | async-start | bytes 2359296 | tf_op jit(solution)/shard_map/all_to_all | solution.py:65
  264.5 15.9 %shard_map.314 = (bf16[3,1024,192]{2,1,0:T(8,128)(2,1)}, bf16[3,768,192]{2,1,0:T(8,128)(2,1)}) custom-call(s32[7]{0:T(128)S(1)} %copy-done.15, bf16[288,768]{1,0:T(8,128)(2,1)S(1)} %get-tuple-element.101.refs_0_.refs_4_, bf16[288,768]{1,0:T(8,128)(2,1)S(1)} %collective-permute-done.26.refs_1_.refs_5_, ...), custom_call_target="tpu_custom_call" | custom-call | flops 16000000000 | bytes 12000000 | tf_op jit(solution)/shard_map/pallas_call | solution.py:90
  280.4 5.1 %shard_map.315 = (bf16[256,768]{1,0:T(8,128)(2,1)S(1)}, bf16[2,256,768]{2,1,0:T(8,128)(2,1)}, bf16[256,768]{1,0:T(8,128)(2,1)S(1)}, bf16[224,768]{1,0:T(8,128)(2,1)S(1)}) custom-call(s32[7]{0:T(128)S(1)} %copy-done.15, bf16[3,1024,192]{2,1,0:T(8,128)(2,1)} %get-tuple-element.109.d_ref, bf16[3,768,192]{2,1,0:T(8,128)(2,1)} %get-tuple-element.110.w_ref, ...), custom_call_target="tpu_custom_call" | custom-call | flops 1200000000 | bytes 7000000 | tf_op jit(solution)/shard_map/pallas_call | solution.py:90
  287.5 6.2 %collective-permute-done.35 = bf16[2,288,512]{2,1,0:T(8,128)(2,1)} collective-permute-done((bf16[2,288,512]{2,1,0:T(8,128)(2,1)}, bf16[2,288,512]{2,1,0:T(8,128)(2,1)}, u32[]{:S(2)}, u32[]{:S(2)}) %collective-permute-start.35) | collective-permute-done | bytes 589856 | tf_op jit(solution)/shard_map/ppermute | solution.py:982
  295.8 2.5 collective-permute-start.36
  298.8 12.5 %collective-permute-done.36 = bf16[1,288,512]{2,1,0:T(8,128)(2,1)} collective-permute-done((bf16[1,288,512]{2,1,0:T(8,128)(2,1)}, bf16[1,288,512]{2,1,0:T(8,128)(2,1)}, u32[]{:S(2)}, u32[]{:S(2)}) %collective-permute-start.36) | collective-permute-done | bytes 294944 | tf_op jit(solution)/shard_map/ppermute | solution.py:982
  312.4 2.4 copy.51
  314.8 4.7 %all-to-all-start.5 = ((bf16[32,3,24,192]{3,2,1,0:T(8,128)(2,1)}), bf16[32,3,24,192]{3,2,1,0:T(8,128)(2,1)}, u32[]{:S(2)}, u32[]{:S(2)}) async-start(bf16[32,3,24,192]{3,2,1,0:T(8,128)(2,1)} %bitcast.108), calls=%async_computation.5 | async-start | bytes 2359296 | tf_op jit(solution)/shard_map/all_to_all | solution.py:65
  322.4 7.8 %collective-permute-done.38 = bf16[48,512]{1,0:T(8,128)(2,1)S(1)} collective-permute-done((bf16[48,512]{1,0:T(8,128)(2,1)S(1)}, bf16[48,512]{1,0:T(8,128)(2,1)S(1)}, u32[]{:S(2)}, u32[]{:S(2)}) %collective-permute-start.38) | collective-permute-done | bytes 49184 | tf_op jit(solution)/shard_map/ppermute | solution.py:883
  330.5 4.9 %collective-permute-done.39 = bf16[48,512]{1,0:T(8,128)(2,1)S(1)} collective-permute-done((bf16[48,512]{1,0:T(8,128)(2,1)S(1)}, bf16[48,512]{1,0:T(8,128)(2,1)S(1)}, u32[]{:S(2)}, u32[]{:S(2)}) %collective-permute-start.39) | collective-permute-done | bytes 49184 | tf_op jit(solution)/shard_map/ppermute | solution.py:883
  335.4 6.8 %collective-permute-done.32 = bf16[2,25,768]{2,1,0:T(8,128)(2,1)S(1)} collective-permute-done((bf16[2,25,768]{2,1,0:T(8,128)(2,1)S(1)}, bf16[2,25,768]{2,1,0:T(8,128)(2,1)S(1)}, u32[]{:S(2)}, u32[]{:S(2)}) %collective-permute-start.32) | collective-permute-done | bytes 76832 | tf_op jit(solution)/shard_map/ppermute | solution.py:78
  342.1 3.5 collective-permute-start.40
  345.7 15.3 %collective-permute-done.40 = bf16[1,288,512]{2,1,0:T(8,128)(2,1)S(1)} collective-permute-done((bf16[1,288,512]{2,1,0:T(8,128)(2,1)S(1)}, bf16[1,288,512]{2,1,0:T(8,128)(2,1)S(1)}, u32[]{:S(2)}, u32[]{:S(2)}) %collective-permute-start.40) | collective-permute-done | bytes 294944 | tf_op jit(solution)/shard_map/ppermute | solution.py:982
  361.9 4.1 collective-permute-done.33
  368.9 4.4 %all-to-all-start.6 = ((bf16[8,97,768]{2,1,0:T(8,128)(2,1)}), bf16[8,97,768]{2,1,0:T(8,128)(2,1)}, u32[]{:S(2)}, u32[]{:S(2)}) async-start(bf16[8,97,768]{2,1,0:T(8,128)(2,1)} %broadcast_in_dim.16), calls=%async_computation.6 | async-start | bytes 2555904 | tf_op jit(solution)/shard_map/all_to_all | solution.py:65
  375.9 9.8 %collective-permute-done.41 = bf16[2,288,512]{2,1,0:T(8,128)(2,1)} collective-permute-done((bf16[2,288,512]{2,1,0:T(8,128)(2,1)}, bf16[2,288,512]{2,1,0:T(8,128)(2,1)}, u32[]{:S(2)}, u32[]{:S(2)}) %collective-permute-start.41) | collective-permute-done | bytes 589856 | tf_op jit(solution)/shard_map/ppermute | solution.py:982
  388.7 8.9 %shard_map.318 = (f32[768,1024]{1,0:T(8,128)}, f32[768,1024]{1,0:T(8,128)}, f32[1024,768]{1,0:T(8,128)}) custom-call(bf16[768,768]{1,0:T(8,128)(2,1)S(1)} %bitcast.106, bf16[768,768]{1,0:T(8,128)(2,1)} %get-tuple-element.125.dyw_ref, bf16[768,2048]{1,0:T(8,128)(2,1)} %get-tuple-element.98.hid_ref, bf16[768,2048]{1,0:T(8,128)(2,1)} %get-tuple-element.126.dg_ref, ...), custom_call_target="tpu_custom_call" | custom-call | flops 3700000000 | bytes 14000000 | tf_op jit(solution)/shard_map/pallas_call | solution.py:90
  399.1 2.3 fusion.4
  401.5 3.2 shard_map.313
  404.7 12.5 %collective-permute-done.42.refs_1_ = bf16[4,288,512]{2,1,0:T(8,128)(2,1)S(1)} collective-permute-done((bf16[4,288,512]{2,1,0:T(8,128)(2,1)S(1)}, bf16[4,288,512]{2,1,0:T(8,128)(2,1)S(1)}, u32[]{:S(2)}, u32[]{:S(2)}) %collective-permute-start.42) | collective-permute-done | bytes 1179680 | tf_op jit(solution)/shard_map/ppermute | solution.py:982
  418.2 3.8 shard_map.316
  422.0 3.9 slice_bitcast_fusion
  (245 shorter events, 69.6 us)
Async XLA Ops:
  6.1 16.8 %all-to-all-start = ((s32[32,1,128]{2,1,0:T(1,128)}), s32[32,1,128]{2,1,0:T(1,128)S(1)}, u32[]{:S(2)}, u32[]{:S(2)}) async-start(s32[32,1,128]{2,1,0:T(1,128)} %bitcast.19), calls=%async_computation | async-start | bytes 32768 | tf_op jit(solution)/shard_map/all_to_all | solution.py:65
  16.5 25.1 %collective-permute-start.1 = (bf16[288,768]{1,0:T(8,128)(2,1)S(1)}, bf16[288,768]{1,0:T(8,128)(2,1)}, u32[]{:S(2)}, u32[]{:S(2)}) collective-permute-start(bf16[288,768]{1,0:T(8,128)(2,1)S(1)} %pad_maximum_fusion.3.refs_0_), channel_id=1, source_target_pairs={{0,2},{2,0},{1,3},{3,1},{4,6},{6,4},{5,7},{7,5},{8,10},{10,8},{9,1... | collective-permute-start | bytes 1327112 | tf_op jit(solution)/shard_map/ppermute | solution.py:53
  19.7 15.5 %collective-permute-start.5 = (bf16[3,192,192]{2,1,0:T(8,128)(2,1)S(1)}, bf16[3,192,192]{2,1,0:T(8,128)(2,1)S(1)}, u32[]{:S(2)}, u32[]{:S(2)}) collective-permute-start(bf16[3,192,192]{2,1,0:T(8,128)(2,1)S(1)} %get-tuple-element.148), channel_id=1, source_target_pairs={{0,3},{1,2},{2,1},{3,0},{4,7},{5,6},{6,5},{7,4},{8,11},{9,10},{10,... | collective-permute-start | bytes 663560 | tf_op jit(solution)/shard_map/ppermute | solution.py:883
  19.7 21.8 %collective-permute-start.4 = (bf16[3,192,192]{2,1,0:T(8,128)(2,1)S(1)}, bf16[3,192,192]{2,1,0:T(8,128)(2,1)S(1)}, u32[]{:S(2)}, u32[]{:S(2)}) collective-permute-start(bf16[3,192,192]{2,1,0:T(8,128)(2,1)S(1)} %get-tuple-element.149), channel_id=1, source_target_pairs={{0,2},{1,3},{2,0},{3,1},{4,6},{5,7},{6,4},{7,5},{8,10},{9,11},{10,... | collective-permute-start | bytes 663560 | tf_op jit(solution)/shard_map/ppermute | solution.py:883
  41.6 47.7 %all-to-all-start.2 = ((bf16[16,48,768]{2,1,0:T(8,128)(2,1)}), bf16[16,48,768]{2,1,0:T(8,128)(2,1)}, u32[]{:S(2)}, u32[]{:S(2)}) async-start(bf16[16,48,768]{2,1,0:T(8,128)(2,1)} %bitcast.123), calls=%async_computation.2 | async-start | bytes 2359296 | tf_op jit(solution)/shard_map/all_to_all | solution.py:65
  48.6 14.7 %collective-permute-start = (bf16[288,768]{1,0:T(8,128)(2,1)S(1)}, bf16[288,768]{1,0:T(8,128)(2,1)}, u32[]{:S(2)}, u32[]{:S(2)}) collective-permute-start(bf16[288,768]{1,0:T(8,128)(2,1)S(1)} %pad_maximum_fusion.3.refs_0_), channel_id=1, source_target_pairs={{0,1},{1,0},{2,3},{3,2},{4,5},{5,4},{6,7},{7,6},{8,9},{9,8},{10,11... | collective-permute-start | bytes 1327112 | tf_op jit(solution)/shard_map/ppermute | solution.py:57
  48.7 13.9 %collective-permute-start.3 = (bf16[3,192,192]{2,1,0:T(8,128)(2,1)}, bf16[3,192,192]{2,1,0:T(8,128)(2,1)S(1)}, u32[]{:S(2)}, u32[]{:S(2)}) collective-permute-start(bf16[3,192,192]{2,1,0:T(8,128)(2,1)} %get-tuple-element.150), channel_id=1, source_target_pairs={{0,1},{1,0},{2,3},{3,2},{4,5},{5,4},{6,7},{7,6},{8,9},{9,8},{10,11... | collective-permute-start | bytes 663560 | tf_op jit(solution)/shard_map/ppermute | solution.py:883
  49.4 13.9 %collective-permute-start.2 = (bf16[288,768]{1,0:T(8,128)(2,1)}, bf16[288,768]{1,0:T(8,128)(2,1)S(1)}, u32[]{:S(2)}, u32[]{:S(2)}) collective-permute-start(bf16[288,768]{1,0:T(8,128)(2,1)} %collective-permute-done.1.refs_2_), channel_id=1, source_target_pairs={{0,1},{1,0},{2,3},{3,2},{4,5},{5,4},{6,7},{7,6},{8,9},{9,8},{10,11... | collective-permute-start | bytes 1327112 | tf_op jit(solution)/shard_map/ppermute | solution.py:57
  49.6 12.9 %collective-permute-start.10 = (bf16[192,768]{1,0:T(8,128)(2,1)S(1)}, bf16[192,768]{1,0:T(8,128)(2,1)S(1)}, u32[]{:S(2)}, u32[]{:S(2)}) collective-permute-start(bf16[192,768]{1,0:T(8,128)(2,1)S(1)} %copy-done.8), channel_id=1, source_target_pairs={{0,2},{2,0},{1,3},{3,1},{4,6},{6,4},{5,7},{7,5},{8,10},{10,8},{9,1... | collective-permute-start | bytes 884744 | tf_op jit(solution)/shard_map/ppermute | solution.py:53
  51.7 29.4 %collective-permute-start.9 = (bf16[192,768]{1,0:T(8,128)(2,1)S(1)}, bf16[192,768]{1,0:T(8,128)(2,1)S(1)}, u32[]{:S(2)}, u32[]{:S(2)}) collective-permute-start(bf16[192,768]{1,0:T(8,128)(2,1)S(1)} %copy-done.8), channel_id=1, source_target_pairs={{0,1},{1,0},{2,3},{3,2},{4,5},{5,4},{6,7},{7,6},{8,9},{9,8},{10,11... | collective-permute-start | bytes 884744 | tf_op jit(solution)/shard_map/ppermute | solution.py:57
  62.5 23.3 %collective-permute-start.11 = (bf16[192,768]{1,0:T(8,128)(2,1)S(1)}, bf16[192,768]{1,0:T(8,128)(2,1)S(1)}, u32[]{:S(2)}, u32[]{:S(2)}) collective-permute-start(bf16[192,768]{1,0:T(8,128)(2,1)S(1)} %collective-permute-done.10.refs_6_), channel_id=1, source_target_pairs={{0,1},{1,0},{2,3},{3,2},{4,5},{5,4},{6,7},{7,6},{8,9},{9,8},{10,11... | collective-permute-start | bytes 884744 | tf_op jit(solution)/shard_map/ppermute | solution.py:57
  78.3 6.3 %collective-permute-start.7 = (bf16[256,192]{1,0:T(8,128)(2,1)S(1)}, bf16[256,192]{1,0:T(8,128)(2,1)S(1)}, u32[]{:S(2)}, u32[]{:S(2)}) collective-permute-start(bf16[256,192]{1,0:T(8,128)(2,1)S(1)} %get-tuple-element.77.refs_2_), channel_id=1, source_target_pairs={{0,2},{1,3},{2,0},{3,1},{4,6},{5,7},{6,4},{7,5},{8,10},{9,11},{10,... | collective-permute-start | bytes 294920 | tf_op jit(solution)/shard_map/ppermute | solution.py:883
  89.3 65.8 %all-to-all-start.1 = ((bf16[16,48,768]{2,1,0:T(8,128)(2,1)}), bf16[16,48,768]{2,1,0:T(8,128)(2,1)S(1)}, u32[]{:S(2)}, u32[]{:S(2)}) async-start(bf16[16,48,768]{2,1,0:T(8,128)(2,1)} %bitcast.124), calls=%async_computation.1 | async-start | bytes 2359296 | tf_op jit(solution)/shard_map/all_to_all | solution.py:65
  96.8 21.2 %collective-permute-start.16 = (bf16[256,768]{1,0:T(8,128)(2,1)S(1)}, bf16[256,768]{1,0:T(8,128)(2,1)}, u32[]{:S(2)}, u32[]{:S(2)}) collective-permute-start(bf16[256,768]{1,0:T(8,128)(2,1)S(1)} %copy-done.17), channel_id=1, source_target_pairs={{0,2},{2,0},{1,3},{3,1},{4,6},{6,4},{5,7},{7,5},{8,10},{10,8},{9,1... | collective-permute-start | bytes 1179656 | tf_op jit(solution)/shard_map/ppermute | solution.py:53
  98.9 55.6 %collective-permute-start.12 = (bf16[768,1024]{1,0:T(8,128)(2,1)}, bf16[768,1024]{1,0:T(8,128)(2,1)}, u32[]{:S(2)}, u32[]{:S(2)}) collective-permute-start(bf16[768,1024]{1,0:T(8,128)(2,1)} %refs_0_.1), channel_id=1, source_target_pairs={{0,1},{1,0},{2,3},{3,2},{4,5},{5,4},{6,7},{7,6},{8,9},{9,8},{10,11... | collective-permute-start | bytes 4718600 | tf_op jit(solution)/shard_map/ppermute | solution.py:57
  98.9 55.6 %collective-permute-start.13 = (bf16[768,1024]{1,0:T(8,128)(2,1)}, bf16[768,1024]{1,0:T(8,128)(2,1)}, u32[]{:S(2)}, u32[]{:S(2)}) collective-permute-start(bf16[768,1024]{1,0:T(8,128)(2,1)} %refs_1_.1), channel_id=1, source_target_pairs={{0,1},{1,0},{2,3},{3,2},{4,5},{5,4},{6,7},{7,6},{8,9},{9,8},{10,11... | collective-permute-start | bytes 4718600 | tf_op jit(solution)/shard_map/ppermute | solution.py:57
  99.4 55.6 %collective-permute-start.14 = (bf16[1024,768]{1,0:T(8,128)(2,1)}, bf16[1024,768]{1,0:T(8,128)(2,1)}, u32[]{:S(2)}, u32[]{:S(2)}) collective-permute-start(bf16[1024,768]{1,0:T(8,128)(2,1)} %own_ref.1), channel_id=1, source_target_pairs={{0,1},{1,0},{2,3},{3,2},{4,5},{5,4},{6,7},{7,6},{8,9},{9,8},{10,11... | collective-permute-start | bytes 4718600 | tf_op jit(solution)/shard_map/ppermute | solution.py:57
  118.0 13.9 %collective-permute-start.19 = (bf16[256,768]{1,0:T(8,128)(2,1)S(1)}, bf16[256,768]{1,0:T(8,128)(2,1)}, u32[]{:S(2)}, u32[]{:S(2)}) collective-permute-start(bf16[256,768]{1,0:T(8,128)(2,1)S(1)} %copy-done.7), channel_id=1, source_target_pairs={{0,2},{2,0},{1,3},{3,1},{4,6},{6,4},{5,7},{7,5},{8,10},{10,8},{9,1... | collective-permute-start | bytes 1179656 | tf_op jit(solution)/shard_map/ppermute | solution.py:53
  131.9 19.2 %collective-permute-start.22 = (bf16[2,192,1024]{2,1,0:T(8,128)(2,1)}, bf16[2,192,1024]{2,1,0:T(8,128)(2,1)}, u32[]{:S(2)}, u32[]{:S(2)}) collective-permute-start(bf16[2,192,1024]{2,1,0:T(8,128)(2,1)} %fusion.6), channel_id=1, source_target_pairs={{0,2},{2,0},{1,3},{3,1},{4,6},{6,4},{5,7},{7,5},{8,10},{10,8},{9,1... | collective-permute-start | bytes 2359304 | tf_op jit(solution)/shard_map/ppermute | solution.py:53
  132.4 20.8 %collective-permute-start.15 = (bf16[256,768]{1,0:T(8,128)(2,1)S(1)}, bf16[256,768]{1,0:T(8,128)(2,1)S(1)}, u32[]{:S(2)}, u32[]{:S(2)}) collective-permute-start(bf16[256,768]{1,0:T(8,128)(2,1)S(1)} %copy-done.17), channel_id=1, source_target_pairs={{0,1},{1,0},{2,3},{3,2},{4,5},{5,4},{6,7},{7,6},{8,9},{9,8},{10,11... | collective-permute-start | bytes 1179656 | tf_op jit(solution)/shard_map/ppermute | solution.py:57
  151.1 27.6 %collective-permute-start.18 = (bf16[256,768]{1,0:T(8,128)(2,1)S(1)}, bf16[256,768]{1,0:T(8,128)(2,1)}, u32[]{:S(2)}, u32[]{:S(2)}) collective-permute-start(bf16[256,768]{1,0:T(8,128)(2,1)S(1)} %copy-done.7), channel_id=1, source_target_pairs={{0,1},{1,0},{2,3},{3,2},{4,5},{5,4},{6,7},{7,6},{8,9},{9,8},{10,11... | collective-permute-start | bytes 1179656 | tf_op jit(solution)/shard_map/ppermute | solution.py:57
  154.0 24.8 %collective-permute-start.21 = (bf16[2,192,512]{2,1,0:T(8,128)(2,1)}, bf16[2,192,512]{2,1,0:T(8,128)(2,1)}, u32[]{:S(2)}, u32[]{:S(2)}) collective-permute-start(bf16[2,192,512]{2,1,0:T(8,128)(2,1)} %get-tuple-element.92), channel_id=1, source_target_pairs={{0,1},{1,0},{2,3},{3,2},{4,5},{5,4},{6,7},{7,6},{8,9},{9,8},{10,11... | collective-permute-start | bytes 1179656 | tf_op jit(solution)/shard_map/ppermute | solution.py:57
  154.5 24.3 %collective-permute-start.17 = (bf16[256,768]{1,0:T(8,128)(2,1)}, bf16[256,768]{1,0:T(8,128)(2,1)}, u32[]{:S(2)}, u32[]{:S(2)}) collective-permute-start(bf16[256,768]{1,0:T(8,128)(2,1)} %collective-permute-done.16.refs_2_), channel_id=1, source_target_pairs={{0,1},{1,0},{2,3},{3,2},{4,5},{5,4},{6,7},{7,6},{8,9},{9,8},{10,11... | collective-permute-start | bytes 1179656 | tf_op jit(solution)/shard_map/ppermute | solution.py:57
  154.5 24.3 %collective-permute-start.20 = (bf16[256,768]{1,0:T(8,128)(2,1)}, bf16[256,768]{1,0:T(8,128)(2,1)}, u32[]{:S(2)}, u32[]{:S(2)}) collective-permute-start(bf16[256,768]{1,0:T(8,128)(2,1)} %collective-permute-done.19.refs_6_), channel_id=1, source_target_pairs={{0,1},{1,0},{2,3},{3,2},{4,5},{5,4},{6,7},{7,6},{8,9},{9,8},{10,11... | collective-permute-start | bytes 1179656 | tf_op jit(solution)/shard_map/ppermute | solution.py:57
  155.0 23.8 %collective-permute-start.23 = (bf16[2,192,512]{2,1,0:T(8,128)(2,1)}, bf16[2,192,512]{2,1,0:T(8,128)(2,1)}, u32[]{:S(2)}, u32[]{:S(2)}) collective-permute-start(bf16[2,192,512]{2,1,0:T(8,128)(2,1)} %get-tuple-element.152), channel_id=1, source_target_pairs={{0,1},{1,0},{2,3},{3,2},{4,5},{5,4},{6,7},{7,6},{8,9},{9,8},{10,11... | collective-permute-start | bytes 1179656 | tf_op jit(solution)/shard_map/ppermute | solution.py:57
  191.7 6.4 %collective-permute-start.24 = (bf16[2,2,256,768]{3,2,1,0:T(8,128)(2,1)}, bf16[2,2,256,768]{3,2,1,0:T(8,128)(2,1)}, u32[]{:S(2)}, u32[]{:S(2)}) collective-permute-start(bf16[2,2,256,768]{3,2,1,0:T(8,128)(2,1)} %get-tuple-element.95), channel_id=1, source_target_pairs={{0,1},{1,0},{2,3},{3,2},{4,5},{5,4},{6,7},{7,6},{8,9},{9,8},{10,11... | collective-permute-start | bytes 4718600 | tf_op jit(solution)/shard_map/ppermute | solution.py:57
  192.1 33.0 %all-to-all-start.3 = ((bf16[16,48,768]{2,1,0:T(8,128)(2,1)}), bf16[16,48,768]{2,1,0:T(8,128)(2,1)S(1)}, u32[]{:S(2)}, u32[]{:S(2)}) async-start(bf16[16,48,768]{2,1,0:T(8,128)(2,1)} %bitcast.126), calls=%async_computation.3 | async-start | bytes 2359296 | tf_op jit(solution)/shard_map/all_to_all | solution.py:65
  200.5 29.6 %collective-permute-start.25 = (bf16[2,256,768]{2,1,0:T(8,128)(2,1)}, bf16[2,256,768]{2,1,0:T(8,128)(2,1)}, u32[]{:S(2)}, u32[]{:S(2)}) collective-permute-start(bf16[2,256,768]{2,1,0:T(8,128)(2,1)} %fusion), channel_id=1, source_target_pairs={{0,2},{2,0},{1,3},{3,1},{4,6},{6,4},{5,7},{7,5},{8,10},{10,8},{9,1... | collective-permute-start | bytes 2359304 | tf_op jit(solution)/shard_map/ppermute | solution.py:53
  202.4 51.4 %collective-permute-start.34 = (bf16[4,288,512]{2,1,0:T(8,128)(2,1)}, bf16[4,288,512]{2,1,0:T(8,128)(2,1)}, u32[]{:S(2)}, u32[]{:S(2)}) collective-permute-start(bf16[4,288,512]{2,1,0:T(8,128)(2,1)} %get-tuple-element.118), channel_id=1, source_target_pairs={{0,4},{4,0},{8,12},{12,8},{16,20},{20,16},{24,28},{28,24},{1,5},{5... | collective-permute-start | bytes 3538952 | tf_op jit(solution)/shard_map/ppermute | solution.py:982
  234.2 11.6 %collective-permute-start.27 = (bf16[288,768]{1,0:T(8,128)(2,1)S(1)}, bf16[288,768]{1,0:T(8,128)(2,1)S(1)}, u32[]{:S(2)}, u32[]{:S(2)}) collective-permute-start(bf16[288,768]{1,0:T(8,128)(2,1)S(1)} %get-tuple-element.101.refs_0_.refs_4_), channel_id=1, source_target_pairs={{0,2},{2,0},{1,3},{3,1},{4,6},{6,4},{5,7},{7,5},{8,10},{10,8},{9,1... | collective-permute-start | bytes 1327112 | tf_op jit(solution)/shard_map/ppermute | solution.py:53
  242.5 20.1 %collective-permute-start.26 = (bf16[288,768]{1,0:T(8,128)(2,1)S(1)}, bf16[288,768]{1,0:T(8,128)(2,1)S(1)}, u32[]{:S(2)}, u32[]{:S(2)}) collective-permute-start(bf16[288,768]{1,0:T(8,128)(2,1)S(1)} %get-tuple-element.101.refs_0_.refs_4_), channel_id=1, source_target_pairs={{0,1},{1,0},{2,3},{3,2},{4,5},{5,4},{6,7},{7,6},{8,9},{9,8},{10,11... | collective-permute-start | bytes 1327112 | tf_op jit(solution)/shard_map/ppermute | solution.py:57
  245.8 18.7 %collective-permute-start.28 = (bf16[288,768]{1,0:T(8,128)(2,1)S(1)}, bf16[288,768]{1,0:T(8,128)(2,1)}, u32[]{:S(2)}, u32[]{:S(2)}) collective-permute-start(bf16[288,768]{1,0:T(8,128)(2,1)S(1)} %collective-permute-done.27.refs_2_.refs_6_), channel_id=1, source_target_pairs={{0,1},{1,0},{2,3},{3,2},{4,5},{5,4},{6,7},{7,6},{8,9},{9,8},{10,11... | collective-permute-start | bytes 1327112 | tf_op jit(solution)/shard_map/ppermute | solution.py:57
  253.3 135.5 %collective-permute-start.43 = (bf16[768,1024]{1,0:T(8,128)(2,1)}, bf16[768,1024]{1,0:T(8,128)(2,1)}, u32[]{:S(2)}, u32[]{:S(2)}) collective-permute-start(bf16[768,1024]{1,0:T(8,128)(2,1)} %get-tuple-element.129), channel_id=1, source_target_pairs={{0,1},{1,0},{2,3},{3,2},{4,5},{5,4},{6,7},{7,6},{8,9},{9,8},{10,11... | collective-permute-start | bytes 4718600 | tf_op jit(solution)/shard_map/ppermute | solution.py:57
  253.6 135.1 %collective-permute-start.44 = (bf16[768,1024]{1,0:T(8,128)(2,1)}, bf16[768,1024]{1,0:T(8,128)(2,1)}, u32[]{:S(2)}, u32[]{:S(2)}) collective-permute-start(bf16[768,1024]{1,0:T(8,128)(2,1)} %get-tuple-element.130), channel_id=1, source_target_pairs={{0,1},{1,0},{2,3},{3,2},{4,5},{5,4},{6,7},{7,6},{8,9},{9,8},{10,11... | collective-permute-start | bytes 4718600 | tf_op jit(solution)/shard_map/ppermute | solution.py:57
  253.8 135.0 %collective-permute-start.45 = (bf16[1024,768]{1,0:T(8,128)(2,1)}, bf16[1024,768]{1,0:T(8,128)(2,1)}, u32[]{:S(2)}, u32[]{:S(2)}) collective-permute-start(bf16[1024,768]{1,0:T(8,128)(2,1)} %get-tuple-element.131), channel_id=1, source_target_pairs={{0,1},{1,0},{2,3},{3,2},{4,5},{5,4},{6,7},{7,6},{8,9},{9,8},{10,11... | collective-permute-start | bytes 4718600 | tf_op jit(solution)/shard_map/ppermute | solution.py:57
  254.1 44.7 %all-to-all-start.4 = ((bf16[16,48,768]{2,1,0:T(8,128)(2,1)}), bf16[16,48,768]{2,1,0:T(8,128)(2,1)}, u32[]{:S(2)}, u32[]{:S(2)}) async-start(bf16[16,48,768]{2,1,0:T(8,128)(2,1)} %bitcast.32), calls=%async_computation.4 | async-start | bytes 2359296 | tf_op jit(solution)/shard_map/all_to_all | solution.py:65
  262.6 31.0 %collective-permute-start.35 = (bf16[2,288,512]{2,1,0:T(8,128)(2,1)}, bf16[2,288,512]{2,1,0:T(8,128)(2,1)}, u32[]{:S(2)}, u32[]{:S(2)}) collective-permute-start(bf16[2,288,512]{2,1,0:T(8,128)(2,1)} %slice.135), channel_id=1, source_target_pairs={{0,8},{4,12},{8,0},{12,4},{16,24},{20,28},{24,16},{28,20},{1,9},{5... | collective-permute-start | bytes 1769480 | tf_op jit(solution)/shard_map/ppermute | solution.py:982
  286.0 12.3 %collective-permute-start.31 = (bf16[4,25,768]{2,0,1:T(4,128)(2,1)S(1)}, bf16[4,25,768]{2,0,1:T(4,128)(2,1)S(1)}, u32[]{:S(2)}, u32[]{:S(2)}) collective-permute-start(bf16[4,25,768]{2,0,1:T(4,128)(2,1)S(1)} %dynamic-slice_bitcast_fusion), channel_id=1, source_target_pairs={{0,4},{4,0},{8,12},{12,8},{16,20},{20,16},{24,28},{28,24},{1,5},{5... | collective-permute-start | bytes 460808 | tf_op jit(solution)/shard_map/ppermute | solution.py:78
  295.8 15.5 %collective-permute-start.36 = (bf16[1,288,512]{2,1,0:T(8,128)(2,1)}, bf16[1,288,512]{2,1,0:T(8,128)(2,1)}, u32[]{:S(2)}, u32[]{:S(2)}) collective-permute-start(bf16[1,288,512]{2,1,0:T(8,128)(2,1)} %slice.163), channel_id=1, source_target_pairs={{0,16},{4,20},{8,24},{12,28},{16,0},{20,4},{24,8},{28,12},{1,17},{... | collective-permute-start | bytes 884744 | tf_op jit(solution)/shard_map/ppermute | solution.py:982
  298.3 75.0 %collective-permute-start.29 = (bf16[2,256,768]{2,1,0:T(8,128)(2,1)}, bf16[2,256,768]{2,1,0:T(8,128)(2,1)}, u32[]{:S(2)}, u32[]{:S(2)}) collective-permute-start(bf16[2,256,768]{2,1,0:T(8,128)(2,1)} %get-tuple-element.112), channel_id=1, source_target_pairs={{0,1},{1,0},{2,3},{3,2},{4,5},{5,4},{6,7},{7,6},{8,9},{9,8},{10,11... | collective-permute-start | bytes 2359304 | tf_op jit(solution)/shard_map/ppermute | solution.py:57
  314.8 51.3 %all-to-all-start.5 = ((bf16[32,3,24,192]{3,2,1,0:T(8,128)(2,1)}), bf16[32,3,24,192]{3,2,1,0:T(8,128)(2,1)}, u32[]{:S(2)}, u32[]{:S(2)}) async-start(bf16[32,3,24,192]{3,2,1,0:T(8,128)(2,1)} %bitcast.108), calls=%async_computation.5 | async-start | bytes 2359296 | tf_op jit(solution)/shard_map/all_to_all | solution.py:65
  320.7 9.5 %collective-permute-start.38 = (bf16[48,512]{1,0:T(8,128)(2,1)S(1)}, bf16[48,512]{1,0:T(8,128)(2,1)S(1)}, u32[]{:S(2)}, u32[]{:S(2)}) collective-permute-start(bf16[48,512]{1,0:T(8,128)(2,1)S(1)} %get-tuple-element.155), channel_id=1, source_target_pairs={{0,2},{1,3},{2,0},{3,1},{4,6},{5,7},{6,4},{7,5},{8,10},{9,11},{10,... | collective-permute-start | bytes 147464 | tf_op jit(solution)/shard_map/ppermute | solution.py:883
  335.4 6.8 %collective-permute-start.32 = (bf16[2,25,768]{2,1,0:T(8,128)(2,1)S(1)}, bf16[2,25,768]{2,1,0:T(8,128)(2,1)S(1)}, u32[]{:S(2)}, u32[]{:S(2)}) collective-permute-start(bf16[2,25,768]{2,1,0:T(8,128)(2,1)S(1)} %bitcast.136), channel_id=1, source_target_pairs={{0,8},{4,12},{8,0},{12,4},{16,24},{20,28},{24,16},{28,20},{1,9},{5... | collective-permute-start | bytes 230408 | tf_op jit(solution)/shard_map/ppermute | solution.py:78
  342.1 18.9 %collective-permute-start.40 = (bf16[1,288,512]{2,1,0:T(8,128)(2,1)S(1)}, bf16[1,288,512]{2,1,0:T(8,128)(2,1)S(1)}, u32[]{:S(2)}, u32[]{:S(2)}) collective-permute-start(bf16[1,288,512]{2,1,0:T(8,128)(2,1)S(1)} %bitcast.120), channel_id=1, source_target_pairs={{0,16},{4,20},{8,24},{12,28},{16,0},{20,4},{24,8},{28,12},{1,17},{... | collective-permute-start | bytes 884744 | tf_op jit(solution)/shard_map/ppermute | solution.py:982
  366.0 19.7 %collective-permute-start.41 = (bf16[2,288,512]{2,1,0:T(8,128)(2,1)}, bf16[2,288,512]{2,1,0:T(8,128)(2,1)}, u32[]{:S(2)}, u32[]{:S(2)}) collective-permute-start(bf16[2,288,512]{2,1,0:T(8,128)(2,1)} %pad_maximum_fusion.2), channel_id=1, source_target_pairs={{0,8},{4,12},{8,0},{12,4},{16,24},{20,28},{24,16},{28,20},{1,9},{5... | collective-permute-start | bytes 1769480 | tf_op jit(solution)/shard_map/ppermute | solution.py:982
  368.9 57.0 %all-to-all-start.6 = ((bf16[8,97,768]{2,1,0:T(8,128)(2,1)}), bf16[8,97,768]{2,1,0:T(8,128)(2,1)}, u32[]{:S(2)}, u32[]{:S(2)}) async-start(bf16[8,97,768]{2,1,0:T(8,128)(2,1)} %broadcast_in_dim.16), calls=%async_computation.6 | async-start | bytes 2555904 | tf_op jit(solution)/shard_map/all_to_all | solution.py:65
  374.4 23.3 %collective-permute-start.30 = (bf16[256,768]{1,0:T(8,128)(2,1)S(1)}, bf16[256,768]{1,0:T(8,128)(2,1)S(1)}, u32[]{:S(2)}, u32[]{:S(2)}) collective-permute-start(bf16[256,768]{1,0:T(8,128)(2,1)S(1)} %fusion.7), channel_id=1, source_target_pairs={{0,2},{2,0},{1,3},{3,1},{4,6},{6,4},{5,7},{7,5},{8,10},{10,8},{9,1... | collective-permute-start | bytes 1179656 | tf_op jit(solution)/shard_map/ppermute | solution.py:53
  387.0 30.3 %collective-permute-start.42 = (bf16[4,288,512]{2,1,0:T(8,128)(2,1)S(1)}, bf16[4,288,512]{2,1,0:T(8,128)(2,1)S(1)}, u32[]{:S(2)}, u32[]{:S(2)}) collective-permute-start(bf16[4,288,512]{2,1,0:T(8,128)(2,1)S(1)} %pad_maximum_fusion.refs_0_), channel_id=1, source_target_pairs={{0,4},{4,0},{8,12},{12,8},{16,20},{20,16},{24,28},{28,24},{1,5},{5... | collective-permute-start | bytes 3538952 | tf_op jit(solution)/shard_map/ppermute | solution.py:982
  (46 other events, 550.3 us)
